TPU v7x, 128 devices: a whole 4x4x4 slice. The times are simulated.
128 devices in a mesh: dev: 128 (over y, z, x, core).
Axes of the slice: x: 4, y: 4, z: 4, core: 2. Of those that a mesh axis runs over, the one named last changes fastest.
Arguments:
- vectors: bfloat16 [131072, 768], P('dev'), may hold values from -6 to 6
- row_list: int32 [131072], P('dev'), may hold values from 0 to 511
- block_owner: int32 [4096], P('dev'), may hold values from 0 to 127, as said below
- block_fill: int32 [4096], P('dev'), may hold values from 1 to 32
- old_centroids: float32 [65536, 768], P('dev'), may hold values from -6 to 6
- codebook: bfloat16 [24, 32, 256], replicated, may hold values from -6 to 6
Outputs:
- new_centroids: float32 [65536, 768], P('dev')
- slot_error: float32 [16384, 32], P('dev')
- sub_covariance: float32 [24, 32, 32], replicated
Inputs may be any that keep to these rules, and one draw needn't show every extreme that they name: `block_owner`: the blocks of one device go to distinct owners, and in every draw some owner receives one block from every device.
All inputs are finite; a program needn't handle non-finite values.
Results may differ from a plain program's by a relative error of at most 0.0003.
Values may be sent and summed in bfloat16 or wider, within the bound.
No kernel may reach another device: no remote copies, remote signals or barrier semaphores. Data moves between devices by JAX's collectives and lax.ppermute only.
A program may use at most 128 MiB of HBM per device.

v0:
```python
import jax
import jax.numpy as jnp
from jax import lax
from jax.sharding import PartitionSpec as P


def error_terms(residual, weights, codebook, book_norm, subspaces, sub_width, feature_width):
    count_rows = residual.shape[0]
    pieces = residual.reshape(count_rows, subspaces, sub_width).transpose(1, 2, 0)
    cross_terms = jnp.einsum("mdr,mdk->mkr", pieces, codebook, preferred_element_type=jnp.float32)
    row_norm = jnp.sum(jnp.square(pieces.astype(jnp.float32)), axis=1)
    distance = row_norm[:, None, :] - 2.0 * cross_terms + book_norm[:, :, None]
    row_error = jnp.sum(jnp.min(distance, axis=1), axis=0) / feature_width * weights
    moment = jnp.einsum("mdr,mer->mde", pieces, pieces, preferred_element_type=jnp.float32)
    return (row_error, moment)


def body(vectors, row_list, block_owner, block_fill, old_centroids, codebook):
    devices = lax.axis_size("dev")
    blocks_here = block_owner.shape[0]
    block_rows = row_list.shape[0] // blocks_here
    feature_width = vectors.shape[1]
    subspaces = codebook.shape[0]
    sub_width = codebook.shape[1]
    own_lists = old_centroids.shape[0]
    total_rows = devices * block_rows
    book_norm = jnp.sum(jnp.square(codebook.astype(jnp.float32)), axis=1)
    zero_moment = jnp.zeros((subspaces, sub_width, sub_width), jnp.float32)
    send_rows = (
        jnp.zeros((devices, block_rows, feature_width), jnp.bfloat16)
        .at[block_owner]
        .set(vectors.reshape(blocks_here, block_rows, feature_width))
    )
    send_lists = (
        jnp.zeros((devices, block_rows), jnp.int32)
        .at[block_owner]
        .set(row_list.reshape(blocks_here, block_rows))
    )
    send_fill = jnp.zeros((devices,), jnp.int32).at[block_owner].set(block_fill)
    recv_rows, recv_lists, recv_fill = (
        lax.all_to_all(send_rows, "dev", split_axis=0, concat_axis=0, tiled=True),
        lax.all_to_all(send_lists, "dev", split_axis=0, concat_axis=0, tiled=True),
        lax.all_to_all(send_fill, "dev", split_axis=0, concat_axis=0, tiled=True),
    )
    flat_rows = recv_rows.reshape(total_rows, feature_width)
    flat_lists = recv_lists.reshape(total_rows)
    offsets = lax.broadcasted_iota(jnp.int32, (devices, block_rows), 1)
    flat_valid = (offsets < recv_fill[:, None]).reshape(total_rows)
    members = (
        (lax.broadcasted_iota(jnp.int32, (own_lists, total_rows), 0) == flat_lists[None, :])
        & flat_valid[None, :]
    ).astype(jnp.bfloat16)
    list_sums = jnp.dot(members, flat_rows, preferred_element_type=jnp.float32)
    counts = jnp.sum(members, axis=1, dtype=jnp.float32)
    centroids = (list_sums + old_centroids) / (counts + 1.0)[:, None]

    def quantize(slot_rows, slot_lists, slot_fill):
        count_slots = slot_rows.shape[0]
        count_rows = count_slots * block_rows
        weights = (
            (lax.broadcasted_iota(jnp.int32, (count_slots, block_rows), 1) < slot_fill[:, None])
            .reshape(count_rows)
            .astype(jnp.float32)
        )
        picked = jnp.take(centroids, slot_lists.reshape(count_rows), axis=0)
        residual = (
            (slot_rows.reshape(count_rows, feature_width).astype(jnp.float32) - picked)
            * weights[:, None]
        ).astype(jnp.bfloat16)
        residual = lax.optimization_barrier(residual)
        row_error, moment = error_terms(
            residual, weights, codebook, book_norm, subspaces, sub_width, feature_width
        )
        return (row_error.reshape(count_slots, block_rows), moment)

    slot_group = max(1, min(devices, 1024 // block_rows))
    round_count = devices // slot_group

    def visit(moment_sum, pieces_in):
        row_error, moment = quantize(pieces_in[0], pieces_in[1], pieces_in[2])
        return (moment_sum + moment, row_error)

    moment_sum, error_store = lax.scan(
        visit,
        zero_moment,
        (
            recv_rows.reshape(round_count, slot_group, block_rows, feature_width),
            recv_lists.reshape(round_count, slot_group, block_rows),
            recv_fill.reshape(round_count, slot_group),
        ),
    )
    slot_error = error_store.reshape(devices, block_rows)
    local_total = jnp.sum(block_fill.astype(jnp.float32))
    moment_all, total_all = lax.psum((moment_sum, local_total), "dev")
    return (centroids, slot_error, moment_all / total_all)


def solution(mesh):
    return jax.shard_map(
        body,
        mesh=mesh,
        in_specs=(P("dev", None), P("dev"), P("dev"), P("dev"), P("dev", None), P()),
        out_specs=(P("dev", None), P("dev", None), P()),
        check_vma=False,
    )
```

profile of v0, /device:TPU:0, one launch (start us, length us, event | category | flops | bytes accessed | tf_op | source)
XLA Modules:
  0.0 389.1 jit_solution(2170653258805801279)
XLA Ops:
  9.4 11.1 %all-to-all-start.1 = ((s32[128,1,1]{2,1,0:T(1,128)}), s32[128,1,1]{2,1,0:T(1,128)S(1)}, u32[]{:S(2)}, u32[]{:S(2)}) async-start(s32[128,1,1]{2,1,0:T(1,128)} %copy.20), calls=%async_computation.1 | async-start | bytes 131072 | tf_op jit(solution)/shard_map/all_to_all | solution.py:43
  22.5 7.2 %all-to-all-done.1 = s32[128,1,1]{2,1,0:T(1,128)S(1)} async-done(((s32[128,1,1]{2,1,0:T(1,128)}), s32[128,1,1]{2,1,0:T(1,128)S(1)}, u32[]{:S(2)}, u32[]{:S(2)}) %all-to-all-start.1) | async-done | bytes 544 | tf_op jit(solution)/shard_map/all_to_all | solution.py:43
  29.7 5.7 %all-to-all-start = ((s32[128,1,32]{2,1,0:T(1,128)}), s32[128,1,32]{2,1,0:T(1,128)}, u32[]{:S(2)}, u32[]{:S(2)}) async-start(s32[128,1,32]{2,1,0:T(1,128)} %bitcast), calls=%async_computation | async-start | bytes 131072 | tf_op jit(solution)/shard_map/all_to_all | solution.py:42
  35.4 3.4 broadcast_in_dim.41
  38.9 5.0 %scatter_fusion = bf16[128,32,768]{2,1,0:T(8,128)(2,1)} fusion(bf16[128,32,768]{2,1,0:T(8,128)(2,1)} %broadcast_in_dim.41, s32[32]{0:T(128)S(1)} %compare_select_fusion.2, bf16[32,32,768]{2,1,0:T(8,128)(2,1)S(1)} %bitcast.40), kind=kCustom, calls=%fused_computation.3 | custom fusion | bytes 4718720 | tf_op jit(solution)/shard_map/scatter | solution.py:32
  44.7 9.4 %all-to-all-start.2 = ((bf16[128,32,768]{2,1,0:T(8,128)(2,1)}), bf16[128,32,768]{2,1,0:T(8,128)(2,1)}, u32[]{:S(2)}, u32[]{:S(2)}) async-start(bf16[128,32,768]{2,1,0:T(8,128)(2,1)} %scatter_fusion), calls=%async_computation.2 | async-start | bytes 12582912 | tf_op jit(solution)/shard_map/all_to_all | solution.py:41
  54.8 2.3 reduce.2
  60.3 1.9 convert_reduce_fusion
  62.2 67.6 %all-to-all-done.2 = bf16[128,32,768]{2,1,0:T(8,128)(2,1)} async-done(((bf16[128,32,768]{2,1,0:T(8,128)(2,1)}), bf16[128,32,768]{2,1,0:T(8,128)(2,1)}, u32[]{:S(2)}, u32[]{:S(2)}) %all-to-all-start.2) | async-done | bytes 6291488 | tf_op jit(solution)/shard_map/all_to_all | solution.py:41
  129.8 7.2 %add_divide_fusion = f32[512,768]{1,0:T(8,128)S(1)} fusion(f32[512,768]{1,0:T(8,128)} %param.12, bf16[4096,768]{1,0:T(8,128)(2,1)} %bitcast.3, s32[4096]{0:T(1024)S(1)} %eq.10, pred[4096]{0:T(1024)(128)(4,1)S(1)} %lt.77, f32[512]{0:T(512)S(1)} %broadcast_add_fusion), kind=kOutput, calls=%fused_computation.30 | convolution fusion | flops 3226206208 | bytes 9459712 | tf_op jit(solution)/shard_map/dot_general | solution.py:53
  137.0 97.0 %while.13 = (s32[]{:T(128)}, f32[24,32,32]{2,1,0:T(8,128)S(1)}, f32[4,32,32]{2,1,0:T(8,128)}, bf16[4,32,32,768]{3,2,1,0:T(8,128)(2,1)}, s32[4,32,32]{2,1,0:T(8,1...) while((s32[]{:T(128)}, f32[24,32,32]{2,1,0:T(8,128)S(1)}, ...), condition=%wide.region_9.10_spmd.clone, body=%wide.region_5.9_spmd.clone.sunk | while | flops 484481024 | bytes 37294148 | solution.py:83
  138.0 5.4 %gather_fusion = f32[1024,768]{1,0:T(8,128)} fusion(f32[512,768]{1,0:T(8,128)S(1)} %get-tuple-element.185, s32[1024]{0:T(1024)S(1)} %broadcast_clamp_fusion.2), kind=kCustom, calls=%fused_computation.clone.clone.1 | custom fusion | bytes 6295552 | tf_op jit(solution)/shard_map/while/body/eval_jaxpr/jit(_take)/gather | solution.py:65
  144.9 1.7 constant_dynamic-slice_fusion.6
  147.2 1.7 fusion.34
  148.9 1.7 copy.24
  151.1 6.1 %add_reduce_fusion.2 = f32[24,1024]{1,0:T(8,128)} fusion(f32[24,256]{1,0:T(8,128)} %get-tuple-element.188, f32[24,1024]{1,0:T(8,128)S(1)} %multiply_reduce_fusion.3, bf16[24,32,1024]{2,1,0:T(8,128)(2,1)S(1)} %bitcast.38, bf16[24,32,256]{2,1,0:T(8,128)(2,1)} %get-tuple-element.187), kind=kOutput, calls=%fused_computation.4.clone.1 | convolution fusion | flops 427794432 | bytes 2187264 | tf_op jit(solution)/shard_map/while/body/eval_jaxpr/mdr,mdk->mkr/dot_general | solution.py:10
  162.3 5.4 %gather_fusion = f32[1024,768]{1,0:T(8,128)} fusion(f32[512,768]{1,0:T(8,128)S(1)} %get-tuple-element.185, s32[1024]{0:T(1024)S(1)} %broadcast_clamp_fusion.2), kind=kCustom, calls=%fused_computation.clone.clone.1 | custom fusion | bytes 6295552 | tf_op jit(solution)/shard_map/while/body/eval_jaxpr/jit(_take)/gather | solution.py:65
  169.1 1.7 constant_dynamic-slice_fusion.6
  171.4 1.7 fusion.34
  173.1 1.7 copy.24
  175.3 6.1 %add_reduce_fusion.2 = f32[24,1024]{1,0:T(8,128)} fusion(f32[24,256]{1,0:T(8,128)} %get-tuple-element.188, f32[24,1024]{1,0:T(8,128)S(1)} %multiply_reduce_fusion.3, bf16[24,32,1024]{2,1,0:T(8,128)(2,1)S(1)} %bitcast.38, bf16[24,32,256]{2,1,0:T(8,128)(2,1)} %get-tuple-element.187), kind=kOutput, calls=%fused_computation.4.clone.1 | convolution fusion | flops 427794432 | bytes 2187264 | tf_op jit(solution)/shard_map/while/body/eval_jaxpr/mdr,mdk->mkr/dot_general | solution.py:10
  186.5 5.4 %gather_fusion = f32[1024,768]{1,0:T(8,128)} fusion(f32[512,768]{1,0:T(8,128)S(1)} %get-tuple-element.185, s32[1024]{0:T(1024)S(1)} %broadcast_clamp_fusion.2), kind=kCustom, calls=%fused_computation.clone.clone.1 | custom fusion | bytes 6295552 | tf_op jit(solution)/shard_map/while/body/eval_jaxpr/jit(_take)/gather | solution.py:65
  195.7 1.7 fusion.34
  197.4 1.7 copy.24
  199.6 6.1 %add_reduce_fusion.2 = f32[24,1024]{1,0:T(8,128)} fusion(f32[24,256]{1,0:T(8,128)} %get-tuple-element.188, f32[24,1024]{1,0:T(8,128)S(1)} %multiply_reduce_fusion.3, bf16[24,32,1024]{2,1,0:T(8,128)(2,1)S(1)} %bitcast.38, bf16[24,32,256]{2,1,0:T(8,128)(2,1)} %get-tuple-element.187), kind=kOutput, calls=%fused_computation.4.clone.1 | convolution fusion | flops 427794432 | bytes 2187264 | tf_op jit(solution)/shard_map/while/body/eval_jaxpr/mdr,mdk->mkr/dot_general | solution.py:10
  210.7 5.4 %gather_fusion = f32[1024,768]{1,0:T(8,128)} fusion(f32[512,768]{1,0:T(8,128)S(1)} %get-tuple-element.185, s32[1024]{0:T(1024)S(1)} %broadcast_clamp_fusion.2), kind=kCustom, calls=%fused_computation.clone.clone.1 | custom fusion | bytes 6295552 | tf_op jit(solution)/shard_map/while/body/eval_jaxpr/jit(_take)/gather | solution.py:65
  219.9 1.7 fusion.34
  221.6 1.7 copy.24
  223.8 6.1 %add_reduce_fusion.2 = f32[24,1024]{1,0:T(8,128)} fusion(f32[24,256]{1,0:T(8,128)} %get-tuple-element.188, f32[24,1024]{1,0:T(8,128)S(1)} %multiply_reduce_fusion.3, bf16[24,32,1024]{2,1,0:T(8,128)(2,1)S(1)} %bitcast.38, bf16[24,32,256]{2,1,0:T(8,128)(2,1)} %get-tuple-element.187), kind=kOutput, calls=%fused_computation.4.clone.1 | convolution fusion | flops 427794432 | bytes 2187264 | tf_op jit(solution)/shard_map/while/body/eval_jaxpr/mdr,mdk->mkr/dot_general | solution.py:10
  236.1 65.4 %psum.15 = f32[]{:T(128)} all-reduce(f32[]{:T(128)} %convert_reduce_fusion.1), channel_id=1, replica_groups=mesh['dev'=128] {'dev'}, use_global_device_ids=true, to_apply=%region_12.13 | all-reduce | flops 1 | bytes 8 | tf_op jit(solution)/shard_map/psum | solution.py:94
  303.0 76.8 %all-reduce.2.cloned.1.call-done = f32[24,32,32]{2,1,0:T(8,128)} async-done(((f32[24,32,32]{2,1,0:T(8,128)}), f32[24,32,32]{2,1,0:T(8,128)}) %all-reduce.2.cloned.1.call-update) | async-done | bytes 98320 | tf_op jit(solution)/shard_map/psum | solution.py:94
  379.8 2.4 broadcast_divide_fusion
  (106 shorter events, 46.0 us)
Async XLA Ops:
  9.4 20.4 %all-to-all-start.1 = ((s32[128,1,1]{2,1,0:T(1,128)}), s32[128,1,1]{2,1,0:T(1,128)S(1)}, u32[]{:S(2)}, u32[]{:S(2)}) async-start(s32[128,1,1]{2,1,0:T(1,128)} %copy.20), calls=%async_computation.1 | async-start | bytes 131072 | tf_op jit(solution)/shard_map/all_to_all | solution.py:43
  29.7 14.9 %all-to-all-start = ((s32[128,1,32]{2,1,0:T(1,128)}), s32[128,1,32]{2,1,0:T(1,128)}, u32[]{:S(2)}, u32[]{:S(2)}) async-start(s32[128,1,32]{2,1,0:T(1,128)} %bitcast), calls=%async_computation | async-start | bytes 131072 | tf_op jit(solution)/shard_map/all_to_all | solution.py:42
  35.4 3.5 copy-start.3
  43.9 10.2 %copy-start.4 = (bf16[24,32,256]{2,1,0:T(8,128)(2,1)S(1)}, bf16[24,32,256]{2,1,0:T(8,128)(2,1)}, u32[]{:S(2)}) copy-start(bf16[24,32,256]{2,1,0:T(8,128)(2,1)} %param.13) | copy-start | bytes 1179652
  44.7 85.1 %all-to-all-start.2 = ((bf16[128,32,768]{2,1,0:T(8,128)(2,1)}), bf16[128,32,768]{2,1,0:T(8,128)(2,1)}, u32[]{:S(2)}, u32[]{:S(2)}) async-start(bf16[128,32,768]{2,1,0:T(8,128)(2,1)} %scatter_fusion), calls=%async_computation.2 | async-start | bytes 12582912 | tf_op jit(solution)/shard_map/all_to_all | solution.py:41
  54.0 325.8 %all-reduce.2.cloned.1.call-start = ((), (), s32[]{:S(2)}) async-start(), calls=%async_computation.3 | async-start | bytes 786432 | tf_op jit(solution)/shard_map/psum | solution.py:94
  144.2 0.6 copy-start.5
  144.9 2.4 copy-start.1
  168.4 0.6 copy-start.5
  169.1 2.4 copy-start.1
  192.6 0.6 copy-start.5
  193.3 2.4 copy-start.1
  216.8 0.6 copy-start.5
  217.5 2.4 copy-start.1
  234.1 0.7 copy-start.2
  234.1 148.2 %copy-start = (f32[512,768]{1,0:T(8,128)}, f32[512,768]{1,0:T(8,128)S(1)}, u32[]{:S(2)}) copy-start(f32[512,768]{1,0:T(8,128)S(1)} %get-tuple-element.193) | copy-start | bytes 4718596
Sparse Core Ops, SparseCore 0:
  235.0 144.8 all-reduce.1
where the time goes:
time: 391 us; the launch traced here: 389 us
  waiting for transfers between devices  152 us (39%)
  blocking collectives  65.4 us (17%)
  local copies, waits for them, and re-layouts  65.1 us (17%)
  matrix products  34 us (9%)
  other arithmetic  31.4 us (8%)
  starting transfers between devices  26.2 us (7%)
  between operations  14.1 us (4%)
    psum x1, waiting for transfers between devices, body(): moment_all, total_all = lax.psum((moment_sum, local_total), 'dev')  76.8 us
    all_to_all x1, waiting for transfers between devices, body(): lax.all_to_all(send_rows, 'dev', split_axis=0, concat_axis=0, tiled=True)  67.6 us
    psum x1, blocking collectives, body(): moment_all, total_all = lax.psum((moment_sum, local_total), 'dev')  65.4 us
    dot_general x4, matrix products, error_terms(): jnp.einsum('mdr,mdk->mkr', pieces, codebook, preferred_element_type=jnp.f...  24.6 us
    gather x4, local copies, waits for them, and re-layouts, quantize(): picked = jnp.take(centroids, slot_lists.reshape(count_rows), axis=0)  21.4 us
    all_to_all x1, starting transfers between devices, body(): lax.all_to_all(send_fill, 'dev', split_axis=0, concat_axis=0, tiled=True)  11.1 us
    dynamic_slice x8, local copies, waits for them, and re-layouts, body(): lax.scan(visit, zero_moment, (recv_rows.reshape(round_count, slot_group,...  9.54 us
    all_to_all x1, starting transfers between devices, body(): lax.all_to_all(send_rows, 'dev', split_axis=0, concat_axis=0, tiled=True)  9.37 us
  transfers between devices with their start and end apart: 4, of which 4 were waited for; matrix products, arithmetic and copies ran while one was open for 5% of the time, Pallas kernels for 0%

commit v1 on v0

v1 whole, which is shorter than its diff:
```python
import functools

import jax
import jax.numpy as jnp
from jax import lax
from jax.experimental import pallas as pl
from jax.experimental.pallas import tpu as pltpu
from jax.sharding import PartitionSpec as P

LANES = 128
META = 16
AUG = 16
GROUP = 512
VMEM = 56 * 1024 * 1024


def send_kernel(blk, owner_ref, fill_ref, vec_ref, list_ref, send_ref, tiles, meta, sems):
    blocks = owner_ref.shape[0]
    width = vec_ref.shape[1]
    chunks = width // LANES
    span = LANES // blk
    place = lax.rem(lax.axis_index("dev"), span)
    for j in range(chunks):
        tiles[:, j * blk : (j + 1) * blk, :] = vec_ref[:, j * LANES : (j + 1) * LANES].reshape(
            blocks, blk, LANES
        )
    copies = []
    for b in range(blocks):
        copy = pltpu.make_async_copy(
            tiles.at[b], send_ref.at[owner_ref[b], pl.ds(0, chunks * blk), :], sems.at[b]
        )
        copy.start()
        copies.append(copy)
    total = functools.reduce(lambda a, b: a + b, [fill_ref[b] for b in range(blocks)])
    rows = lax.broadcasted_iota(jnp.int32, (META, LANES), 0)
    lane = lax.broadcasted_iota(jnp.int32, (1, LANES), 1)
    base = jnp.where(rows == 3, total >> 8, jnp.where(rows == 4, total & 255, 0))
    meta[...] = jnp.broadcast_to(base.astype(jnp.float32).astype(jnp.bfloat16)[None], meta.shape)
    for b in range(blocks):
        line = list_ref[b // span : b // span + 1, :] + 1
        line = pltpu.roll(line, lax.rem(place + span - b % span, span) * blk, 1)
        kept = (lane // blk == place) & (lax.rem(lane, blk) < fill_ref[b])
        line = jnp.broadcast_to(jnp.where(kept, line, 0), (META, LANES))
        tile = jnp.where(
            rows == 0, line & 255, jnp.where(rows == 1, line >> 8, jnp.where(rows == 2, 1, base))
        )
        meta[owner_ref[b]] = tile.astype(jnp.float32).astype(jnp.bfloat16)
    last = pltpu.make_async_copy(
        meta, send_ref.at[:, pl.ds(chunks * blk, META), :], sems.at[blocks]
    )
    last.start()
    for copy in copies:
        copy.wait()
    last.wait()


def build_send(vectors, row_list, block_owner, block_fill, devices):
    rows, width = vectors.shape
    blocks = block_owner.shape[0]
    blk = rows // blocks
    height = width // LANES * blk
    return pl.pallas_call(
        functools.partial(send_kernel, blk),
        out_shape=jax.ShapeDtypeStruct((devices, height + META, LANES), jnp.bfloat16),
        in_specs=[
            pl.BlockSpec(memory_space=pltpu.SMEM),
            pl.BlockSpec(memory_space=pltpu.SMEM),
            pl.BlockSpec(memory_space=pltpu.VMEM),
            pl.BlockSpec(memory_space=pltpu.VMEM),
        ],
        out_specs=pl.BlockSpec(memory_space=pl.ANY),
        scratch_shapes=[
            pltpu.VMEM((blocks, height, LANES), jnp.bfloat16),
            pltpu.VMEM((devices, META, LANES), jnp.bfloat16),
            pltpu.SemaphoreType.DMA((blocks + 1,)),
        ],
        compiler_params=pltpu.CompilerParams(vmem_limit_bytes=VMEM),
        name="build_send",
    )(block_owner, block_fill, vectors, row_list.reshape(rows // LANES, LANES))


def update_kernel(
    blk, recv_ref, old_ref, cent_ref, resid_ref, code_ref, mom_ref, total_ref,
    hot, turned, codes, sums, counts, high, low, gram, tot,
):
    step = pl.program_id(0)
    groups = pl.num_programs(0) // 2
    slots = recv_ref.shape[0]
    lists, width = old_ref.shape
    chunks = width // LANES
    span = LANES // blk

    @pl.when(step == 0)
    def _():
        sums[...] = jnp.zeros_like(sums)
        counts[...] = jnp.zeros_like(counts)
        tot[...] = jnp.zeros_like(tot)

    @pl.when(step < groups)
    def _():
        lines = []
        pieces = [[] for _ in range(chunks)]
        seen = jnp.zeros((1, LANES), jnp.float32)
        for s in range(slots):
            info = recv_ref[s, chunks * blk : chunks * blk + META, :].astype(jnp.float32)
            line = info[0:1] + 256.0 * info[1:2]
            if s % span == 0:
                lines.append(line)
            else:
                lines[-1] = lines[-1] + line
            seen = seen + (info[4:5] + 256.0 * info[3:4])
            there = jnp.broadcast_to(info[2:3], (blk, LANES)) > 0.0
            for j in range(chunks):
                piece = recv_ref[s, j * blk : (j + 1) * blk, :].astype(jnp.float32)
                pieces[j].append(jnp.where(there, piece, 0.0).astype(jnp.bfloat16))
        tot[...] += seen
        code = jnp.concatenate(lines, axis=1)
        codes[step] = jnp.broadcast_to(code, codes.shape[1:])
        ids = lax.broadcasted_iota(jnp.int32, (lists, GROUP), 0).astype(jnp.float32) + 1.0
        match = jnp.where(ids == code, 1.0, 0.0)
        chosen = match.astype(jnp.bfloat16)
        hot[step] = chosen
        part = match[:, 0:LANES]
        for k in range(1, GROUP // LANES):
            part = part + match[:, k * LANES : (k + 1) * LANES]
        counts[...] += part
        for j in range(chunks):
            column = jnp.concatenate(pieces[j], axis=0)
            turned[step, j * LANES : (j + 1) * LANES, :] = column.T
            pieces[j] = column
        values = jnp.concatenate(pieces, axis=1)
        sums[...] += jnp.dot(chosen, values, preferred_element_type=jnp.float32)

    @pl.when(step == groups)
    def _():
        count = jnp.sum(counts[...], axis=1, keepdims=True) + 1.0
        cent = (sums[...] + old_ref[...]) / count
        cent_ref[...] = cent
        flipped = cent.T
        head = flipped.astype(jnp.bfloat16)
        high[...] = head
        low[...] = (flipped - head.astype(jnp.float32)).astype(jnp.bfloat16)
        gram[...] = jnp.zeros_like(gram)

    @pl.when(step >= groups)
    def _():
        now = step - groups
        chosen = hot[now]
        code = codes[now][0:1]
        weight = jnp.where(code > 0.0, 1.0, 0.0)
        code_ref[...] = jnp.broadcast_to(weight, code_ref.shape)
        wide = 2 * LANES
        for j in range(width // wide):
            at = slice(j * wide, (j + 1) * wide)
            picked = jnp.dot(high[at], chosen, preferred_element_type=jnp.float32)
            picked = picked + jnp.dot(low[at], chosen, preferred_element_type=jnp.float32)
            resid = ((turned[now, at].astype(jnp.float32) - picked) * weight).astype(jnp.bfloat16)
            resid_ref[0, at] = resid
            gram[j] += lax.dot_general(
                resid, resid, (((1,), (1,)), ((), ())), preferred_element_type=jnp.float32
            )

    @pl.when(step == 2 * groups - 1)
    def _():
        sub = mom_ref.shape[1]
        across = LANES // sub
        lane = lax.broadcasted_iota(jnp.int32, (sub, LANES), 1)
        for q in range(chunks):
            half = slice((q % 2) * LANES, (q % 2 + 1) * LANES)
            line = jnp.zeros((sub, LANES), jnp.float32)
            for a in range(across):
                top = ((q % 2) * across + a) * sub
                line = jnp.where(lane // sub == a, gram[q // 2, top : top + sub, half], line)
            mom_ref[q] = line
        total_ref[...] = jnp.broadcast_to(tot[...], total_ref.shape)


def update_lists(recv, old, blk, sub):
    slots, height, _ = recv.shape
    lists, width = old.shape
    rows = slots * blk
    groups = rows // GROUP
    each = GROUP // blk
    return pl.pallas_call(
        functools.partial(update_kernel, blk),
        grid=(2 * groups,),
        out_shape=(
            jax.ShapeDtypeStruct((lists, width), jnp.float32),
            jax.ShapeDtypeStruct((groups, width, GROUP), jnp.bfloat16),
            jax.ShapeDtypeStruct((groups, 8, GROUP), jnp.float32),
            jax.ShapeDtypeStruct((width // LANES, sub, LANES), jnp.float32),
            jax.ShapeDtypeStruct((8, LANES), jnp.float32),
        ),
        in_specs=[
            pl.BlockSpec((each, height, LANES), lambda i: (jnp.minimum(i, groups - 1), 0, 0)),
            pl.BlockSpec((lists, width), lambda i: (0, 0)),
        ],
        out_specs=(
            pl.BlockSpec((lists, width), lambda i: (0, 0)),
            pl.BlockSpec((1, width, GROUP), lambda i: (jnp.maximum(i - groups, 0), 0, 0)),
            pl.BlockSpec((1, 8, GROUP), lambda i: (jnp.maximum(i - groups, 0), 0, 0)),
            pl.BlockSpec((width // LANES, sub, LANES), lambda i: (0, 0, 0)),
            pl.BlockSpec((8, LANES), lambda i: (0, 0)),
        ),
        scratch_shapes=[
            pltpu.VMEM((groups, lists, GROUP), jnp.bfloat16),
            pltpu.VMEM((groups, width, GROUP), jnp.bfloat16),
            pltpu.VMEM((groups, 8, GROUP), jnp.float32),
            pltpu.VMEM((lists, width), jnp.float32),
            pltpu.VMEM((lists, LANES), jnp.float32),
            pltpu.VMEM((width, lists), jnp.bfloat16),
            pltpu.VMEM((width, lists), jnp.bfloat16),
            pltpu.VMEM((width // (2 * LANES), 2 * LANES, 2 * LANES), jnp.float32),
            pltpu.VMEM((1, LANES), jnp.float32),
        ],
        compiler_params=pltpu.CompilerParams(vmem_limit_bytes=VMEM),
        name="update_lists",
    )(recv, old)


def error_kernel(sub, resid_ref, weight_ref, book_ref, error_ref):
    subspaces = book_ref.shape[0]
    ones = jnp.ones((AUG, GROUP), jnp.bfloat16)
    norm = jnp.zeros((8, GROUP), jnp.float32)
    least = jnp.zeros((1, GROUP), jnp.float32)
    for m in range(subspaces):
        piece = resid_ref[0, m * sub : (m + 1) * sub, :]
        long = piece.astype(jnp.float32)
        square = long * long
        for k in range(sub // 8):
            norm = norm + square[k * 8 : (k + 1) * 8]
        distance = jnp.dot(
            book_ref[m],
            jnp.concatenate([piece, ones], axis=0),
            preferred_element_type=jnp.float32,
        )
        least = least + jnp.min(distance, axis=0, keepdims=True)
    width = subspaces * sub
    error = (least + jnp.sum(norm, axis=0, keepdims=True)) * (weight_ref[0, 0:1] / width)
    error_ref[0] = jnp.broadcast_to(error, error_ref.shape[1:])


def row_errors(resid, weight, book, sub, first, count):
    groups, width, _ = resid.shape
    subspaces, codes, depth = book.shape
    return pl.pallas_call(
        functools.partial(error_kernel, sub),
        grid=(count,),
        out_shape=jax.ShapeDtypeStruct((count, 8, GROUP), jnp.float32),
        in_specs=[
            pl.BlockSpec((1, width, GROUP), lambda i: (first + i, 0, 0)),
            pl.BlockSpec((1, 8, GROUP), lambda i: (first + i, 0, 0)),
            pl.BlockSpec((subspaces, codes, depth), lambda i: (0, 0, 0)),
        ],
        out_specs=pl.BlockSpec((1, 8, GROUP), lambda i: (i, 0, 0)),
        compiler_params=pltpu.CompilerParams(vmem_limit_bytes=VMEM),
        cost_estimate=pl.CostEstimate(
            flops=2 * 256 * codes * subspaces * GROUP * count,
            bytes_accessed=width * GROUP * count * 2,
            transcendentals=0,
        ),
        name="row_errors",
    )(resid, weight, book)


def extended_book(codebook):
    values = codebook.astype(jnp.float32)
    rest = jnp.sum(jnp.square(values), axis=1)
    parts = []
    for _ in range(3):
        part = lax.reduce_precision(rest, 8, 7)
        parts.append(part)
        rest = rest - part
    parts = jnp.stack(parts, axis=2)
    parts = jnp.pad(parts, ((0, 0), (0, 0), (0, AUG - 3)))
    return jnp.concatenate([-2.0 * values.transpose(0, 2, 1), parts], axis=2).astype(jnp.bfloat16)


def body(vectors, row_list, block_owner, block_fill, old_centroids, codebook):
    devices = lax.axis_size("dev")
    blk = row_list.shape[0] // block_owner.shape[0]
    sub = codebook.shape[1]
    width = vectors.shape[1]
    book = extended_book(codebook)
    send = build_send(vectors, row_list, block_owner, block_fill, devices)
    recv = lax.all_to_all(send, "dev", split_axis=0, concat_axis=0, tiled=True)
    centroids, resid, weight, moment, total = update_lists(recv, old_centroids, blk, sub)

    half = moment.shape[0] // 2
    first, second = moment[:half], moment[half:]
    row = lax.broadcasted_iota(jnp.int32, first.shape, 1)
    column = lax.broadcasted_iota(jnp.int32, first.shape, 2) % sub
    diagonal = jnp.sum(jnp.where(row == column, second, 0.0), axis=1)
    packed = jnp.concatenate(
        [
            jnp.where(row <= column, first, second).reshape(half * sub, LANES),
            jnp.pad(diagonal, ((0, 8 - half), (0, 0))),
        ],
        axis=0,
    )
    stride = 1
    while stride < devices:
        pairs = [(i, i ^ stride) for i in range(devices)]
        packed = packed + lax.ppermute(packed, "dev", pairs)
        stride *= 2
    groups = resid.shape[0]
    parts = 4
    errors = [
        row_errors(resid, weight, book, sub, p * groups // parts, groups // parts)
        for p in range(parts)
    ]
    slot_error = jnp.concatenate([e[:, 0, :] for e in errors], axis=0).reshape(devices, blk)
    across = LANES // sub
    upper = packed[: half * sub].reshape(half, sub, across, sub).transpose(0, 2, 1, 3)
    diagonal = packed[half * sub : half * sub + half].reshape(half, across, 1, sub)
    row = lax.broadcasted_iota(jnp.int32, upper.shape, 2)
    column = lax.broadcasted_iota(jnp.int32, upper.shape, 3)
    flipped = upper.transpose(0, 1, 3, 2)
    one = jnp.where(row <= column, upper, flipped)
    other = jnp.where(row > column, upper, jnp.where(row < column, flipped, diagonal))
    moments = jnp.concatenate([one, other], axis=0).reshape(2 * half * across, sub, sub)
    return centroids, slot_error, moments / total[0, 0]


def solution(mesh):
    return jax.shard_map(
        body,
        mesh=mesh,
        in_specs=(P("dev", None), P("dev"), P("dev"), P("dev"), P("dev", None), P()),
        out_specs=(P("dev", None), P("dev", None), P()),
        check_vma=False,
    )
```

time: 391 us -> 171 us (0.44)
  waiting for transfers between devices: 152 us -> 85.5 us
  blocking collectives: 65.4 us -> 0 us
  local copies, waits for them, and re-layouts: 65.1 us -> 6.45 us
  Pallas kernels: 0 us -> 51.5 us
  matrix products: 34 us -> 0 us
  other arithmetic: 31.4 us -> 5.08 us
  between operations: 14.1 us -> 0.84 us
  starting transfers between devices: 26.2 us -> 21.4 us
    psum x1 -> x0, waiting for transfers between devices: 76.8 us -> none  [body(): moment_all, total_all = lax.psum((moment_sum, local_total), 'dev')]
    psum x1 -> x0, blocking collectives: 65.4 us -> none  [body(): moment_all, total_all = lax.psum((moment_sum, local_total), 'dev')]
    pallas_call x0 -> x6, Pallas kernels: none -> 51.5 us  [the longest x1 24.6 us: update_lists(): pl.pallas_call(functools.partial(update_kernel, blk), grid=(2 * groups,),...]
    dot_general x9 -> x0, matrix products: 34 us -> none  [the longest x4 24.6 us: error_terms(): jnp.einsum('mdr,mdk->mkr', pieces, codebook, preferred_element_type=jnp.f...]
    gather x4 -> x0, local copies, waits for them, and re-layouts: 21.4 us -> none  [quantize(): picked = jnp.take(centroids, slot_lists.reshape(count_rows), axis=0)]
    all_to_all x3 -> x1, starting transfers between devices: 26.2 us -> 11.6 us  [body(): recv = lax.all_to_all(send, 'dev', split_axis=0, concat_axis=0, tiled=True)]
    ppermute x0 -> x7, starting transfers between devices: none -> 9.82 us  [body(): packed = packed + lax.ppermute(packed, 'dev', pairs)]
    dynamic_slice x8 -> x0, local copies, waits for them, and re-layouts: 9.54 us -> none  [body(): lax.scan(visit, zero_moment, (recv_rows.reshape(round_count, slot_group,...]
  transfers between devices with their start and end apart: 4 -> 8, of which waited for: 4 -> 4; matrix products, arithmetic and copies ran while one was open for 5% -> 4% of each run, Pallas kernels for 0% -> 14%
where the time goes in v1:
time: 171 us
  waiting for transfers between devices  85.5 us (50%)
  Pallas kernels  51.5 us (30%)
  starting transfers between devices  21.4 us (13%)
  local copies, waits for them, and re-layouts  6.45 us (4%)
  other arithmetic  5.08 us (3%)
    all_to_all x1, waiting for transfers between devices, body(): recv = lax.all_to_all(send, 'dev', split_axis=0, concat_axis=0, tiled=True)  76.5 us
    pallas_call x1, Pallas kernels, update_lists(): pl.pallas_call(functools.partial(update_kernel, blk), grid=(2 * groups,),...  24.6 us
    pallas_call x4, Pallas kernels, row_errors(): pl.pallas_call(functools.partial(error_kernel, sub), grid=(count,), out_s...  23.5 us
    all_to_all x1, starting transfers between devices, body(): recv = lax.all_to_all(send, 'dev', split_axis=0, concat_axis=0, tiled=True)  11.6 us
    ppermute x7, starting transfers between devices, body(): packed = packed + lax.ppermute(packed, 'dev', pairs)  9.82 us
    ppermute x7, waiting for transfers between devices, body(): packed = packed + lax.ppermute(packed, 'dev', pairs)  8.96 us
  transfers between devices with their start and end apart: 8, of which 4 were waited for; matrix products, arithmetic and copies ran while one was open for 4% of the time, Pallas kernels for 14%

profile of v1, /device:TPU:0, one launch (start us, length us, event | category | flops | bytes accessed | tf_op | source)
XLA Modules:
  0.0 170.8 jit_solution(1482510308230956355)
XLA Ops:
  0.6 3.4 %build_send.1 = bf16[128,208,128]{2,1,0:T(8,128)(2,1)} custom-call(s32[32]{0:T(128)} %owner_ref.1, s32[32]{0:T(128)} %fill_ref.1, bf16[1024,768]{1,0:T(8,128)(2,1)} %vec_ref.1, s32[8,128]{1,0:T(8,128)} %bitcast.32), custom_call_target="tpu_custom_call" | custom-call | tf_op jit(solution)/shard_map/build_send/pallas_call | solution.py:62
  4.0 11.6 %all-to-all-start = ((bf16[128,208,128]{2,1,0:T(8,128)(2,1)}), bf16[128,208,128]{2,1,0:T(8,128)(2,1)}, u32[]{:S(2)}, u32[]{:S(2)}) async-start(bf16[128,208,128]{2,1,0:T(8,128)(2,1)} %build_send.1), calls=%async_computation | async-start | bytes 13631488 | tf_op jit(solution)/shard_map/all_to_all | solution.py:286
  15.7 0.6 copy.44
  16.3 0.1 multiply_reduce_fusion
  16.5 1.6 copy.45
  18.1 0.4 fusion.2
  18.4 1.0 copy-done
  19.5 2.1 %fusion.1.book_ref = bf16[24,256,48]{2,1,0:T(8,128)(2,1)} fusion(bf16[24,256,3]{2,1,0:T(8,128)(2,1)S(1)} %copy-done, bf16[24,256,32]{2,1,0:T(8,128)(2,1)S(1)} %fusion.2), kind=kLoop, calls=%fused_computation.3 | loop fusion | flops 1769472 | bytes 1019904 | tf_op jit(solution)/shard_map/concatenate | solution.py:276
  21.6 76.5 %all-to-all-done.recv_ref = bf16[128,208,128]{2,1,0:T(8,128)(2,1)} async-done(((bf16[128,208,128]{2,1,0:T(8,128)(2,1)}), bf16[128,208,128]{2,1,0:T(8,128)(2,1)}, u32[]{:S(2)}, u32[]{:S(2)}) %all-to-all-start) | async-done | bytes 6815776 | tf_op jit(solution)/shard_map/all_to_all | solution.py:286
  98.2 24.6 %update_lists.1 = (f32[512,768]{1,0:T(8,128)}, bf16[8,768,512]{2,1,0:T(8,128)(2,1)}, f32[8,8,512]{2,1,0:T(8,128)}, f32[6,32,128]{2,1,0:T(8,128)}, f32[8,128]{1,0:T(8,128)}) custom-call(bf16[128,208,128]{2,1,0:T(8,128)(2,1)} %all-to-all-done.recv_ref, f32[512,768]{1,0:T(8,128)} %old_ref.1), custom_call_target="tpu_custom_call" | custom-call | tf_op jit(solution)/shard_map/update_lists/pallas_call | solution.py:184
  122.7 0.8 slice_select_fusion
  123.6 0.1 collective-permute-start
  123.7 5.9 %row_errors.5 = f32[2,8,512]{2,1,0:T(8,128)} custom-call(bf16[8,768,512]{2,1,0:T(8,128)(2,1)} %get-tuple-element.9.resid_ref, f32[8,8,512]{2,1,0:T(8,128)} %get-tuple-element.10.weight_ref, bf16[24,256,48]{2,1,0:T(8,128)(2,1)} %fusion.1.book_ref), custom_call_target="tpu_custom_call" | custom-call | flops 3221225472 | bytes 1572864 | tf_op jit(solution)/shard_map/row_errors/pallas_call | solution.py:246
  129.6 3.2 %collective-permute-start.1 = (f32[104,128]{1,0:T(8,128)S(1)}, f32[104,128]{1,0:T(8,128)S(1)}, u32[]{:S(2)}, u32[]{:S(2)}) collective-permute-start(f32[104,128]{1,0:T(8,128)S(1)} %fusion.6), channel_id=1, source_target_pairs={{0,2},{1,3},{2,0},{3,1},{4,6},{5,7},{6,4},{7,5},{8,10},{9,11},{10,... | collective-permute-start | bytes 159752 | tf_op jit(solution)/shard_map/ppermute | solution.py:304
  132.7 5.9 %row_errors.6 = f32[2,8,512]{2,1,0:T(8,128)} custom-call(bf16[8,768,512]{2,1,0:T(8,128)(2,1)} %get-tuple-element.9.resid_ref, f32[8,8,512]{2,1,0:T(8,128)} %get-tuple-element.10.weight_ref, bf16[24,256,48]{2,1,0:T(8,128)(2,1)} %fusion.1.book_ref), custom_call_target="tpu_custom_call" | custom-call | flops 3221225472 | bytes 1572864 | tf_op jit(solution)/shard_map/row_errors/pallas_call | solution.py:246
  138.6 0.3 collective-permute-start.2
  138.9 5.9 %row_errors.7 = f32[2,8,512]{2,1,0:T(8,128)} custom-call(bf16[8,768,512]{2,1,0:T(8,128)(2,1)} %get-tuple-element.9.resid_ref, f32[8,8,512]{2,1,0:T(8,128)} %get-tuple-element.10.weight_ref, bf16[24,256,48]{2,1,0:T(8,128)(2,1)} %fusion.1.book_ref), custom_call_target="tpu_custom_call" | custom-call | flops 3221225472 | bytes 1572864 | tf_op jit(solution)/shard_map/row_errors/pallas_call | solution.py:246
  144.8 2.5 %collective-permute-start.3 = (f32[104,128]{1,0:T(8,128)S(1)}, f32[104,128]{1,0:T(8,128)S(1)}, u32[]{:S(2)}, u32[]{:S(2)}) collective-permute-start(f32[104,128]{1,0:T(8,128)S(1)} %add.37), channel_id=1, source_target_pairs={{0,8},{1,9},{2,10},{3,11},{4,12},{5,13},{6,14},{7,15},{8,0},{9,1},... | collective-permute-start | bytes 159752 | tf_op jit(solution)/shard_map/ppermute | solution.py:304
  147.3 5.9 %row_errors.4 = f32[2,8,512]{2,1,0:T(8,128)} custom-call(bf16[8,768,512]{2,1,0:T(8,128)(2,1)} %get-tuple-element.9.resid_ref, f32[8,8,512]{2,1,0:T(8,128)} %get-tuple-element.10.weight_ref, bf16[24,256,48]{2,1,0:T(8,128)(2,1)} %fusion.1.book_ref), custom_call_target="tpu_custom_call" | custom-call | flops 3221225472 | bytes 1572864 | tf_op jit(solution)/shard_map/row_errors/pallas_call | solution.py:246
  153.2 0.6 collective-permute-start.4
  153.8 0.8 slice.36
  154.6 4.3 %collective-permute-done.4 = f32[104,128]{1,0:T(8,128)S(1)} collective-permute-done((f32[104,128]{1,0:T(8,128)S(1)}, f32[104,128]{1,0:T(8,128)S(1)}, u32[]{:S(2)}, u32[]{:S(2)}) %collective-permute-start.4) | collective-permute-done | bytes 53280 | tf_op jit(solution)/shard_map/ppermute | solution.py:304
  158.9 0.1 collective-permute-start.5
  159.0 4.1 %collective-permute-done.5 = f32[104,128]{1,0:T(8,128)S(1)} collective-permute-done((f32[104,128]{1,0:T(8,128)S(1)}, f32[104,128]{1,0:T(8,128)S(1)}, u32[]{:S(2)}, u32[]{:S(2)}) %collective-permute-start.5) | collective-permute-done | bytes 53280 | tf_op jit(solution)/shard_map/ppermute | solution.py:304
  163.1 3.2 %collective-permute-start.6 = (f32[104,128]{1,0:T(8,128)S(1)}, f32[104,128]{1,0:T(8,128)S(1)}, u32[]{:S(2)}, u32[]{:S(2)}) collective-permute-start(f32[104,128]{1,0:T(8,128)S(1)} %add.40), channel_id=1, source_target_pairs={{0,64},{1,65},{2,66},{3,67},{4,68},{5,69},{6,70},{7,71},{8,72},{9,... | collective-permute-start | bytes 159752 | tf_op jit(solution)/shard_map/ppermute | solution.py:304
  166.3 1.3 slice.35
  167.7 0.7 copy.51
  168.4 0.5 collective-permute-done.6
  168.9 0.1 reshape.53
  169.0 0.1 copy.50
  169.2 0.1 broadcast_in_dim.15
  169.3 1.5 maximum_divide_fusion
  (32 shorter events, 0.3 us)
Async XLA Ops:
  4.0 11.6 %copy-start.1 = (bf16[24,32,256]{2,1,0:T(8,128)(2,1)S(1)}, bf16[24,32,256]{2,1,0:T(8,128)(2,1)}, u32[]{:S(2)}) copy-start(bf16[24,32,256]{2,1,0:T(8,128)(2,1)} %param.11) | copy-start | bytes 1179652
  4.0 94.1 %all-to-all-start = ((bf16[128,208,128]{2,1,0:T(8,128)(2,1)}), bf16[128,208,128]{2,1,0:T(8,128)(2,1)}, u32[]{:S(2)}, u32[]{:S(2)}) async-start(bf16[128,208,128]{2,1,0:T(8,128)(2,1)} %build_send.1), calls=%async_computation | async-start | bytes 13631488 | tf_op jit(solution)/shard_map/all_to_all | solution.py:286
  18.1 1.4 copy-start
  123.6 6.0 %collective-permute-start = (f32[104,128]{1,0:T(8,128)S(1)}, f32[104,128]{1,0:T(8,128)S(1)}, u32[]{:S(2)}, u32[]{:S(2)}) collective-permute-start(f32[104,128]{1,0:T(8,128)S(1)} %select_maximum_fusion), channel_id=1, source_target_pairs={{0,1},{1,0},{2,3},{3,2},{4,5},{5,4},{6,7},{7,6},{8,9},{9,8},{10,11... | collective-permute-start | bytes 159752 | tf_op jit(solution)/shard_map/ppermute | solution.py:304
  129.6 9.0 %collective-permute-start.1 = (f32[104,128]{1,0:T(8,128)S(1)}, f32[104,128]{1,0:T(8,128)S(1)}, u32[]{:S(2)}, u32[]{:S(2)}) collective-permute-start(f32[104,128]{1,0:T(8,128)S(1)} %fusion.6), channel_id=1, source_target_pairs={{0,2},{1,3},{2,0},{3,1},{4,6},{5,7},{6,4},{7,5},{8,10},{9,11},{10,... | collective-permute-start | bytes 159752 | tf_op jit(solution)/shard_map/ppermute | solution.py:304
  138.6 6.2 %collective-permute-start.2 = (f32[104,128]{1,0:T(8,128)S(1)}, f32[104,128]{1,0:T(8,128)S(1)}, u32[]{:S(2)}, u32[]{:S(2)}) collective-permute-start(f32[104,128]{1,0:T(8,128)S(1)} %add.36), channel_id=1, source_target_pairs={{0,4},{1,5},{2,6},{3,7},{4,0},{5,1},{6,2},{7,3},{8,12},{9,13},{10,... | collective-permute-start | bytes 159752 | tf_op jit(solution)/shard_map/ppermute | solution.py:304
  144.8 9.0 %slice-start = ((f32[2,8,512]{2,1,0:T(8,128)}), f32[2,1,512]{2,1,0:T(1,128)S(1)}, s32[]{:S(2)}) async-start(f32[2,8,512]{2,1,0:T(8,128)} %row_errors.5), calls=%async_computation.1 | async-start | bytes 8192 | tf_op jit(solution)/shard_map/slice | solution.py:312
  144.8 9.0 %slice-start.2 = ((f32[2,8,512]{2,1,0:T(8,128)}), f32[2,1,512]{2,1,0:T(1,128)S(1)}, s32[]{:S(2)}) async-start(f32[2,8,512]{2,1,0:T(8,128)} %row_errors.6), calls=%async_computation.3 | async-start | bytes 8192 | tf_op jit(solution)/shard_map/slice | solution.py:312
  144.8 14.2 %slice-start.1 = ((f32[2,8,512]{2,1,0:T(8,128)}), f32[2,1,512]{2,1,0:T(1,128)S(1)}, s32[]{:S(2)}) async-start(f32[2,8,512]{2,1,0:T(8,128)} %row_errors.7), calls=%async_computation.2 | async-start | bytes 8192 | tf_op jit(solution)/shard_map/slice | solution.py:312
  144.8 8.3 %collective-permute-start.3 = (f32[104,128]{1,0:T(8,128)S(1)}, f32[104,128]{1,0:T(8,128)S(1)}, u32[]{:S(2)}, u32[]{:S(2)}) collective-permute-start(f32[104,128]{1,0:T(8,128)S(1)} %add.37), channel_id=1, source_target_pairs={{0,8},{1,9},{2,10},{3,11},{4,12},{5,13},{6,14},{7,15},{8,0},{9,1},... | collective-permute-start | bytes 159752 | tf_op jit(solution)/shard_map/ppermute | solution.py:304
  153.2 5.7 %collective-permute-start.4 = (f32[104,128]{1,0:T(8,128)S(1)}, f32[104,128]{1,0:T(8,128)S(1)}, u32[]{:S(2)}, u32[]{:S(2)}) collective-permute-start(f32[104,128]{1,0:T(8,128)S(1)} %add.38), channel_id=1, source_target_pairs={{0,16},{1,17},{2,18},{3,19},{4,20},{5,21},{6,22},{7,23},{8,24},{9,... | collective-permute-start | bytes 159752 | tf_op jit(solution)/shard_map/ppermute | solution.py:304
  158.9 4.2 %collective-permute-start.5 = (f32[104,128]{1,0:T(8,128)S(1)}, f32[104,128]{1,0:T(8,128)S(1)}, u32[]{:S(2)}, u32[]{:S(2)}) collective-permute-start(f32[104,128]{1,0:T(8,128)S(1)} %add.39), channel_id=1, source_target_pairs={{0,32},{1,33},{2,34},{3,35},{4,36},{5,37},{6,38},{7,39},{8,40},{9,... | collective-permute-start | bytes 159752 | tf_op jit(solution)/shard_map/ppermute | solution.py:304
  163.1 5.7 %collective-permute-start.6 = (f32[104,128]{1,0:T(8,128)S(1)}, f32[104,128]{1,0:T(8,128)S(1)}, u32[]{:S(2)}, u32[]{:S(2)}) collective-permute-start(f32[104,128]{1,0:T(8,128)S(1)} %add.40), channel_id=1, source_target_pairs={{0,64},{1,65},{2,66},{3,67},{4,68},{5,69},{6,70},{7,71},{8,72},{9,... | collective-permute-start | bytes 159752 | tf_op jit(solution)/shard_map/ppermute | solution.py:304

commit v2 on v1

v2 whole, which is shorter than its diff:
```python
import functools

import jax
import jax.numpy as jnp
from jax import lax
from jax.experimental import pallas as pl
from jax.experimental.pallas import tpu as pltpu
from jax.sharding import PartitionSpec as P

LANES = 128
META = 16
AUG = 16
GROUP = 256
VMEM = 56 * 1024 * 1024


def send_kernel(blk, owner_ref, fill_ref, vec_ref, list_ref, send_ref, tiles, meta, sems):
    blocks = owner_ref.shape[0]
    width = vec_ref.shape[1]
    chunks = width // LANES
    span = LANES // blk
    me = lax.axis_index("dev")
    place = lax.rem(me, span)
    for j in range(chunks):
        tiles[:, j * blk : (j + 1) * blk, :] = vec_ref[:, j * LANES : (j + 1) * LANES].reshape(
            blocks, blk, LANES
        )
    copies = []
    for b in range(blocks):
        copy = pltpu.make_async_copy(
            tiles.at[b], send_ref.at[owner_ref[b], pl.ds(0, chunks * blk), :], sems.at[b]
        )
        copy.start()
        copies.append(copy)
    total = functools.reduce(lambda a, b: a + b, [fill_ref[b] for b in range(blocks)])
    rows = lax.broadcasted_iota(jnp.int32, (META, LANES), 0)
    lane = lax.broadcasted_iota(jnp.int32, (1, LANES), 1)
    base = jnp.where(rows == 3, total >> 8, jnp.where(rows == 4, total & 255, 0))
    meta[...] = jnp.broadcast_to(base.astype(jnp.float32).astype(jnp.bfloat16)[None], meta.shape)
    for b in range(blocks):
        line = list_ref[b // span : b // span + 1, :] + 1
        line = pltpu.roll(line, lax.rem(place + span - b % span, span) * blk, 1)
        kept = (lane // blk == place) & (lax.rem(lane, blk) < fill_ref[b])
        line = jnp.broadcast_to(jnp.where(kept, line, 0), (META, LANES))
        count = jnp.broadcast_to(jnp.where(lane == me, fill_ref[b], 0), (META, LANES))
        tile = jnp.where(
            rows == 0, line & 255, jnp.where(rows == 1, line >> 8, jnp.where(rows == 2, count, base))
        )
        meta[owner_ref[b]] = tile.astype(jnp.float32).astype(jnp.bfloat16)
    last = pltpu.make_async_copy(
        meta, send_ref.at[:, pl.ds(chunks * blk, META), :], sems.at[blocks]
    )
    last.start()
    for copy in copies:
        copy.wait()
    last.wait()


def build_send(vectors, row_list, block_owner, block_fill, devices):
    rows, width = vectors.shape
    blocks = block_owner.shape[0]
    blk = rows // blocks
    height = width // LANES * blk
    return pl.pallas_call(
        functools.partial(send_kernel, blk),
        out_shape=jax.ShapeDtypeStruct((devices, height + META, LANES), jnp.bfloat16),
        in_specs=[
            pl.BlockSpec(memory_space=pltpu.SMEM),
            pl.BlockSpec(memory_space=pltpu.SMEM),
            pl.BlockSpec(memory_space=pltpu.VMEM),
            pl.BlockSpec(memory_space=pltpu.VMEM),
        ],
        out_specs=pl.BlockSpec(memory_space=pl.ANY),
        scratch_shapes=[
            pltpu.VMEM((blocks, height, LANES), jnp.bfloat16),
            pltpu.VMEM((devices, META, LANES), jnp.bfloat16),
            pltpu.SemaphoreType.DMA((blocks + 1,)),
        ],
        compiler_params=pltpu.CompilerParams(vmem_limit_bytes=VMEM),
        name="build_send",
    )(block_owner, block_fill, vectors, row_list.reshape(rows // LANES, LANES))


def update_kernel(
    blk, recv_ref, old_ref, cent_ref, resid_ref, place_ref, packed_ref, total_ref,
    blocks, info, old, dense, hot, turned, column, where_ref, sums, counts, parts, gram, final, sems, out_sems,
):
    slots, height, _ = recv_ref.shape
    lists, width = old_ref.shape
    chunks = width // LANES
    span = LANES // blk
    some = slots // blocks.shape[0]
    rows = slots * blk

    notes = pltpu.make_async_copy(recv_ref.at[:, pl.ds(chunks * blk, META), :], info, sems.at[0])
    notes.start()

    def fetch(c):
        return pltpu.make_async_copy(
            recv_ref.at[pl.ds(c * some, some), pl.ds(0, chunks * blk), :], blocks.at[c], sems.at[1 + c]
        )

    for c in range(blocks.shape[0]):
        fetch(c).start()

    own = pltpu.make_async_copy(old_ref, old, sems.at[1 + blocks.shape[0]])
    own.start()
    notes.wait()
    lines, seen = [], jnp.zeros((META, LANES), jnp.float32)
    for q in range(slots // span):
        note = info[q * span].astype(jnp.float32)
        for s in range(1, span):
            note = note + info[q * span + s].astype(jnp.float32)
        lines.append(note[0:1] + 256.0 * note[1:2])
        seen = seen + note
    fill = jnp.broadcast_to(seen[2:3], (8, LANES))
    before = lax.broadcasted_iota(jnp.int32, (slots, slots), 0)
    after = lax.broadcasted_iota(jnp.int32, (slots, slots), 1)
    start = jnp.dot(
        fill.astype(jnp.bfloat16),
        jnp.where(before < after, 1.0, 0.0).astype(jnp.bfloat16),
        preferred_element_type=jnp.float32,
    )
    which = lax.broadcasted_iota(jnp.int32, (8, slots), 0)
    where_ref[...] = jnp.where(which == 0, start, fill).astype(jnp.int32)
    mover = pltpu.make_async_copy(where_ref, place_ref, sems.at[0])
    mover.start()
    total_ref[...] = jnp.broadcast_to(seen[4:5] + 256.0 * seen[3:4], total_ref.shape)
    lines.append(jnp.zeros((LANES - len(lines), LANES), jnp.float32))
    column[...] = jnp.concatenate(lines, axis=0).T
    sums[...] = jnp.zeros_like(sums)
    counts[...] = jnp.zeros_like(counts)
    gram[...] = jnp.zeros_like(gram)
    mover.wait()

    lane = lax.broadcasted_iota(jnp.int32, (blk, LANES), 1)

    def pack(c, carry):
        fetch(c).wait()
        for s in range(some):
            at = pl.ds(place_ref[0, c * some + s], blk)
            for j in range(chunks):
                dense[j, at, :] = blocks[c, s, j * blk : (j + 1) * blk, :].astype(jnp.float32)
            ids = column[(s % span) * blk : (s % span + 1) * blk, :]
            dense[chunks, at, :] = jnp.where(lane == c * (some // span) + s // span, ids, 0.0)
        return carry

    lax.fori_loop(0, blocks.shape[0], pack, 0)
    used = place_ref[0, slots - 1] + place_ref[1, slots - 1]
    for j in range(chunks + 1):
        dense[j, pl.ds(used, GROUP + blk), :] = jnp.zeros((GROUP + blk, LANES), jnp.float32)
    groups = (used + GROUP - 1) // GROUP

    def gather(g, carry):
        at = pl.ds(pl.multiple_of(g * GROUP, GROUP), GROUP)
        code = jnp.sum(dense[chunks, at, :].T, axis=0, keepdims=True)
        ids = lax.broadcasted_iota(jnp.int32, (lists, GROUP), 0).astype(jnp.float32) + 1.0
        match = jnp.where(ids == code, 1.0, 0.0)
        chosen = match.astype(jnp.bfloat16)
        hot[g] = chosen
        part = match[:, 0:LANES]
        for k in range(1, GROUP // LANES):
            part = part + match[:, k * LANES : (k + 1) * LANES]
        counts[...] += part
        pieces = []
        for j in range(chunks):
            piece = dense[j, at, :].astype(jnp.bfloat16)
            turned[g, j * LANES : (j + 1) * LANES, :] = piece.T
            pieces.append(piece)
        sums[...] += jnp.dot(
            chosen, jnp.concatenate(pieces, axis=1), preferred_element_type=jnp.float32
        )
        return carry

    lax.fori_loop(0, groups, gather, 0)

    count = jnp.sum(counts[...], axis=1, keepdims=True) + 1.0
    own.wait()
    cent = (sums[...] + old[...]) / count
    final[...] = cent
    write = pltpu.make_async_copy(final, cent_ref, sems.at[0])
    write.start()
    flipped = cent.T
    head = flipped.astype(jnp.bfloat16)
    parts[:, 0:lists] = head
    parts[:, lists : 2 * lists] = (flipped - head.astype(jnp.float32)).astype(jnp.bfloat16)

    wide = 2 * LANES
    lane = lax.broadcasted_iota(jnp.int32, (1, GROUP), 1)

    def leave(g):
        return pltpu.make_async_copy(turned.at[g], resid_ref.at[g], out_sems.at[g])

    def encode(g, carry):
        chosen = hot[g]
        weight = jnp.where(lane < used - g * GROUP, 1.0, 0.0)
        both = jnp.concatenate([chosen, chosen], axis=0)
        resids = []
        for j in range(width // wide):
            at = slice(j * wide, (j + 1) * wide)
            picked = jnp.dot(parts[at], both, preferred_element_type=jnp.float32)
            resids.append(((turned[g, at].astype(jnp.float32) - picked) * weight).astype(jnp.bfloat16))
        for j in range(width // wide):
            turned[g, j * wide : (j + 1) * wide] = resids[j]
        squares = [
            lax.dot_general(r, r, (((1,), (1,)), ((), ())), preferred_element_type=jnp.float32)
            for r in resids
        ]
        for j in range(width // wide):
            gram[j] += squares[j]
        leave(g).start()
        return carry

    lax.fori_loop(0, groups, encode, 0)

    sub = (packed_ref.shape[0] - 8) // (chunks // 2)
    across = LANES // sub
    row = lax.broadcasted_iota(jnp.int32, (sub, LANES), 0)
    lane = lax.broadcasted_iota(jnp.int32, (sub, LANES), 1)
    squares = []
    for q in range(chunks):
        half = slice((q % 2) * LANES, (q % 2 + 1) * LANES)
        square = jnp.zeros((sub, LANES), jnp.float32)
        for a in range(across):
            top = ((q % 2) * across + a) * sub
            square = jnp.where(lane // sub == a, gram[q // 2, top : top + sub, half], square)
        squares.append(square)
    half = chunks // 2
    diagonals = []
    for q in range(half):
        packed_ref[q * sub : (q + 1) * sub, :] = jnp.where(
            row <= lane % sub, squares[q], squares[half + q]
        )
        diagonals.append(
            jnp.sum(jnp.where(row == lane % sub, squares[half + q], 0.0), axis=0, keepdims=True)
        )
    diagonals.append(jnp.zeros((8 - half, LANES), jnp.float32))
    packed_ref[half * sub :, :] = jnp.concatenate(diagonals, axis=0)

    def finish(g, carry):
        leave(g).wait()
        return carry

    lax.fori_loop(0, groups, finish, 0)
    write.wait()


def update_lists(recv, old, blk, sub):
    slots, height, _ = recv.shape
    lists, width = old.shape
    rows = slots * blk
    groups = rows // GROUP
    chunks = width // LANES
    return pl.pallas_call(
        functools.partial(update_kernel, blk),
        out_shape=(
            jax.ShapeDtypeStruct((lists, width), jnp.float32),
            jax.ShapeDtypeStruct((groups, width, GROUP), jnp.bfloat16),
            jax.ShapeDtypeStruct((8, slots), jnp.int32),
            jax.ShapeDtypeStruct((chunks // 2 * sub + 8, LANES), jnp.float32),
            jax.ShapeDtypeStruct((8, LANES), jnp.float32),
        ),
        in_specs=[
            pl.BlockSpec(memory_space=pl.ANY),
            pl.BlockSpec(memory_space=pl.ANY),
        ],
        out_specs=(
            pl.BlockSpec(memory_space=pl.ANY),
            pl.BlockSpec(memory_space=pl.ANY),
            pl.BlockSpec(memory_space=pltpu.SMEM),
            pl.BlockSpec(memory_space=pltpu.VMEM),
            pl.BlockSpec(memory_space=pltpu.VMEM),
        ),
        scratch_shapes=[
            pltpu.VMEM((8, slots // 8, chunks * blk, LANES), jnp.bfloat16),
            pltpu.VMEM((slots, META, LANES), jnp.bfloat16),
            pltpu.VMEM((lists, width), jnp.float32),
            pltpu.VMEM((chunks + 1, rows + GROUP + blk, LANES), jnp.float32),
            pltpu.VMEM((groups, lists, GROUP), jnp.bfloat16),
            pltpu.VMEM((groups, width, GROUP), jnp.bfloat16),
            pltpu.VMEM((LANES, LANES), jnp.float32),
            pltpu.VMEM((8, slots), jnp.int32),
            pltpu.VMEM((lists, width), jnp.float32),
            pltpu.VMEM((lists, LANES), jnp.float32),
            pltpu.VMEM((width, 2 * lists), jnp.bfloat16),
            pltpu.VMEM((width // (2 * LANES), 2 * LANES, 2 * LANES), jnp.float32),
            pltpu.VMEM((lists, width), jnp.float32),
            pltpu.SemaphoreType.DMA((10,)),
            pltpu.SemaphoreType.DMA((groups,)),
        ],
        compiler_params=pltpu.CompilerParams(vmem_limit_bytes=VMEM),
        name="update_lists",
    )(recv, old)


def error_kernel(sub, part, pieces, blk, place_ref, resid_ref, book_ref, before_ref, error_ref, *rest):
    slot_ref = rest[0] if part == pieces - 1 else None
    held, sems = rest[-2:]
    subspaces = book_ref.shape[0]
    slots = place_ref.shape[1]
    width = subspaces * sub
    used = place_ref[0, slots - 1] + place_ref[1, slots - 1]
    groups = (used + GROUP - 1) // GROUP
    first, last = part * groups // pieces, (part + 1) * groups // pieces
    error_ref[...] = before_ref[...]

    def fetch(g):
        at = lax.rem(g, 2)
        return pltpu.make_async_copy(resid_ref.at[g], held.at[at], sems.at[at])

    @pl.when(first < last)
    def _():
        fetch(first).start()

    ones = jnp.ones((AUG, GROUP), jnp.bfloat16)

    def visit(g, carry):
        @pl.when(g + 1 < last)
        def _():
            fetch(g + 1).start()

        fetch(g).wait()
        at = lax.rem(g, 2)
        norm = jnp.zeros((8, GROUP), jnp.float32)
        least = jnp.zeros((1, GROUP), jnp.float32)
        for m in range(subspaces):
            piece = held[at, m * sub : (m + 1) * sub, :]
            long = piece.astype(jnp.float32)
            square = long * long
            for k in range(sub // 8):
                norm = norm + square[k * 8 : (k + 1) * 8]
            distance = jnp.dot(
                book_ref[m],
                jnp.concatenate([piece, ones], axis=0),
                preferred_element_type=jnp.float32,
            )
            least = least + jnp.min(distance, axis=0, keepdims=True)
        error = (least + jnp.sum(norm, axis=0, keepdims=True)) / width
        for k in range(GROUP // LANES):
            error_ref[pl.ds(g * (GROUP // LANES) + k, 1), :] = error[:, k * LANES : (k + 1) * LANES]
        return carry

    lax.fori_loop(first, last, visit, 0)

    if slot_ref is not None:
        lane = lax.broadcasted_iota(jnp.int32, (1, LANES), 1)
        for s in range(slots):
            start = place_ref[0, s]
            line = start // LANES
            shift = lax.rem(start, LANES)
            window = jnp.where(
                lane >= shift, error_ref[pl.ds(line, 1), :], error_ref[pl.ds(line + 1, 1), :]
            )
            window = pltpu.roll(window, lax.rem(LANES - shift, LANES), 1)
            window = jnp.where(lane < place_ref[1, s], window, 0.0)
            slot_ref[s : s + 1, :] = window[:, 0:blk]


def row_errors(place, resid, book, before, sub, blk, part, pieces):
    groups, width, _ = resid.shape
    subspaces, codes, depth = book.shape
    slots = place.shape[1]
    lines = slots * blk // LANES + 8
    out = [jax.ShapeDtypeStruct((lines, LANES), jnp.float32)]
    if part == pieces - 1:
        out.append(jax.ShapeDtypeStruct((slots, blk), jnp.float32))
    return pl.pallas_call(
        functools.partial(error_kernel, sub, part, pieces, blk),
        out_shape=tuple(out),
        in_specs=[
            pl.BlockSpec(memory_space=pltpu.SMEM),
            pl.BlockSpec(memory_space=pl.ANY),
            pl.BlockSpec(memory_space=pltpu.VMEM),
            pl.BlockSpec(memory_space=pltpu.VMEM),
        ],
        out_specs=tuple(pl.BlockSpec(memory_space=pltpu.VMEM) for _ in out),
        scratch_shapes=[
            pltpu.VMEM((2, width, GROUP), jnp.bfloat16),
            pltpu.SemaphoreType.DMA((2,)),
        ],
        compiler_params=pltpu.CompilerParams(vmem_limit_bytes=VMEM // 2),
        cost_estimate=pl.CostEstimate(
            flops=2 * 256 * codes * subspaces * GROUP * 3,
            bytes_accessed=width * GROUP * 2 * 3,
            transcendentals=0,
        ),
        name="row_errors",
    )(place, resid, book, before)


def unpack_kernel(one_ref, two_ref, three_ref, four_ref, total_ref, out_ref):
    sub = out_ref.shape[1]
    across = LANES // sub
    half = out_ref.shape[0] // across // 2
    packed = (one_ref[...] + two_ref[...]) + (three_ref[...] + four_ref[...])
    share = 1.0 / total_ref[0:1, 0:1]
    row = lax.broadcasted_iota(jnp.int32, (sub, sub), 0)
    lane = lax.broadcasted_iota(jnp.int32, (sub, sub), 1)
    for q in range(half):
        square = packed[q * sub : (q + 1) * sub]
        turned = square.T
        for a in range(across):
            at = slice(a * sub, (a + 1) * sub)
            here, flip = square[:, at], turned[at]
            diagonal = packed[half * sub + q : half * sub + q + 1, at]
            out_ref[q * across + a] = jnp.where(row <= lane, here, flip) * share
            other = jnp.where(row > lane, here, jnp.where(row < lane, flip, diagonal))
            out_ref[(half + q) * across + a] = other * share


def unpack_moments(terms, total, subspaces, sub):
    return pl.pallas_call(
        unpack_kernel,
        out_shape=jax.ShapeDtypeStruct((subspaces, sub, sub), jnp.float32),
        name="unpack_moments",
    )(*terms, total)


def extended_book(codebook):
    values = codebook.astype(jnp.float32)
    rest = jnp.sum(jnp.square(values), axis=1)
    parts = []
    for _ in range(3):
        part = lax.reduce_precision(rest, 8, 7)
        parts.append(part)
        rest = rest - part
    parts = jnp.stack(parts, axis=2)
    parts = jnp.pad(parts, ((0, 0), (0, 0), (0, AUG - 3)))
    return jnp.concatenate([-2.0 * values.transpose(0, 2, 1), parts], axis=2).astype(jnp.bfloat16)


def body(vectors, row_list, block_owner, block_fill, old_centroids, codebook):
    devices = lax.axis_size("dev")
    blk = row_list.shape[0] // block_owner.shape[0]
    sub = codebook.shape[1]
    width = vectors.shape[1]
    book = extended_book(codebook)
    send = build_send(vectors, row_list, block_owner, block_fill, devices)
    recv = lax.all_to_all(send, "dev", split_axis=0, concat_axis=0, tiled=True)
    centroids, resid, place, packed, total = update_lists(recv, old_centroids, blk, sub)
    pieces = 4
    errors = jnp.zeros((devices * blk // LANES + 8, LANES), jnp.float32)
    slot_error = None
    for part in range(pieces):
        out = row_errors(place, resid, book, errors, sub, blk, part, pieces)
        errors, slot_error = out[0], out[-1]

    def partner(step):
        return lax.ppermute(packed, "dev", [(i, i ^ step) for i in range(devices)])

    packed = packed + partner(1)
    stride = 2
    while True:
        terms = (packed, partner(stride), partner(2 * stride), partner(3 * stride))
        stride *= 4
        if stride >= devices:
            break
        packed = (terms[0] + terms[1]) + (terms[2] + terms[3])
    moments = unpack_moments(terms, total, codebook.shape[0], sub)
    return centroids, slot_error, moments


def solution(mesh):
    return jax.shard_map(
        body,
        mesh=mesh,
        in_specs=(P("dev", None), P("dev"), P("dev"), P("dev"), P("dev", None), P()),
        out_specs=(P("dev", None), P("dev", None), P()),
        check_vma=False,
    )
```

time: 171 us -> 149 us (0.87)
  Pallas kernels: 51.5 us -> 21.9 us
  starting transfers between devices: 21.4 us -> 31.1 us
  waiting for transfers between devices: 85.5 us -> 82.8 us
    pallas_call x5 -> x6, Pallas kernels: 48.1 us -> 18.5 us  [the longest x1 9.25 us: update_lists(): pl.pallas_call(functools.partial(update_kernel, blk), out_shape=(jax.Shap...]
    ppermute x7 -> x10, starting transfers between devices: 9.82 us -> 19.5 us  [partner(): return lax.ppermute(packed, 'dev', [(i, i ^ step) for i in range(devices)])]
    unnamed x5 -> x17, local copies, waits for them, and re-layouts: 1.73 us -> 4.94 us
    ppermute x7 -> x10, waiting for transfers between devices: 8.96 us -> 6.57 us  [partner(): return lax.ppermute(packed, 'dev', [(i, i ^ step) for i in range(devices)])]
    slice x10 -> x0, local copies, waits for them, and re-layouts: 2.06 us -> none  [the longest x1 1.28 us: body(): return (centroids, slot_error, moments / total[0, 0])]
    mul x1, other arithmetic: 0.36 us -> 2.24 us  [extended_book(): -2.0 * values.transpose(0, 2, 1)]
  transfers between devices with their start and end apart: 8 -> 11, of which waited for: 4 -> 5; matrix products, arithmetic and copies ran while one was open for 4% -> 5% of each run, Pallas kernels for 14% -> 5%
where the time goes in v2:
time: 149 us; the launch traced here: 148 us
  waiting for transfers between devices  82.8 us (56%)
  starting transfers between devices  31.1 us (21%)
  Pallas kernels  21.9 us (15%)
  local copies, waits for them, and re-layouts  7.77 us (5%)
  other arithmetic  3.41 us (2%)
    all_to_all x1, waiting for transfers between devices, body(): recv = lax.all_to_all(send, 'dev', split_axis=0, concat_axis=0, tiled=True)  76.3 us
    ppermute x10, starting transfers between devices, partner(): return lax.ppermute(packed, 'dev', [(i, i ^ step) for i in range(devices)])  19.5 us
    all_to_all x1, starting transfers between devices, body(): recv = lax.all_to_all(send, 'dev', split_axis=0, concat_axis=0, tiled=True)  11.7 us
    pallas_call x1, Pallas kernels, update_lists(): pl.pallas_call(functools.partial(update_kernel, blk), out_shape=(jax.Shap...  9.25 us
    pallas_call x4, Pallas kernels, row_errors(): pl.pallas_call(functools.partial(error_kernel, sub, part, pieces, blk), o...  7.45 us
    ppermute x10, waiting for transfers between devices, partner(): return lax.ppermute(packed, 'dev', [(i, i ^ step) for i in range(devices)])  6.57 us
    unnamed x17, local copies, waits for them, and re-layouts  4.94 us
    pallas_call x1, Pallas kernels, build_send(): pl.pallas_call(functools.partial(send_kernel, blk), out_shape=jax.ShapeDt...  3.38 us
  transfers between devices with their start and end apart: 11, of which 5 were waited for; matrix products, arithmetic and copies ran while one was open for 5% of the time, Pallas kernels for 5%

profile of v2, /device:TPU:0, one launch (start us, length us, event | category | flops | bytes accessed | tf_op | source)
XLA Modules:
  0.0 147.9 jit_solution(2170975297679950430)
XLA Ops:
  0.6 3.4 %build_send.1 = bf16[128,208,128]{2,1,0:T(8,128)(2,1)} custom-call(s32[32]{0:T(128)} %owner_ref.1, s32[32]{0:T(128)} %fill_ref.1, bf16[1024,768]{1,0:T(8,128)(2,1)} %vec_ref.1, s32[8,128]{1,0:T(8,128)} %bitcast.10), custom_call_target="tpu_custom_call" | custom-call | tf_op jit(solution)/shard_map/build_send/pallas_call | solution.py:64
  4.0 11.7 %all-to-all-start = ((bf16[128,208,128]{2,1,0:T(8,128)(2,1)}), bf16[128,208,128]{2,1,0:T(8,128)(2,1)}, u32[]{:S(2)}, u32[]{:S(2)}) async-start(bf16[128,208,128]{2,1,0:T(8,128)(2,1)} %build_send.1), calls=%async_computation | async-start | bytes 13631488 | tf_op jit(solution)/shard_map/all_to_all | solution.py:439
  15.7 1.9 %copy.24 = f32[24,32,256]{1,2,0:T(8,128)} copy(bf16[24,32,256]{2,1,0:T(8,128)(2,1)S(1)} %copy-done.2) | data formatting | bytes 1179648 | tf_op jit(solution)/shard_map/convert_element_type | solution.py:420
  17.6 0.1 multiply_reduce_fusion
  17.8 0.9 copy.25
  18.7 2.2 %fusion.2 = bf16[24,256,32]{2,1,0:T(8,128)(2,1)S(1)} fusion(f32[24,32,256]{1,2,0:T(8,128)} %copy.24), kind=kLoop, calls=%fused_computation.4 | loop fusion | flops 393216 | bytes 1179648 | tf_op jit(solution)/shard_map/mul | solution.py:429
  20.9 1.0 fusion.1.book_ref
  21.9 76.3 %all-to-all-done.recv_ref = bf16[128,208,128]{2,1,0:T(8,128)(2,1)} async-done(((bf16[128,208,128]{2,1,0:T(8,128)(2,1)}), bf16[128,208,128]{2,1,0:T(8,128)(2,1)}, u32[]{:S(2)}, u32[]{:S(2)}) %all-to-all-start) | async-done | bytes 6815776 | tf_op jit(solution)/shard_map/all_to_all | solution.py:439
  98.2 9.2 %update_lists.1 = (f32[512,768]{1,0:T(8,128)}, bf16[16,768,256]{2,1,0:T(8,128)(2,1)}, s32[8,128]{1,0:T(8,128)}, f32[104,128]{1,0:T(8,128)}, f32[8,128]{1,0:T(8,128)}) custom-call(bf16[128,208,128]{2,1,0:T(8,128)(2,1)} %all-to-all-done.recv_ref, f32[512,768]{1,0:T(8,128)} %old_ref.1), custom_call_target="tpu_custom_call" | custom-call | tf_op jit(solution)/shard_map/update_lists/pallas_call | solution.py:254
  107.4 0.1 collective-permute-start
  107.6 2.8 %copy-done = bf16[16,768,256]{2,1,0:T(8,128)(2,1)S(1)} copy-done((bf16[16,768,256]{2,1,0:T(8,128)(2,1)S(1)}, bf16[16,768,256]{2,1,0:T(8,128)(2,1)}, u32[]{:S(2)}) %copy-start) | copy-done | bytes 6291480
  110.3 0.7 copy-done.1
  111.0 0.6 row_errors.4.before_ref
  111.7 0.1 copy-done.7
  111.8 1.8 %collective-permute-start.1 = (f32[104,128]{1,0:T(8,128)S(1)}, f32[104,128]{1,0:T(8,128)S(1)}, u32[]{:S(2)}, u32[]{:S(2)}) collective-permute-start(f32[104,128]{1,0:T(8,128)S(1)} %add.23), channel_id=1, source_target_pairs={{0,2},{1,3},{2,0},{3,1},{4,6},{5,7},{6,4},{7,5},{8,10},{9,11},{10,... | collective-permute-start | bytes 159752 | tf_op jit(solution)/shard_map/ppermute | solution.py:449
  113.6 6.2 %collective-permute-start.2 = (f32[104,128]{1,0:T(8,128)S(1)}, f32[104,128]{1,0:T(8,128)S(1)}, u32[]{:S(2)}, u32[]{:S(2)}) collective-permute-start(f32[104,128]{1,0:T(8,128)S(1)} %add.23), channel_id=1, source_target_pairs={{0,4},{1,5},{2,6},{3,7},{4,0},{5,1},{6,2},{7,3},{8,12},{9,13},{10,... | collective-permute-start | bytes 159752 | tf_op jit(solution)/shard_map/ppermute | solution.py:449
  119.9 0.5 collective-permute-start.3
  120.3 1.8 %row_errors.5.before_ref = f32[40,128]{1,0:T(8,128)S(1)} custom-call(s32[8,128]{1,0:T(8,128)S(1)} %copy-done.1, bf16[16,768,256]{2,1,0:T(8,128)(2,1)S(1)} %copy-done, bf16[24,256,48]{2,1,0:T(8,128)(2,1)S(1)} %fusion.1.book_ref, f32[40,128]{1,0:T(8,128)S(1)} %row_errors.4.before_ref), custom_call_target="tpu_custom_call" | custom-call | flops 2415919104 | bytes 1179648 | tf_op jit(solution)/shard_map/row_errors/pallas_call | solution.py:367
  122.2 0.3 collective-permute-done.2
  122.5 2.8 %collective-permute-done.3 = f32[104,128]{1,0:T(8,128)S(1)} collective-permute-done((f32[104,128]{1,0:T(8,128)S(1)}, f32[104,128]{1,0:T(8,128)S(1)}, u32[]{:S(2)}, u32[]{:S(2)}) %collective-permute-start.3) | collective-permute-done | bytes 53280 | tf_op jit(solution)/shard_map/ppermute | solution.py:449
  125.2 0.1 collective-permute-start.4
  125.3 6.0 %collective-permute-start.5 = (f32[104,128]{1,0:T(8,128)S(1)}, f32[104,128]{1,0:T(8,128)S(1)}, u32[]{:S(2)}, u32[]{:S(2)}) collective-permute-start(f32[104,128]{1,0:T(8,128)S(1)} %add_add_fusion.1), channel_id=1, source_target_pairs={{0,16},{1,17},{2,18},{3,19},{4,20},{5,21},{6,22},{7,23},{8,24},{9,... | collective-permute-start | bytes 159752 | tf_op jit(solution)/shard_map/ppermute | solution.py:449
  131.3 1.8 %row_errors.6.before_ref = f32[40,128]{1,0:T(8,128)S(1)} custom-call(s32[8,128]{1,0:T(8,128)S(1)} %copy-done.1, bf16[16,768,256]{2,1,0:T(8,128)(2,1)S(1)} %copy-done, bf16[24,256,48]{2,1,0:T(8,128)(2,1)S(1)} %fusion.1.book_ref, f32[40,128]{1,0:T(8,128)S(1)} %row_errors.5.before_ref), custom_call_target="tpu_custom_call" | custom-call | flops 2415919104 | bytes 1179648 | tf_op jit(solution)/shard_map/row_errors/pallas_call | solution.py:367
  133.2 0.8 collective-permute-done.5
  134.0 2.7 %collective-permute-done.6 = f32[104,128]{1,0:T(8,128)S(1)} collective-permute-done((f32[104,128]{1,0:T(8,128)S(1)}, f32[104,128]{1,0:T(8,128)S(1)}, u32[]{:S(2)}, u32[]{:S(2)}) %collective-permute-start.6) | collective-permute-done | bytes 53280 | tf_op jit(solution)/shard_map/ppermute | solution.py:449
  136.7 0.1 collective-permute-start.7
  136.8 2.7 %collective-permute-start.8 = (f32[104,128]{1,0:T(8,128)S(1)}, f32[104,128]{1,0:T(8,128)S(1)}, u32[]{:S(2)}, u32[]{:S(2)}) collective-permute-start(f32[104,128]{1,0:T(8,128)S(1)} %add_add_fusion.one_ref), channel_id=1, source_target_pairs={{0,64},{1,65},{2,66},{3,67},{4,68},{5,69},{6,70},{7,71},{8,72},{9,... | collective-permute-start | bytes 159752 | tf_op jit(solution)/shard_map/ppermute | solution.py:449
  139.5 2.0 %collective-permute-start.9 = (f32[104,128]{1,0:T(8,128)S(1)}, f32[104,128]{1,0:T(8,128)S(1)}, u32[]{:S(2)}, u32[]{:S(2)}) collective-permute-start(f32[104,128]{1,0:T(8,128)S(1)} %add_add_fusion.one_ref), channel_id=1, source_target_pairs={{0,96},{1,97},{2,98},{3,99},{4,100},{5,101},{6,102},{7,103},{8,104... | collective-permute-start | bytes 159752 | tf_op jit(solution)/shard_map/ppermute | solution.py:449
  141.5 3.2 %row_errors.7 = (f32[40,128]{1,0:T(8,128)}, f32[128,32]{1,0:T(8,128)S(1)}) custom-call(s32[8,128]{1,0:T(8,128)S(1)} %copy-done.1, bf16[16,768,256]{2,1,0:T(8,128)(2,1)S(1)} %copy-done, bf16[24,256,48]{2,1,0:T(8,128)(2,1)S(1)} %fusion.1.book_ref, f32[40,128]{1,0:T(8,128)S(1)} %row_errors.6.before_ref), custom_call_target="tpu_custom_call" | custom-call | flops 2415919104 | bytes 1179648 | tf_op jit(solution)/shard_map/row_errors/pallas_call | solution.py:367
  144.7 0.7 copy.26
  145.4 0.6 copy-done.4
  146.0 1.8 %unpack_moments.1 = f32[24,32,32]{2,1,0:T(8,128)} custom-call(f32[104,128]{1,0:T(8,128)} %copy-done.3, f32[104,128]{1,0:T(8,128)} %copy-done.4, f32[104,128]{1,0:T(8,128)} %copy-done.5, f32[104,128]{1,0:T(8,128)} %copy-done.6, f32[8,128]{1,0:T(8,128)} %get-tuple-element.14.total_ref), custom_call_target="tpu_custom_call" | custom-call | tf_op jit(solution)/shard_map/unpack_moments/pallas_call | solution.py:412
  (25 shorter events, 0.1 us)
Async XLA Ops:
  4.0 11.7 %copy-start.2 = (bf16[24,32,256]{2,1,0:T(8,128)(2,1)S(1)}, bf16[24,32,256]{2,1,0:T(8,128)(2,1)}, u32[]{:S(2)}) copy-start(bf16[24,32,256]{2,1,0:T(8,128)(2,1)} %param.11) | copy-start | bytes 1179652
  4.0 94.2 %all-to-all-start = ((bf16[128,208,128]{2,1,0:T(8,128)(2,1)}), bf16[128,208,128]{2,1,0:T(8,128)(2,1)}, u32[]{:S(2)}, u32[]{:S(2)}) async-start(bf16[128,208,128]{2,1,0:T(8,128)(2,1)} %build_send.1), calls=%async_computation | async-start | bytes 13631488 | tf_op jit(solution)/shard_map/all_to_all | solution.py:439
  107.4 4.2 %collective-permute-start = (f32[104,128]{1,0:T(8,128)}, f32[104,128]{1,0:T(8,128)S(1)}, u32[]{:S(2)}, u32[]{:S(2)}) collective-permute-start(f32[104,128]{1,0:T(8,128)} %get-tuple-element.13), channel_id=1, source_target_pairs={{0,1},{1,0},{2,3},{3,2},{4,5},{5,4},{6,7},{7,6},{8,9},{9,8},{10,11... | collective-permute-start | bytes 159752 | tf_op jit(solution)/shard_map/ppermute | solution.py:449
  107.5 2.8 %copy-start = (bf16[16,768,256]{2,1,0:T(8,128)(2,1)S(1)}, bf16[16,768,256]{2,1,0:T(8,128)(2,1)}, u32[]{:S(2)}) copy-start(bf16[16,768,256]{2,1,0:T(8,128)(2,1)} %get-tuple-element.11.resid_ref) | copy-start | bytes 18874372
  110.3 0.7 copy-start.1
  111.0 0.8 copy-start.7
  111.8 10.3 %collective-permute-start.1 = (f32[104,128]{1,0:T(8,128)S(1)}, f32[104,128]{1,0:T(8,128)S(1)}, u32[]{:S(2)}, u32[]{:S(2)}) collective-permute-start(f32[104,128]{1,0:T(8,128)S(1)} %add.23), channel_id=1, source_target_pairs={{0,2},{1,3},{2,0},{3,1},{4,6},{5,7},{6,4},{7,5},{8,10},{9,11},{10,... | collective-permute-start | bytes 159752 | tf_op jit(solution)/shard_map/ppermute | solution.py:449
  113.6 8.8 %collective-permute-start.2 = (f32[104,128]{1,0:T(8,128)S(1)}, f32[104,128]{1,0:T(8,128)S(1)}, u32[]{:S(2)}, u32[]{:S(2)}) collective-permute-start(f32[104,128]{1,0:T(8,128)S(1)} %add.23), channel_id=1, source_target_pairs={{0,4},{1,5},{2,6},{3,7},{4,0},{5,1},{6,2},{7,3},{8,12},{9,13},{10,... | collective-permute-start | bytes 159752 | tf_op jit(solution)/shard_map/ppermute | solution.py:449
  119.9 5.3 %collective-permute-start.3 = (f32[104,128]{1,0:T(8,128)S(1)}, f32[104,128]{1,0:T(8,128)S(1)}, u32[]{:S(2)}, u32[]{:S(2)}) collective-permute-start(f32[104,128]{1,0:T(8,128)S(1)} %add.23), channel_id=1, source_target_pairs={{0,6},{1,7},{2,4},{3,5},{4,2},{5,3},{6,0},{7,1},{8,14},{9,15},{10,... | collective-permute-start | bytes 159752 | tf_op jit(solution)/shard_map/ppermute | solution.py:449
  125.2 7.9 %collective-permute-start.4 = (f32[104,128]{1,0:T(8,128)S(1)}, f32[104,128]{1,0:T(8,128)S(1)}, u32[]{:S(2)}, u32[]{:S(2)}) collective-permute-start(f32[104,128]{1,0:T(8,128)S(1)} %add_add_fusion.1), channel_id=1, source_target_pairs={{0,8},{1,9},{2,10},{3,11},{4,12},{5,13},{6,14},{7,15},{8,0},{9,1},... | collective-permute-start | bytes 159752 | tf_op jit(solution)/shard_map/ppermute | solution.py:449
  125.3 8.7 %collective-permute-start.5 = (f32[104,128]{1,0:T(8,128)S(1)}, f32[104,128]{1,0:T(8,128)S(1)}, u32[]{:S(2)}, u32[]{:S(2)}) collective-permute-start(f32[104,128]{1,0:T(8,128)S(1)} %add_add_fusion.1), channel_id=1, source_target_pairs={{0,16},{1,17},{2,18},{3,19},{4,20},{5,21},{6,22},{7,23},{8,24},{9,... | collective-permute-start | bytes 159752 | tf_op jit(solution)/shard_map/ppermute | solution.py:449
  131.3 5.3 %collective-permute-start.6 = (f32[104,128]{1,0:T(8,128)S(1)}, f32[104,128]{1,0:T(8,128)S(1)}, u32[]{:S(2)}, u32[]{:S(2)}) collective-permute-start(f32[104,128]{1,0:T(8,128)S(1)} %add_add_fusion.1), channel_id=1, source_target_pairs={{0,24},{1,25},{2,26},{3,27},{4,28},{5,29},{6,30},{7,31},{8,16},{9,... | collective-permute-start | bytes 159752 | tf_op jit(solution)/shard_map/ppermute | solution.py:449
  136.7 8.0 %copy-start.3 = (f32[104,128]{1,0:T(8,128)}, f32[104,128]{1,0:T(8,128)S(1)}, u32[]{:S(2)}) copy-start(f32[104,128]{1,0:T(8,128)S(1)} %add_add_fusion.one_ref) | copy-start | bytes 159748
  136.7 8.7 %collective-permute-start.7 = (f32[104,128]{1,0:T(8,128)S(1)}, f32[104,128]{1,0:T(8,128)S(1)}, u32[]{:S(2)}, u32[]{:S(2)}) collective-permute-start(f32[104,128]{1,0:T(8,128)S(1)} %add_add_fusion.one_ref), channel_id=1, source_target_pairs={{0,32},{1,33},{2,34},{3,35},{4,36},{5,37},{6,38},{7,39},{8,40},{9,... | collective-permute-start | bytes 159752 | tf_op jit(solution)/shard_map/ppermute | solution.py:449
  136.8 8.6 %collective-permute-start.8 = (f32[104,128]{1,0:T(8,128)S(1)}, f32[104,128]{1,0:T(8,128)S(1)}, u32[]{:S(2)}, u32[]{:S(2)}) collective-permute-start(f32[104,128]{1,0:T(8,128)S(1)} %add_add_fusion.one_ref), channel_id=1, source_target_pairs={{0,64},{1,65},{2,66},{3,67},{4,68},{5,69},{6,70},{7,71},{8,72},{9,... | collective-permute-start | bytes 159752 | tf_op jit(solution)/shard_map/ppermute | solution.py:449
  139.5 5.9 %collective-permute-start.9 = (f32[104,128]{1,0:T(8,128)S(1)}, f32[104,128]{1,0:T(8,128)S(1)}, u32[]{:S(2)}, u32[]{:S(2)}) collective-permute-start(f32[104,128]{1,0:T(8,128)S(1)} %add_add_fusion.one_ref), channel_id=1, source_target_pairs={{0,96},{1,97},{2,98},{3,99},{4,100},{5,101},{6,102},{7,103},{8,104... | collective-permute-start | bytes 159752 | tf_op jit(solution)/shard_map/ppermute | solution.py:449
  145.4 0.6 copy-start.4
  145.4 0.6 copy-start.5
  145.4 0.6 copy-start.6

commit v3 on v2

--- a/solution.py
+++ b/solution.py
@@ -8,30 +8,32 @@
 from jax.sharding import PartitionSpec as P
 
 LANES = 128
-META = 16
+META = 8
 AUG = 16
 GROUP = 256
-VMEM = 56 * 1024 * 1024
-
-
-def send_kernel(blk, owner_ref, fill_ref, vec_ref, list_ref, send_ref, tiles, meta, sems):
+VMEM = 42 * 1024 * 1024
+LARGE_VMEM = 56 * 1024 * 1024
+SMALL_VMEM = 10 * 1024 * 1024
+BOUNDS = ((0, 0), (1, 8), (4, 4), (7, 4), (9, 0))
+
+
+def send_kernel(blk, owner_ref, fill_ref, vec_ref, list_ref, send_ref, held, tiles, meta, sems):
     blocks = owner_ref.shape[0]
     width = vec_ref.shape[1]
     chunks = width // LANES
     span = LANES // blk
     me = lax.axis_index("dev")
     place = lax.rem(me, span)
-    for j in range(chunks):
-        tiles[:, j * blk : (j + 1) * blk, :] = vec_ref[:, j * LANES : (j + 1) * LANES].reshape(
-            blocks, blk, LANES
-        )
-    copies = []
-    for b in range(blocks):
-        copy = pltpu.make_async_copy(
-            tiles.at[b], send_ref.at[owner_ref[b], pl.ds(0, chunks * blk), :], sems.at[b]
-        )
-        copy.start()
-        copies.append(copy)
+    stages = held.shape[0]
+    some = blocks // stages
+    loads = [
+        pltpu.make_async_copy(
+            vec_ref.at[pl.ds(c * some * blk, some * blk), :], held.at[c], sems.at[blocks + 1 + c]
+        )
+        for c in range(stages)
+    ]
+    for load in loads:
+        load.start()
     total = functools.reduce(lambda a, b: a + b, [fill_ref[b] for b in range(blocks)])
     rows = lax.broadcasted_iota(jnp.int32, (META, LANES), 0)
     lane = lax.broadcasted_iota(jnp.int32, (1, LANES), 1)
@@ -51,6 +53,18 @@
         meta, send_ref.at[:, pl.ds(chunks * blk, META), :], sems.at[blocks]
     )
     last.start()
+    copies = []
+    for c in range(stages):
+        loads[c].wait()
+        for b in range(c * some, (c + 1) * some):
+            at = slice((b - c * some) * blk, (b - c * some + 1) * blk)
+            for j in range(chunks):
+                tiles[b, j * blk : (j + 1) * blk, :] = held[c, at, j * LANES : (j + 1) * LANES]
+            copy = pltpu.make_async_copy(
+                tiles.at[b], send_ref.at[owner_ref[b], pl.ds(0, chunks * blk), :], sems.at[b]
+            )
+            copy.start()
+            copies.append(copy)
     for copy in copies:
         copy.wait()
     last.wait()
@@ -67,23 +81,24 @@
         in_specs=[
             pl.BlockSpec(memory_space=pltpu.SMEM),
             pl.BlockSpec(memory_space=pltpu.SMEM),
-            pl.BlockSpec(memory_space=pltpu.VMEM),
+            pl.BlockSpec(memory_space=pl.ANY),
             pl.BlockSpec(memory_space=pltpu.VMEM),
         ],
         out_specs=pl.BlockSpec(memory_space=pl.ANY),
         scratch_shapes=[
+            pltpu.VMEM((4, rows // 4, width), jnp.bfloat16),
             pltpu.VMEM((blocks, height, LANES), jnp.bfloat16),
             pltpu.VMEM((devices, META, LANES), jnp.bfloat16),
-            pltpu.SemaphoreType.DMA((blocks + 1,)),
+            pltpu.SemaphoreType.DMA((blocks + 5,)),
         ],
-        compiler_params=pltpu.CompilerParams(vmem_limit_bytes=VMEM),
+        compiler_params=pltpu.CompilerParams(vmem_limit_bytes=LARGE_VMEM),
         name="build_send",
     )(block_owner, block_fill, vectors, row_list.reshape(rows // LANES, LANES))
 
 
 def update_kernel(
-    blk, recv_ref, old_ref, cent_ref, resid_ref, place_ref, packed_ref, total_ref,
-    blocks, info, old, dense, hot, turned, column, where_ref, sums, counts, parts, gram, final, sems, out_sems,
+    blk, recv_ref, old_ref, cent_ref, resid_ref, where_ref, packed_ref, total_ref,
+    blocks, info, old, dense, hot, turned, column, place_ref, sums, counts, parts, gram, sems, out_sems,
 ):
     slots, height, _ = recv_ref.shape
     lists, width = old_ref.shape
@@ -177,8 +192,8 @@
     count = jnp.sum(counts[...], axis=1, keepdims=True) + 1.0
     own.wait()
     cent = (sums[...] + old[...]) / count
-    final[...] = cent
-    write = pltpu.make_async_copy(final, cent_ref, sems.at[0])
+    sums[...] = cent
+    write = pltpu.make_async_copy(sums, cent_ref, sems.at[0])
     write.start()
     flipped = cent.T
     head = flipped.astype(jnp.bfloat16)
@@ -267,7 +282,7 @@
         out_specs=(
             pl.BlockSpec(memory_space=pl.ANY),
             pl.BlockSpec(memory_space=pl.ANY),
-            pl.BlockSpec(memory_space=pltpu.SMEM),
+            pl.BlockSpec(memory_space=pltpu.VMEM),
             pl.BlockSpec(memory_space=pltpu.VMEM),
             pl.BlockSpec(memory_space=pltpu.VMEM),
         ),
@@ -279,12 +294,11 @@
             pltpu.VMEM((groups, lists, GROUP), jnp.bfloat16),
             pltpu.VMEM((groups, width, GROUP), jnp.bfloat16),
             pltpu.VMEM((LANES, LANES), jnp.float32),
-            pltpu.VMEM((8, slots), jnp.int32),
+            pltpu.SMEM((8, slots), jnp.int32),
             pltpu.VMEM((lists, width), jnp.float32),
             pltpu.VMEM((lists, LANES), jnp.float32),
             pltpu.VMEM((width, 2 * lists), jnp.bfloat16),
             pltpu.VMEM((width // (2 * LANES), 2 * LANES, 2 * LANES), jnp.float32),
-            pltpu.VMEM((lists, width), jnp.float32),
             pltpu.SemaphoreType.DMA((10,)),
             pltpu.SemaphoreType.DMA((groups,)),
         ],
@@ -293,38 +307,26 @@
     )(recv, old)
 
 
-def error_kernel(sub, part, pieces, blk, place_ref, resid_ref, book_ref, before_ref, error_ref, *rest):
-    slot_ref = rest[0] if part == pieces - 1 else None
-    held, sems = rest[-2:]
+def error_kernel(sub, part, blk, place_ref, resid_ref, book_ref, *rest):
+    before_ref, error_ref = rest[:2] if part else (None, rest[0])
+    slot_ref, lines = rest[2:4] if part == len(BOUNDS) - 2 else (None, None)
     subspaces = book_ref.shape[0]
     slots = place_ref.shape[1]
     width = subspaces * sub
     used = place_ref[0, slots - 1] + place_ref[1, slots - 1]
     groups = (used + GROUP - 1) // GROUP
-    first, last = part * groups // pieces, (part + 1) * groups // pieces
-    error_ref[...] = before_ref[...]
-
-    def fetch(g):
-        at = lax.rem(g, 2)
-        return pltpu.make_async_copy(resid_ref.at[g], held.at[at], sems.at[at])
-
-    @pl.when(first < last)
-    def _():
-        fetch(first).start()
+    first, last = (
+        (groups * top + rest) // BOUNDS[-1][0] for top, rest in (BOUNDS[part], BOUNDS[part + 1])
+    )
+    error_ref[...] = before_ref[...] if part else jnp.zeros_like(error_ref)
 
     ones = jnp.ones((AUG, GROUP), jnp.bfloat16)
 
     def visit(g, carry):
-        @pl.when(g + 1 < last)
-        def _():
-            fetch(g + 1).start()
-
-        fetch(g).wait()
-        at = lax.rem(g, 2)
         norm = jnp.zeros((8, GROUP), jnp.float32)
         least = jnp.zeros((1, GROUP), jnp.float32)
         for m in range(subspaces):
-            piece = held[at, m * sub : (m + 1) * sub, :]
+            piece = resid_ref[g, m * sub : (m + 1) * sub, :]
             long = piece.astype(jnp.float32)
             square = long * long
             for k in range(sub // 8):
@@ -353,39 +355,40 @@
             )
             window = pltpu.roll(window, lax.rem(LANES - shift, LANES), 1)
             window = jnp.where(lane < place_ref[1, s], window, 0.0)
-            slot_ref[s : s + 1, :] = window[:, 0:blk]
-
-
-def row_errors(place, resid, book, before, sub, blk, part, pieces):
+            lines[s : s + 1, :] = window
+        slot_ref[...] = lines[...].T[0:blk]
+
+
+def row_errors(place, resid, book, before, sub, blk, part):
     groups, width, _ = resid.shape
     subspaces, codes, depth = book.shape
     slots = place.shape[1]
-    lines = slots * blk // LANES + 8
-    out = [jax.ShapeDtypeStruct((lines, LANES), jnp.float32)]
-    if part == pieces - 1:
-        out.append(jax.ShapeDtypeStruct((slots, blk), jnp.float32))
+    vmem = pl.BlockSpec(memory_space=pltpu.VMEM)
+    out = [jax.ShapeDtypeStruct((slots * blk // LANES + 8, LANES), jnp.float32)]
+    scratch = []
+    if part == len(BOUNDS) - 2:
+        out.append(jax.ShapeDtypeStruct((blk, slots), jnp.float32))
+        scratch.append(pltpu.VMEM((slots, LANES), jnp.float32))
+    operands = [place, resid, book] + ([before] if part else [])
     return pl.pallas_call(
-        functools.partial(error_kernel, sub, part, pieces, blk),
+        functools.partial(error_kernel, sub, part, blk),
         out_shape=tuple(out),
         in_specs=[
             pl.BlockSpec(memory_space=pltpu.SMEM),
-            pl.BlockSpec(memory_space=pl.ANY),
-            pl.BlockSpec(memory_space=pltpu.VMEM),
-            pl.BlockSpec(memory_space=pltpu.VMEM),
-        ],
-        out_specs=tuple(pl.BlockSpec(memory_space=pltpu.VMEM) for _ in out),
-        scratch_shapes=[
-            pltpu.VMEM((2, width, GROUP), jnp.bfloat16),
-            pltpu.SemaphoreType.DMA((2,)),
-        ],
-        compiler_params=pltpu.CompilerParams(vmem_limit_bytes=VMEM // 2),
+            vmem,
+            vmem,
+            vmem,
+        ][: len(operands)],
+        out_specs=tuple(vmem for _ in out),
+        scratch_shapes=scratch,
+        compiler_params=pltpu.CompilerParams(vmem_limit_bytes=SMALL_VMEM),
         cost_estimate=pl.CostEstimate(
             flops=2 * 256 * codes * subspaces * GROUP * 3,
             bytes_accessed=width * GROUP * 2 * 3,
             transcendentals=0,
         ),
         name="row_errors",
-    )(place, resid, book, before)
+    )(*operands)
 
 
 def unpack_kernel(one_ref, two_ref, three_ref, four_ref, total_ref, out_ref):
@@ -412,6 +415,7 @@
     return pl.pallas_call(
         unpack_kernel,
         out_shape=jax.ShapeDtypeStruct((subspaces, sub, sub), jnp.float32),
+        compiler_params=pltpu.CompilerParams(vmem_limit_bytes=SMALL_VMEM),
         name="unpack_moments",
     )(*terms, total)
 
@@ -438,11 +442,9 @@
     send = build_send(vectors, row_list, block_owner, block_fill, devices)
     recv = lax.all_to_all(send, "dev", split_axis=0, concat_axis=0, tiled=True)
     centroids, resid, place, packed, total = update_lists(recv, old_centroids, blk, sub)
-    pieces = 4
-    errors = jnp.zeros((devices * blk // LANES + 8, LANES), jnp.float32)
-    slot_error = None
-    for part in range(pieces):
-        out = row_errors(place, resid, book, errors, sub, blk, part, pieces)
+    errors, slot_error = None, None
+    for part in range(len(BOUNDS) - 1):
+        out = row_errors(place, resid, book, errors, sub, blk, part)
         errors, slot_error = out[0], out[-1]
 
     def partner(step):
@@ -457,7 +459,7 @@
             break
         packed = (terms[0] + terms[1]) + (terms[2] + terms[3])
     moments = unpack_moments(terms, total, codebook.shape[0], sub)
-    return centroids, slot_error, moments
+    return centroids, slot_error.T, moments
 
 
 def solution(mesh):

time: 149 us -> 139 us (0.933)
  local copies, waits for them, and re-layouts: 7.77 us -> 3.29 us
  waiting for transfers between devices: 82.8 us -> 79.8 us
  Pallas kernels: 21.9 us -> 19.7 us
  other arithmetic: 3.41 us -> 1.51 us
    unnamed x17 -> x6, local copies, waits for them, and re-layouts: 4.94 us -> 1.05 us
    all_to_all x1, waiting for transfers between devices: 76.3 us -> 73.7 us  [body(): recv = lax.all_to_all(send, 'dev', split_axis=0, concat_axis=0, tiled=True)]
    mul x1, other arithmetic: 2.24 us -> 0.36 us  [extended_book(): -2.0 * values.transpose(0, 2, 1)]
  transfers between devices with their start and end apart: 11 -> 11, of which waited for: 5 -> 7; matrix products, arithmetic and copies ran while one was open for 5% -> 3% of each run, Pallas kernels for 5% -> 5%
where the time goes in v3:
time: 139 us; the launch traced here: 138 us
  waiting for transfers between devices  79.8 us (57%)
  starting transfers between devices  32.5 us (23%)
  Pallas kernels  19.7 us (14%)
  local copies, waits for them, and re-layouts  3.29 us (2%)
  other arithmetic  1.51 us (1%)
    all_to_all x1, waiting for transfers between devices, body(): recv = lax.all_to_all(send, 'dev', split_axis=0, concat_axis=0, tiled=True)  73.7 us
    ppermute x10, starting transfers between devices, partner(): return lax.ppermute(packed, 'dev', [(i, i ^ step) for i in range(devices)])  20.9 us
    all_to_all x1, starting transfers between devices, body(): recv = lax.all_to_all(send, 'dev', split_axis=0, concat_axis=0, tiled=True)  11.6 us
    pallas_call x1, Pallas kernels, update_lists(): pl.pallas_call(functools.partial(update_kernel, blk), out_shape=(jax.Shap...  8.57 us
    pallas_call x4, Pallas kernels, row_errors(): pl.pallas_call(functools.partial(error_kernel, sub, part, blk), out_shape...  6.87 us
    ppermute x10, waiting for transfers between devices, partner(): return lax.ppermute(packed, 'dev', [(i, i ^ step) for i in range(devices)])  6.11 us
    pallas_call x1, Pallas kernels, build_send(): pl.pallas_call(functools.partial(send_kernel, blk), out_shape=jax.ShapeDt...  3.36 us
  transfers between devices with their start and end apart: 11, of which 7 were waited for; matrix products, arithmetic and copies ran while one was open for 3% of the time, Pallas kernels for 5%

profile of v3, /device:TPU:0, one launch (start us, length us, event | category | flops | bytes accessed | tf_op | source)
XLA Modules:
  0.0 137.7 jit_solution(14873484182674291477)
XLA Ops:
  0.6 3.4 %build_send.1 = bf16[128,200,128]{2,1,0:T(8,128)(2,1)} custom-call(s32[32]{0:T(128)} %owner_ref.1, s32[32]{0:T(128)} %fill_ref.1, bf16[1024,768]{1,0:T(8,128)(2,1)} %vec_ref.1, s32[8,128]{1,0:T(8,128)} %bitcast.11), custom_call_target="tpu_custom_call" | custom-call | tf_op jit(solution)/shard_map/build_send/pallas_call | solution.py:78
  4.0 0.0 copy-start.2
  4.0 11.6 %all-to-all-start = ((bf16[128,200,128]{2,1,0:T(8,128)(2,1)}), bf16[128,200,128]{2,1,0:T(8,128)(2,1)}, u32[]{:S(2)}, u32[]{:S(2)}) async-start(bf16[128,200,128]{2,1,0:T(8,128)(2,1)} %build_send.1), calls=%async_computation | async-start | bytes 13107200 | tf_op jit(solution)/shard_map/all_to_all | solution.py:443
  15.6 0.6 copy.20
  16.3 0.1 multiply_reduce_fusion
  16.4 1.6 %copy.21 = bf16[24,256,3]{2,1,0:T(8,128)(2,1)} copy(bf16[24,256,3]{1,0,2:T(8,128)(2,1)S(1)} %pad_maximum_fusion) | data formatting | bytes 73728 | tf_op jit(solution)/shard_map/stack | solution.py:431
  18.0 0.4 fusion.2
  18.4 1.0 copy-done.1
  19.5 1.0 fusion.1.book_ref
  20.4 73.7 %all-to-all-done.recv_ref = bf16[128,200,128]{2,1,0:T(8,128)(2,1)} async-done(((bf16[128,200,128]{2,1,0:T(8,128)(2,1)}), bf16[128,200,128]{2,1,0:T(8,128)(2,1)}, u32[]{:S(2)}, u32[]{:S(2)}) %all-to-all-start) | async-done | bytes 6553632 | tf_op jit(solution)/shard_map/all_to_all | solution.py:443
  94.2 8.6 %update_lists.1 = (f32[512,768]{1,0:T(8,128)}, bf16[16,768,256]{2,1,0:T(8,128)(2,1)S(1)}, s32[8,128]{1,0:T(8,128)S(1)}, f32[104,128]{1,0:T(8,128)S(1)}, f32[8,128]{1,0:T(8,128)S(1)}) custom-call(bf16[128,200,128]{2,1,0:T(8,128)(2,1)} %all-to-all-done.recv_ref, f32[512,768]{1,0:T(8,128)S(1)} %copy-done), custom_call_target="tpu_custom_call" | custom-call | tf_op jit(solution)/shard_map/update_lists/pallas_call | solution.py:269
  102.7 0.1 collective-permute-start
  102.8 1.6 %row_errors.4.rest_0_ = f32[40,128]{1,0:T(8,128)S(1)} custom-call(s32[8,128]{1,0:T(8,128)S(1)} %get-tuple-element.10.place_ref, bf16[16,768,256]{2,1,0:T(8,128)(2,1)S(1)} %get-tuple-element.11.resid_ref, bf16[24,256,48]{2,1,0:T(8,128)(2,1)S(1)} %fusion.1.book_ref), custom_call_target="tpu_custom_call" | custom-call | flops 2415919104 | bytes 1179648 | tf_op jit(solution)/shard_map/row_errors/pallas_call | solution.py:373
  104.4 0.0 collective-permute-done
  104.5 0.1 collective-permute-start.2
  104.5 4.9 %collective-permute-start.3 = (f32[104,128]{1,0:T(8,128)S(1)}, f32[104,128]{1,0:T(8,128)S(1)}, u32[]{:S(2)}, u32[]{:S(2)}) collective-permute-start(f32[104,128]{1,0:T(8,128)S(1)} %add.23), channel_id=1, source_target_pairs={{0,6},{1,7},{2,4},{3,5},{4,2},{5,3},{6,0},{7,1},{8,14},{9,15},{10,... | collective-permute-start | bytes 159752 | tf_op jit(solution)/shard_map/ppermute | solution.py:451
  109.4 0.0 collective-permute-start.1
  109.4 0.6 row_errors.5.rest_0_
  110.1 0.2 collective-permute-done.2
  110.3 1.4 %collective-permute-done.3 = f32[104,128]{1,0:T(8,128)S(1)} collective-permute-done((f32[104,128]{1,0:T(8,128)S(1)}, f32[104,128]{1,0:T(8,128)S(1)}, u32[]{:S(2)}, u32[]{:S(2)}) %collective-permute-start.3) | collective-permute-done | bytes 53280 | tf_op jit(solution)/shard_map/ppermute | solution.py:451
  111.7 1.9 %collective-permute-done.1 = f32[104,128]{1,0:T(8,128)S(1)} collective-permute-done((f32[104,128]{1,0:T(8,128)S(1)}, f32[104,128]{1,0:T(8,128)S(1)}, u32[]{:S(2)}, u32[]{:S(2)}) %collective-permute-start.1) | collective-permute-done | bytes 53280 | tf_op jit(solution)/shard_map/ppermute | solution.py:451
  113.6 1.2 collective-permute-start.5
  114.8 6.9 %collective-permute-start.6 = (f32[104,128]{1,0:T(8,128)S(1)}, f32[104,128]{1,0:T(8,128)S(1)}, u32[]{:S(2)}, u32[]{:S(2)}) collective-permute-start(f32[104,128]{1,0:T(8,128)S(1)} %add_add_fusion.1), channel_id=1, source_target_pairs={{0,24},{1,25},{2,26},{3,27},{4,28},{5,29},{6,30},{7,31},{8,16},{9,... | collective-permute-start | bytes 159752 | tf_op jit(solution)/shard_map/ppermute | solution.py:451
  121.7 0.0 collective-permute-start.4
  121.7 1.6 %row_errors.6.rest_0_ = f32[40,128]{1,0:T(8,128)S(1)} custom-call(s32[8,128]{1,0:T(8,128)S(1)} %get-tuple-element.10.place_ref, bf16[16,768,256]{2,1,0:T(8,128)(2,1)S(1)} %get-tuple-element.11.resid_ref, bf16[24,256,48]{2,1,0:T(8,128)(2,1)S(1)} %fusion.1.book_ref, f32[40,128]{1,0:T(8,128)S(1)} %row_errors.5.rest_0_), custom_call_target="tpu_custom_call" | custom-call | flops 2415919104 | bytes 1179648 | tf_op jit(solution)/shard_map/row_errors/pallas_call | solution.py:373
  123.3 0.5 collective-permute-done.6
  123.8 2.0 %collective-permute-done.4 = f32[104,128]{1,0:T(8,128)S(1)} collective-permute-done((f32[104,128]{1,0:T(8,128)S(1)}, f32[104,128]{1,0:T(8,128)S(1)}, u32[]{:S(2)}, u32[]{:S(2)}) %collective-permute-start.4) | collective-permute-done | bytes 53280 | tf_op jit(solution)/shard_map/ppermute | solution.py:451
  125.9 4.9 %collective-permute-start.7 = (f32[104,128]{1,0:T(8,128)S(1)}, f32[104,128]{1,0:T(8,128)S(1)}, u32[]{:S(2)}, u32[]{:S(2)}) collective-permute-start(f32[104,128]{1,0:T(8,128)S(1)} %add_add_fusion.one_ref), channel_id=1, source_target_pairs={{0,32},{1,33},{2,34},{3,35},{4,36},{5,37},{6,38},{7,39},{8,40},{9,... | collective-permute-start | bytes 159752 | tf_op jit(solution)/shard_map/ppermute | solution.py:451
  130.8 2.8 %collective-permute-start.9 = (f32[104,128]{1,0:T(8,128)S(1)}, f32[104,128]{1,0:T(8,128)S(1)}, u32[]{:S(2)}, u32[]{:S(2)}) collective-permute-start(f32[104,128]{1,0:T(8,128)S(1)} %add_add_fusion.one_ref), channel_id=1, source_target_pairs={{0,96},{1,97},{2,98},{3,99},{4,100},{5,101},{6,102},{7,103},{8,104... | collective-permute-start | bytes 159752 | tf_op jit(solution)/shard_map/ppermute | solution.py:451
  133.6 3.1 %row_errors.7 = (f32[40,128]{1,0:T(8,128)}, f32[32,128]{1,0:T(8,128)}) custom-call(s32[8,128]{1,0:T(8,128)S(1)} %get-tuple-element.10.place_ref, bf16[16,768,256]{2,1,0:T(8,128)(2,1)S(1)} %get-tuple-element.11.resid_ref, bf16[24,256,48]{2,1,0:T(8,128)(2,1)S(1)} %fusion.1.book_ref, f32[40,128]{1,0:T(8,128)S(1)} %row_errors.6.rest_0_), custom_call_target="tpu_custom_call" | custom-call | flops 2415919104 | bytes 1179648 | tf_op jit(solution)/shard_map/row_errors/pallas_call | solution.py:373
  136.6 0.1 collective-permute-done.9.four_ref
  136.7 0.9 unpack_moments.1
  (13 shorter events, 0.1 us)
Async XLA Ops:
  4.0 11.6 %copy-start.2 = (bf16[24,32,256]{2,1,0:T(8,128)(2,1)S(1)}, bf16[24,32,256]{2,1,0:T(8,128)(2,1)}, u32[]{:S(2)}) copy-start(bf16[24,32,256]{2,1,0:T(8,128)(2,1)} %param.11) | copy-start | bytes 1179652
  4.0 90.1 %all-to-all-start = ((bf16[128,200,128]{2,1,0:T(8,128)(2,1)}), bf16[128,200,128]{2,1,0:T(8,128)(2,1)}, u32[]{:S(2)}, u32[]{:S(2)}) async-start(bf16[128,200,128]{2,1,0:T(8,128)(2,1)} %build_send.1), calls=%async_computation | async-start | bytes 13107200 | tf_op jit(solution)/shard_map/all_to_all | solution.py:443
  18.0 1.4 %copy-start.1 = (bf16[24,256,3]{2,1,0:T(8,128)(2,1)S(1)}, bf16[24,256,3]{2,1,0:T(8,128)(2,1)}, u32[]{:S(2)}) copy-start(bf16[24,256,3]{2,1,0:T(8,128)(2,1)} %copy.21) | copy-start | bytes 110596
  19.4 74.7 %copy-start = (f32[512,768]{1,0:T(8,128)S(1)}, f32[512,768]{1,0:T(8,128)}, u32[]{:S(2)}) copy-start(f32[512,768]{1,0:T(8,128)} %old_ref.1) | copy-start | bytes 4718596
  102.7 1.7 %collective-permute-start = (f32[104,128]{1,0:T(8,128)S(1)}, f32[104,128]{1,0:T(8,128)S(1)}, u32[]{:S(2)}, u32[]{:S(2)}) collective-permute-start(f32[104,128]{1,0:T(8,128)S(1)} %get-tuple-element.13), channel_id=1, source_target_pairs={{0,1},{1,0},{2,3},{3,2},{4,5},{5,4},{6,7},{7,6},{8,9},{9,8},{10,11... | collective-permute-start | bytes 159752 | tf_op jit(solution)/shard_map/ppermute | solution.py:451
  104.5 5.8 %collective-permute-start.2 = (f32[104,128]{1,0:T(8,128)S(1)}, f32[104,128]{1,0:T(8,128)S(1)}, u32[]{:S(2)}, u32[]{:S(2)}) collective-permute-start(f32[104,128]{1,0:T(8,128)S(1)} %add.23), channel_id=1, source_target_pairs={{0,4},{1,5},{2,6},{3,7},{4,0},{5,1},{6,2},{7,3},{8,12},{9,13},{10,... | collective-permute-start | bytes 159752 | tf_op jit(solution)/shard_map/ppermute | solution.py:451
  104.5 7.1 %collective-permute-start.3 = (f32[104,128]{1,0:T(8,128)S(1)}, f32[104,128]{1,0:T(8,128)S(1)}, u32[]{:S(2)}, u32[]{:S(2)}) collective-permute-start(f32[104,128]{1,0:T(8,128)S(1)} %add.23), channel_id=1, source_target_pairs={{0,6},{1,7},{2,4},{3,5},{4,2},{5,3},{6,0},{7,1},{8,14},{9,15},{10,... | collective-permute-start | bytes 159752 | tf_op jit(solution)/shard_map/ppermute | solution.py:451
  109.4 4.1 %collective-permute-start.1 = (f32[104,128]{1,0:T(8,128)S(1)}, f32[104,128]{1,0:T(8,128)S(1)}, u32[]{:S(2)}, u32[]{:S(2)}) collective-permute-start(f32[104,128]{1,0:T(8,128)S(1)} %add.23), channel_id=1, source_target_pairs={{0,2},{1,3},{2,0},{3,1},{4,6},{5,7},{6,4},{7,5},{8,10},{9,11},{10,... | collective-permute-start | bytes 159752 | tf_op jit(solution)/shard_map/ppermute | solution.py:451
  113.6 9.7 %collective-permute-start.5 = (f32[104,128]{1,0:T(8,128)S(1)}, f32[104,128]{1,0:T(8,128)S(1)}, u32[]{:S(2)}, u32[]{:S(2)}) collective-permute-start(f32[104,128]{1,0:T(8,128)S(1)} %add_add_fusion.1), channel_id=1, source_target_pairs={{0,16},{1,17},{2,18},{3,19},{4,20},{5,21},{6,22},{7,23},{8,24},{9,... | collective-permute-start | bytes 159752 | tf_op jit(solution)/shard_map/ppermute | solution.py:451
  114.8 9.0 %collective-permute-start.6 = (f32[104,128]{1,0:T(8,128)S(1)}, f32[104,128]{1,0:T(8,128)S(1)}, u32[]{:S(2)}, u32[]{:S(2)}) collective-permute-start(f32[104,128]{1,0:T(8,128)S(1)} %add_add_fusion.1), channel_id=1, source_target_pairs={{0,24},{1,25},{2,26},{3,27},{4,28},{5,29},{6,30},{7,31},{8,16},{9,... | collective-permute-start | bytes 159752 | tf_op jit(solution)/shard_map/ppermute | solution.py:451
  121.7 4.1 %collective-permute-start.4 = (f32[104,128]{1,0:T(8,128)S(1)}, f32[104,128]{1,0:T(8,128)S(1)}, u32[]{:S(2)}, u32[]{:S(2)}) collective-permute-start(f32[104,128]{1,0:T(8,128)S(1)} %add_add_fusion.1), channel_id=1, source_target_pairs={{0,8},{1,9},{2,10},{3,11},{4,12},{5,13},{6,14},{7,15},{8,0},{9,1},... | collective-permute-start | bytes 159752 | tf_op jit(solution)/shard_map/ppermute | solution.py:451
  125.9 10.8 %collective-permute-start.7 = (f32[104,128]{1,0:T(8,128)S(1)}, f32[104,128]{1,0:T(8,128)S(1)}, u32[]{:S(2)}, u32[]{:S(2)}) collective-permute-start(f32[104,128]{1,0:T(8,128)S(1)} %add_add_fusion.one_ref), channel_id=1, source_target_pairs={{0,32},{1,33},{2,34},{3,35},{4,36},{5,37},{6,38},{7,39},{8,40},{9,... | collective-permute-start | bytes 159752 | tf_op jit(solution)/shard_map/ppermute | solution.py:451
  130.8 5.8 %collective-permute-start.8 = (f32[104,128]{1,0:T(8,128)S(1)}, f32[104,128]{1,0:T(8,128)S(1)}, u32[]{:S(2)}, u32[]{:S(2)}) collective-permute-start(f32[104,128]{1,0:T(8,128)S(1)} %add_add_fusion.one_ref), channel_id=1, source_target_pairs={{0,64},{1,65},{2,66},{3,67},{4,68},{5,69},{6,70},{7,71},{8,72},{9,... | collective-permute-start | bytes 159752 | tf_op jit(solution)/shard_map/ppermute | solution.py:451
  130.8 5.9 %collective-permute-start.9 = (f32[104,128]{1,0:T(8,128)S(1)}, f32[104,128]{1,0:T(8,128)S(1)}, u32[]{:S(2)}, u32[]{:S(2)}) collective-permute-start(f32[104,128]{1,0:T(8,128)S(1)} %add_add_fusion.one_ref), channel_id=1, source_target_pairs={{0,96},{1,97},{2,98},{3,99},{4,100},{5,101},{6,102},{7,103},{8,104... | collective-permute-start | bytes 159752 | tf_op jit(solution)/shard_map/ppermute | solution.py:451

commit v4 on v3

--- a/solution.py
+++ b/solution.py
@@ -11,7 +11,7 @@
 META = 8
 AUG = 16
 GROUP = 256
-VMEM = 42 * 1024 * 1024
+VMEM = 37 * 1024 * 1024
 LARGE_VMEM = 56 * 1024 * 1024
 SMALL_VMEM = 10 * 1024 * 1024
 BOUNDS = ((0, 0), (1, 8), (4, 4), (7, 4), (9, 0))
@@ -97,8 +97,8 @@
 
 
 def update_kernel(
-    blk, recv_ref, old_ref, cent_ref, resid_ref, where_ref, packed_ref, total_ref,
-    blocks, info, old, dense, hot, turned, column, place_ref, sums, counts, parts, gram, sems, out_sems,
+    blk, recv_ref, old_ref, cent_ref, turned, where_ref, packed_ref, total_ref,
+    blocks, info, old, dense, hot, values, column, place_ref, sums, counts, parts, gram, sems,
 ):
     slots, height, _ = recv_ref.shape
     lists, width = old_ref.shape
@@ -164,27 +164,29 @@
     used = place_ref[0, slots - 1] + place_ref[1, slots - 1]
     for j in range(chunks + 1):
         dense[j, pl.ds(used, GROUP + blk), :] = jnp.zeros((GROUP + blk, LANES), jnp.float32)
-    groups = (used + GROUP - 1) // GROUP
-
-    def gather(g, carry):
+    groups = jnp.maximum((used + GROUP - 1) // GROUP, 1)
+
+    def prepare(g):
         at = pl.ds(pl.multiple_of(g * GROUP, GROUP), GROUP)
         code = jnp.sum(dense[chunks, at, :].T, axis=0, keepdims=True)
         ids = lax.broadcasted_iota(jnp.int32, (lists, GROUP), 0).astype(jnp.float32) + 1.0
-        match = jnp.where(ids == code, 1.0, 0.0)
-        chosen = match.astype(jnp.bfloat16)
-        hot[g] = chosen
-        part = match[:, 0:LANES]
-        for k in range(1, GROUP // LANES):
-            part = part + match[:, k * LANES : (k + 1) * LANES]
-        counts[...] += part
-        pieces = []
+        hot[g] = jnp.where(ids == code, 1.0, 0.0).astype(jnp.bfloat16)
         for j in range(chunks):
             piece = dense[j, at, :].astype(jnp.bfloat16)
             turned[g, j * LANES : (j + 1) * LANES, :] = piece.T
-            pieces.append(piece)
-        sums[...] += jnp.dot(
-            chosen, jnp.concatenate(pieces, axis=1), preferred_element_type=jnp.float32
-        )
+            values[g & 1, :, j * LANES : (j + 1) * LANES] = piece
+
+    prepare(0)
+
+    def gather(g, carry):
+        chosen = hot[g]
+        added = jnp.dot(chosen, values[g & 1], preferred_element_type=jnp.float32)
+        part = chosen[:, 0:LANES].astype(jnp.float32)
+        for k in range(1, GROUP // LANES):
+            part = part + chosen[:, k * LANES : (k + 1) * LANES].astype(jnp.float32)
+        prepare(g + 1)
+        sums[...] += added
+        counts[...] += part
         return carry
 
     lax.fori_loop(0, groups, gather, 0)
@@ -203,10 +205,7 @@
     wide = 2 * LANES
     lane = lax.broadcasted_iota(jnp.int32, (1, GROUP), 1)
 
-    def leave(g):
-        return pltpu.make_async_copy(turned.at[g], resid_ref.at[g], out_sems.at[g])
-
-    def encode(g, carry):
+    def subtract(g):
         chosen = hot[g]
         weight = jnp.where(lane < used - g * GROUP, 1.0, 0.0)
         both = jnp.concatenate([chosen, chosen], axis=0)
@@ -217,16 +216,27 @@
             resids.append(((turned[g, at].astype(jnp.float32) - picked) * weight).astype(jnp.bfloat16))
         for j in range(width // wide):
             turned[g, j * wide : (j + 1) * wide] = resids[j]
-        squares = [
+
+    def multiply(g):
+        resids = [turned[g, j * wide : (j + 1) * wide] for j in range(width // wide)]
+        return [
             lax.dot_general(r, r, (((1,), (1,)), ((), ())), preferred_element_type=jnp.float32)
             for r in resids
         ]
+
+    subtract(0)
+
+    def encode(g, carry):
+        squares = multiply(g)
+        subtract(g + 1)
         for j in range(width // wide):
             gram[j] += squares[j]
-        leave(g).start()
         return carry
 
-    lax.fori_loop(0, groups, encode, 0)
+    lax.fori_loop(0, groups - 1, encode, 0)
+    squares = multiply(groups - 1)
+    for j in range(width // wide):
+        gram[j] += squares[j]
 
     sub = (packed_ref.shape[0] - 8) // (chunks // 2)
     across = LANES // sub
@@ -252,11 +262,6 @@
     diagonals.append(jnp.zeros((8 - half, LANES), jnp.float32))
     packed_ref[half * sub :, :] = jnp.concatenate(diagonals, axis=0)
 
-    def finish(g, carry):
-        leave(g).wait()
-        return carry
-
-    lax.fori_loop(0, groups, finish, 0)
     write.wait()
 
 
@@ -270,7 +275,7 @@
         functools.partial(update_kernel, blk),
         out_shape=(
             jax.ShapeDtypeStruct((lists, width), jnp.float32),
-            jax.ShapeDtypeStruct((groups, width, GROUP), jnp.bfloat16),
+            jax.ShapeDtypeStruct((groups + 1, width, GROUP), jnp.bfloat16),
             jax.ShapeDtypeStruct((8, slots), jnp.int32),
             jax.ShapeDtypeStruct((chunks // 2 * sub + 8, LANES), jnp.float32),
             jax.ShapeDtypeStruct((8, LANES), jnp.float32),
@@ -281,7 +286,7 @@
         ],
         out_specs=(
             pl.BlockSpec(memory_space=pl.ANY),
-            pl.BlockSpec(memory_space=pl.ANY),
+            pl.BlockSpec(memory_space=pltpu.VMEM),
             pl.BlockSpec(memory_space=pltpu.VMEM),
             pl.BlockSpec(memory_space=pltpu.VMEM),
             pl.BlockSpec(memory_space=pltpu.VMEM),
@@ -291,8 +296,8 @@
             pltpu.VMEM((slots, META, LANES), jnp.bfloat16),
             pltpu.VMEM((lists, width), jnp.float32),
             pltpu.VMEM((chunks + 1, rows + GROUP + blk, LANES), jnp.float32),
-            pltpu.VMEM((groups, lists, GROUP), jnp.bfloat16),
-            pltpu.VMEM((groups, width, GROUP), jnp.bfloat16),
+            pltpu.VMEM((groups + 1, lists, GROUP), jnp.bfloat16),
+            pltpu.VMEM((2, GROUP, width), jnp.bfloat16),
             pltpu.VMEM((LANES, LANES), jnp.float32),
             pltpu.SMEM((8, slots), jnp.int32),
             pltpu.VMEM((lists, width), jnp.float32),
@@ -300,7 +305,6 @@
             pltpu.VMEM((width, 2 * lists), jnp.bfloat16),
             pltpu.VMEM((width // (2 * LANES), 2 * LANES, 2 * LANES), jnp.float32),
             pltpu.SemaphoreType.DMA((10,)),
-            pltpu.SemaphoreType.DMA((groups,)),
         ],
         compiler_params=pltpu.CompilerParams(vmem_limit_bytes=VMEM),
         name="update_lists",
@@ -348,12 +352,12 @@
         lane = lax.broadcasted_iota(jnp.int32, (1, LANES), 1)
         for s in range(slots):
             start = place_ref[0, s]
-            line = start // LANES
-            shift = lax.rem(start, LANES)
+            line = lax.shift_right_logical(start, LANES.bit_length() - 1)
+            shift = start & (LANES - 1)
             window = jnp.where(
                 lane >= shift, error_ref[pl.ds(line, 1), :], error_ref[pl.ds(line + 1, 1), :]
             )
-            window = pltpu.roll(window, lax.rem(LANES - shift, LANES), 1)
+            window = pltpu.roll(window, (LANES - shift) & (LANES - 1), 1)
             window = jnp.where(lane < place_ref[1, s], window, 0.0)
             lines[s : s + 1, :] = window
         slot_ref[...] = lines[...].T[0:blk]
@@ -391,11 +395,13 @@
     )(*operands)
 
 
-def unpack_kernel(one_ref, two_ref, three_ref, four_ref, total_ref, out_ref):
+def unpack_kernel(even_ref, own_ref, one_ref, two_ref, three_ref, total_ref, out_ref):
     sub = out_ref.shape[1]
     across = LANES // sub
     half = out_ref.shape[0] // across // 2
-    packed = (one_ref[...] + two_ref[...]) + (three_ref[...] + four_ref[...])
+    even = even_ref[0] != 0
+    one, three = one_ref[...], three_ref[...]
+    packed = (own_ref[...] + jnp.where(even, three, one)) + (two_ref[...] + jnp.where(even, one, three))
     share = 1.0 / total_ref[0:1, 0:1]
     row = lax.broadcasted_iota(jnp.int32, (sub, sub), 0)
     lane = lax.broadcasted_iota(jnp.int32, (sub, sub), 1)
@@ -411,13 +417,14 @@
             out_ref[(half + q) * across + a] = other * share
 
 
-def unpack_moments(terms, total, subspaces, sub):
+def unpack_moments(terms, even, total, subspaces, sub):
     return pl.pallas_call(
         unpack_kernel,
         out_shape=jax.ShapeDtypeStruct((subspaces, sub, sub), jnp.float32),
+        in_specs=[pl.BlockSpec(memory_space=pltpu.SMEM)] + [pl.BlockSpec(memory_space=pltpu.VMEM)] * 5,
         compiler_params=pltpu.CompilerParams(vmem_limit_bytes=SMALL_VMEM),
         name="unpack_moments",
-    )(*terms, total)
+    )(even, *terms, total)
 
 
 def extended_book(codebook):
@@ -447,18 +454,26 @@
         out = row_errors(place, resid, book, errors, sub, blk, part)
         errors, slot_error = out[0], out[-1]
 
-    def partner(step):
-        return lax.ppermute(packed, "dev", [(i, i ^ step) for i in range(devices)])
-
-    packed = packed + partner(1)
+    me = lax.axis_index("dev")
+
+    def shifted(values, stride, step, size):
+        pairs = []
+        for i in range(devices):
+            digit = i // stride % size
+            pairs.append((i, i + ((digit + step) % size - digit) * stride))
+        return lax.ppermute(values, "dev", pairs)
+
+    packed = packed + shifted(packed, 1, 1, 2)
     stride = 2
     while True:
-        terms = (packed, partner(stride), partner(2 * stride), partner(3 * stride))
+        two, one, three = (shifted(packed, stride, k, 4) for k in (2, 1, 3))
+        even = me // stride % 2 == 0
+        terms = (packed, jnp.where(even, three, one), two, jnp.where(even, one, three))
         stride *= 4
         if stride >= devices:
             break
         packed = (terms[0] + terms[1]) + (terms[2] + terms[3])
-    moments = unpack_moments(terms, total, codebook.shape[0], sub)
+    moments = unpack_moments((packed, one, two, three), even.astype(jnp.int32).reshape(1), total, codebook.shape[0], sub)
     return centroids, slot_error.T, moments
 
 

time: 139 us -> 134 us (0.964)
  waiting for transfers between devices: 79.8 us -> 76 us
  Pallas kernels: 19.7 us -> 16.1 us
  starting transfers between devices: 32.5 us -> 36 us
    ppermute x10, waiting for transfers between devices: 6.11 us -> 2.28 us  [shifted(): return lax.ppermute(values, 'dev', pairs)]
    ppermute x10, starting transfers between devices: 20.9 us -> 24.5 us  [shifted(): return lax.ppermute(values, 'dev', pairs)]
    pallas_call x1, Pallas kernels: 8.57 us -> 6.4 us  [update_lists(): pl.pallas_call(functools.partial(update_kernel, blk), out_shape=(jax.Shap...]
    pallas_call x4, Pallas kernels: 6.87 us -> 5.37 us  [row_errors(): pl.pallas_call(functools.partial(error_kernel, sub, part, blk), out_shape...]
  transfers between devices with their start and end apart: 11 -> 11, of which waited for: 7 -> 4; matrix products, arithmetic and copies ran while one was open for 3% -> 3% of each run, Pallas kernels for 5% -> 4%
where the time goes in v4:
time: 134 us
  waiting for transfers between devices  76 us (57%)
  starting transfers between devices  36 us (27%)
  Pallas kernels  16.1 us (12%)
  local copies, waits for them, and re-layouts  3.29 us (2%)
  other arithmetic  1.5 us (1%)
    all_to_all x1, waiting for transfers between devices, body(): recv = lax.all_to_all(send, 'dev', split_axis=0, concat_axis=0, tiled=True)  73.7 us
    ppermute x10, starting transfers between devices, shifted(): return lax.ppermute(values, 'dev', pairs)  24.5 us
    all_to_all x1, starting transfers between devices, body(): recv = lax.all_to_all(send, 'dev', split_axis=0, concat_axis=0, tiled=True)  11.6 us
    pallas_call x1, Pallas kernels, update_lists(): pl.pallas_call(functools.partial(update_kernel, blk), out_shape=(jax.Shap...  6.4 us
    pallas_call x4, Pallas kernels, row_errors(): pl.pallas_call(functools.partial(error_kernel, sub, part, blk), out_shape...  5.37 us
    pallas_call x1, Pallas kernels, build_send(): pl.pallas_call(functools.partial(send_kernel, blk), out_shape=jax.ShapeDt...  3.37 us
  transfers between devices with their start and end apart: 11, of which 4 were waited for; matrix products, arithmetic and copies ran while one was open for 3% of the time, Pallas kernels for 4%

profile of v4, /device:TPU:0, one launch (start us, length us, event | category | flops | bytes accessed | tf_op | source)
XLA Modules:
  0.0 133.7 jit_solution(10525663528317397430)
XLA Ops:
  0.6 3.4 %build_send.1 = bf16[128,200,128]{2,1,0:T(8,128)(2,1)} custom-call(s32[32]{0:T(128)} %owner_ref.1, s32[32]{0:T(128)} %fill_ref.1, bf16[1024,768]{1,0:T(8,128)(2,1)} %vec_ref.1, s32[8,128]{1,0:T(8,128)} %bitcast.12), custom_call_target="tpu_custom_call" | custom-call | tf_op jit(solution)/shard_map/build_send/pallas_call | solution.py:78
  4.0 0.0 copy-start.2
  4.0 11.6 %all-to-all-start = ((bf16[128,200,128]{2,1,0:T(8,128)(2,1)}), bf16[128,200,128]{2,1,0:T(8,128)(2,1)}, u32[]{:S(2)}, u32[]{:S(2)}) async-start(bf16[128,200,128]{2,1,0:T(8,128)(2,1)} %build_send.1), calls=%async_computation | async-start | bytes 13107200 | tf_op jit(solution)/shard_map/all_to_all | solution.py:450
  15.7 0.6 copy.20
  16.3 0.1 multiply_reduce_fusion
  16.5 1.6 %copy.21 = bf16[24,256,3]{2,1,0:T(8,128)(2,1)} copy(bf16[24,256,3]{1,0,2:T(8,128)(2,1)S(1)} %pad_maximum_fusion) | data formatting | bytes 73728 | tf_op jit(solution)/shard_map/stack | solution.py:438
  18.1 0.4 fusion.2
  18.5 1.0 copy-done.1
  19.5 1.0 fusion.1.book_ref
  20.5 73.7 %all-to-all-done.recv_ref = bf16[128,200,128]{2,1,0:T(8,128)(2,1)} async-done(((bf16[128,200,128]{2,1,0:T(8,128)(2,1)}), bf16[128,200,128]{2,1,0:T(8,128)(2,1)}, u32[]{:S(2)}, u32[]{:S(2)}) %all-to-all-start) | async-done | bytes 6553632 | tf_op jit(solution)/shard_map/all_to_all | solution.py:450
  94.1 6.4 %update_lists.1 = (f32[512,768]{1,0:T(8,128)}, bf16[17,768,256]{2,1,0:T(8,128)(2,1)S(1)}, s32[8,128]{1,0:T(8,128)S(1)}, f32[104,128]{1,0:T(8,128)S(1)}, f32[8,128]{1,0:T(8,128)S(1)}) custom-call(bf16[128,200,128]{2,1,0:T(8,128)(2,1)} %all-to-all-done.recv_ref, f32[512,768]{1,0:T(8,128)S(1)} %copy-done), custom_call_target="tpu_custom_call" | custom-call | tf_op jit(solution)/shard_map/update_lists/pallas_call | solution.py:274
  100.5 0.6 collective-permute-start
  101.2 1.6 %row_errors.4.rest_0_ = f32[40,128]{1,0:T(8,128)S(1)} custom-call(s32[8,128]{1,0:T(8,128)S(1)} %get-tuple-element.10.place_ref, bf16[17,768,256]{2,1,0:T(8,128)(2,1)S(1)} %get-tuple-element.11.resid_ref, bf16[24,256,48]{2,1,0:T(8,128)(2,1)S(1)} %fusion.1.book_ref), custom_call_target="tpu_custom_call" | custom-call | flops 2415919104 | bytes 1179648 | tf_op jit(solution)/shard_map/row_errors/pallas_call | solution.py:377
  102.7 0.0 collective-permute-done
  102.8 0.8 collective-permute-start.3
  103.6 2.6 %collective-permute-start.2 = (f32[104,128]{1,0:T(8,128)S(1)}, f32[104,128]{1,0:T(8,128)S(1)}, u32[]{:S(2)}, u32[]{:S(2)}) collective-permute-start(f32[104,128]{1,0:T(8,128)S(1)} %add.37), channel_id=1, source_target_pairs={{0,2},{1,3},{2,4},{3,5},{4,6},{5,7},{6,0},{7,1},{8,10},{9,11},{10,... | collective-permute-start | bytes 159752 | tf_op jit(solution)/shard_map/ppermute | solution.py:464
  106.2 2.6 %collective-permute-start.1 = (f32[104,128]{1,0:T(8,128)S(1)}, f32[104,128]{1,0:T(8,128)S(1)}, u32[]{:S(2)}, u32[]{:S(2)}) collective-permute-start(f32[104,128]{1,0:T(8,128)S(1)} %add.37), channel_id=1, source_target_pairs={{0,6},{1,7},{2,0},{3,1},{4,2},{5,3},{6,4},{7,5},{8,14},{9,15},{10,... | collective-permute-start | bytes 159752 | tf_op jit(solution)/shard_map/ppermute | solution.py:464
  108.8 0.6 row_errors.5.rest_0_
  109.4 0.0 collective-permute-done.3
  109.4 1.6 %collective-permute-done.2 = f32[104,128]{1,0:T(8,128)S(1)} collective-permute-done((f32[104,128]{1,0:T(8,128)S(1)}, f32[104,128]{1,0:T(8,128)S(1)}, u32[]{:S(2)}, u32[]{:S(2)}) %collective-permute-start.2) | collective-permute-done | bytes 53280 | tf_op jit(solution)/shard_map/ppermute | solution.py:464
  111.0 0.0 collective-permute-done.1
  111.0 1.1 collective-permute-start.6
  112.1 7.3 %collective-permute-start.5 = (f32[104,128]{1,0:T(8,128)S(1)}, f32[104,128]{1,0:T(8,128)S(1)}, u32[]{:S(2)}, u32[]{:S(2)}) collective-permute-start(f32[104,128]{1,0:T(8,128)S(1)} %add_add_fusion.1), channel_id=1, source_target_pairs={{0,8},{1,9},{2,10},{3,11},{4,12},{5,13},{6,14},{7,15},{8,16},{9,17... | collective-permute-start | bytes 159752 | tf_op jit(solution)/shard_map/ppermute | solution.py:464
  119.4 2.6 %collective-permute-start.4 = (f32[104,128]{1,0:T(8,128)S(1)}, f32[104,128]{1,0:T(8,128)S(1)}, u32[]{:S(2)}, u32[]{:S(2)}) collective-permute-start(f32[104,128]{1,0:T(8,128)S(1)} %add_add_fusion.1), channel_id=1, source_target_pairs={{0,24},{1,25},{2,26},{3,27},{4,28},{5,29},{6,30},{7,31},{8,0},{9,1... | collective-permute-start | bytes 159752 | tf_op jit(solution)/shard_map/ppermute | solution.py:464
  122.0 1.6 %row_errors.6.rest_0_ = f32[40,128]{1,0:T(8,128)S(1)} custom-call(s32[8,128]{1,0:T(8,128)S(1)} %get-tuple-element.10.place_ref, bf16[17,768,256]{2,1,0:T(8,128)(2,1)S(1)} %get-tuple-element.11.resid_ref, bf16[24,256,48]{2,1,0:T(8,128)(2,1)S(1)} %fusion.1.book_ref, f32[40,128]{1,0:T(8,128)S(1)} %row_errors.5.rest_0_), custom_call_target="tpu_custom_call" | custom-call | flops 2415919104 | bytes 1179648 | tf_op jit(solution)/shard_map/row_errors/pallas_call | solution.py:377
  123.6 0.5 collective-permute-done.5
  124.1 0.1 collective-permute-start.7
  124.2 4.2 %collective-permute-start.8 = (f32[104,128]{1,0:T(8,128)S(1)}, f32[104,128]{1,0:T(8,128)S(1)}, u32[]{:S(2)}, u32[]{:S(2)}) collective-permute-start(f32[104,128]{1,0:T(8,128)S(1)} %add_add_fusion.own_ref), channel_id=1, source_target_pairs={{0,64},{1,65},{2,66},{3,67},{4,68},{5,69},{6,70},{7,71},{8,72},{9,... | collective-permute-start | bytes 159752 | tf_op jit(solution)/shard_map/ppermute | solution.py:464
  128.5 2.5 %collective-permute-start.9 = (f32[104,128]{1,0:T(8,128)S(1)}, f32[104,128]{1,0:T(8,128)S(1)}, u32[]{:S(2)}, u32[]{:S(2)}) collective-permute-start(f32[104,128]{1,0:T(8,128)S(1)} %add_add_fusion.own_ref), channel_id=1, source_target_pairs={{0,96},{1,97},{2,98},{3,99},{4,100},{5,101},{6,102},{7,103},{8,104... | collective-permute-start | bytes 159752 | tf_op jit(solution)/shard_map/ppermute | solution.py:464
  131.0 1.6 %row_errors.7 = (f32[40,128]{1,0:T(8,128)}, f32[32,128]{1,0:T(8,128)}) custom-call(s32[8,128]{1,0:T(8,128)S(1)} %get-tuple-element.10.place_ref, bf16[17,768,256]{2,1,0:T(8,128)(2,1)S(1)} %get-tuple-element.11.resid_ref, bf16[24,256,48]{2,1,0:T(8,128)(2,1)S(1)} %fusion.1.book_ref, f32[40,128]{1,0:T(8,128)S(1)} %row_errors.6.rest_0_), custom_call_target="tpu_custom_call" | custom-call | flops 2415919104 | bytes 1179648 | tf_op jit(solution)/shard_map/row_errors/pallas_call | solution.py:377
  132.6 0.2 collective-permute-done.9.three_ref
  132.8 0.9 unpack_moments.1
  (13 shorter events, 0.1 us)
Async XLA Ops:
  4.0 11.7 %copy-start.2 = (bf16[24,32,256]{2,1,0:T(8,128)(2,1)S(1)}, bf16[24,32,256]{2,1,0:T(8,128)(2,1)}, u32[]{:S(2)}) copy-start(bf16[24,32,256]{2,1,0:T(8,128)(2,1)} %param.11) | copy-start | bytes 1179652
  4.0 90.1 %all-to-all-start = ((bf16[128,200,128]{2,1,0:T(8,128)(2,1)}), bf16[128,200,128]{2,1,0:T(8,128)(2,1)}, u32[]{:S(2)}, u32[]{:S(2)}) async-start(bf16[128,200,128]{2,1,0:T(8,128)(2,1)} %build_send.1), calls=%async_computation | async-start | bytes 13107200 | tf_op jit(solution)/shard_map/all_to_all | solution.py:450
  18.1 1.4 %copy-start.1 = (bf16[24,256,3]{2,1,0:T(8,128)(2,1)S(1)}, bf16[24,256,3]{2,1,0:T(8,128)(2,1)}, u32[]{:S(2)}) copy-start(bf16[24,256,3]{2,1,0:T(8,128)(2,1)} %copy.21) | copy-start | bytes 110596
  19.5 74.6 %copy-start = (f32[512,768]{1,0:T(8,128)S(1)}, f32[512,768]{1,0:T(8,128)}, u32[]{:S(2)}) copy-start(f32[512,768]{1,0:T(8,128)} %old_ref.1) | copy-start | bytes 4718596
  100.5 2.2 %collective-permute-start = (f32[104,128]{1,0:T(8,128)S(1)}, f32[104,128]{1,0:T(8,128)S(1)}, u32[]{:S(2)}, u32[]{:S(2)}) collective-permute-start(f32[104,128]{1,0:T(8,128)S(1)} %get-tuple-element.13), channel_id=1, source_target_pairs={{0,1},{1,0},{2,3},{3,2},{4,5},{5,4},{6,7},{7,6},{8,9},{9,8},{10,11... | collective-permute-start | bytes 159752 | tf_op jit(solution)/shard_map/ppermute | solution.py:464
  102.8 6.6 %collective-permute-start.3 = (f32[104,128]{1,0:T(8,128)S(1)}, f32[104,128]{1,0:T(8,128)S(1)}, u32[]{:S(2)}, u32[]{:S(2)}) collective-permute-start(f32[104,128]{1,0:T(8,128)S(1)} %add.37), channel_id=1, source_target_pairs={{0,4},{1,5},{2,6},{3,7},{4,0},{5,1},{6,2},{7,3},{8,12},{9,13},{10,... | collective-permute-start | bytes 159752 | tf_op jit(solution)/shard_map/ppermute | solution.py:464
  103.6 7.4 %collective-permute-start.2 = (f32[104,128]{1,0:T(8,128)S(1)}, f32[104,128]{1,0:T(8,128)S(1)}, u32[]{:S(2)}, u32[]{:S(2)}) collective-permute-start(f32[104,128]{1,0:T(8,128)S(1)} %add.37), channel_id=1, source_target_pairs={{0,2},{1,3},{2,4},{3,5},{4,6},{5,7},{6,0},{7,1},{8,10},{9,11},{10,... | collective-permute-start | bytes 159752 | tf_op jit(solution)/shard_map/ppermute | solution.py:464
  106.2 4.8 %collective-permute-start.1 = (f32[104,128]{1,0:T(8,128)S(1)}, f32[104,128]{1,0:T(8,128)S(1)}, u32[]{:S(2)}, u32[]{:S(2)}) collective-permute-start(f32[104,128]{1,0:T(8,128)S(1)} %add.37), channel_id=1, source_target_pairs={{0,6},{1,7},{2,0},{3,1},{4,2},{5,3},{6,4},{7,5},{8,14},{9,15},{10,... | collective-permute-start | bytes 159752 | tf_op jit(solution)/shard_map/ppermute | solution.py:464
  111.0 12.6 %collective-permute-start.6 = (f32[104,128]{1,0:T(8,128)S(1)}, f32[104,128]{1,0:T(8,128)S(1)}, u32[]{:S(2)}, u32[]{:S(2)}) collective-permute-start(f32[104,128]{1,0:T(8,128)S(1)} %add_add_fusion.1), channel_id=1, source_target_pairs={{0,16},{1,17},{2,18},{3,19},{4,20},{5,21},{6,22},{7,23},{8,24},{9,... | collective-permute-start | bytes 159752 | tf_op jit(solution)/shard_map/ppermute | solution.py:464
  112.1 12.0 %collective-permute-start.5 = (f32[104,128]{1,0:T(8,128)S(1)}, f32[104,128]{1,0:T(8,128)S(1)}, u32[]{:S(2)}, u32[]{:S(2)}) collective-permute-start(f32[104,128]{1,0:T(8,128)S(1)} %add_add_fusion.1), channel_id=1, source_target_pairs={{0,8},{1,9},{2,10},{3,11},{4,12},{5,13},{6,14},{7,15},{8,16},{9,17... | collective-permute-start | bytes 159752 | tf_op jit(solution)/shard_map/ppermute | solution.py:464
  119.4 4.7 %collective-permute-start.4 = (f32[104,128]{1,0:T(8,128)S(1)}, f32[104,128]{1,0:T(8,128)S(1)}, u32[]{:S(2)}, u32[]{:S(2)}) collective-permute-start(f32[104,128]{1,0:T(8,128)S(1)} %add_add_fusion.1), channel_id=1, source_target_pairs={{0,24},{1,25},{2,26},{3,27},{4,28},{5,29},{6,30},{7,31},{8,0},{9,1... | collective-permute-start | bytes 159752 | tf_op jit(solution)/shard_map/ppermute | solution.py:464
  124.1 8.4 %collective-permute-start.7 = (f32[104,128]{1,0:T(8,128)S(1)}, f32[104,128]{1,0:T(8,128)S(1)}, u32[]{:S(2)}, u32[]{:S(2)}) collective-permute-start(f32[104,128]{1,0:T(8,128)S(1)} %add_add_fusion.own_ref), channel_id=1, source_target_pairs={{0,32},{1,33},{2,34},{3,35},{4,36},{5,37},{6,38},{7,39},{8,40},{9,... | collective-permute-start | bytes 159752 | tf_op jit(solution)/shard_map/ppermute | solution.py:464
  124.2 8.4 %collective-permute-start.8 = (f32[104,128]{1,0:T(8,128)S(1)}, f32[104,128]{1,0:T(8,128)S(1)}, u32[]{:S(2)}, u32[]{:S(2)}) collective-permute-start(f32[104,128]{1,0:T(8,128)S(1)} %add_add_fusion.own_ref), channel_id=1, source_target_pairs={{0,64},{1,65},{2,66},{3,67},{4,68},{5,69},{6,70},{7,71},{8,72},{9,... | collective-permute-start | bytes 159752 | tf_op jit(solution)/shard_map/ppermute | solution.py:464
  128.5 4.3 %collective-permute-start.9 = (f32[104,128]{1,0:T(8,128)S(1)}, f32[104,128]{1,0:T(8,128)S(1)}, u32[]{:S(2)}, u32[]{:S(2)}) collective-permute-start(f32[104,128]{1,0:T(8,128)S(1)} %add_add_fusion.own_ref), channel_id=1, source_target_pairs={{0,96},{1,97},{2,98},{3,99},{4,100},{5,101},{6,102},{7,103},{8,104... | collective-permute-start | bytes 159752 | tf_op jit(solution)/shard_map/ppermute | solution.py:464

commit v5 on v4

--- a/solution.py
+++ b/solution.py
@@ -14,12 +14,22 @@
 VMEM = 37 * 1024 * 1024
 LARGE_VMEM = 56 * 1024 * 1024
 SMALL_VMEM = 10 * 1024 * 1024
-BOUNDS = ((0, 0), (1, 8), (4, 4), (7, 4), (9, 0))
-
-
-def send_kernel(blk, owner_ref, fill_ref, vec_ref, list_ref, send_ref, held, tiles, meta, sems):
+BOUNDS = ((0, 0), (1, 8), (4, 8), (7, 4), (9, 0))
+
+
+def send_kernel(
+    blk, owner_hbm, fill_hbm, vec_ref, list_hbm, send_ref, owner_ref, fill_ref, list_ref, held, tiles, meta, sems
+):
     blocks = owner_ref.shape[0]
     width = vec_ref.shape[1]
+    small = [
+        pltpu.make_async_copy(source, target, sems.at[blocks + 5 + i])
+        for i, (source, target) in enumerate(
+            ((owner_hbm, owner_ref), (fill_hbm, fill_ref), (list_hbm, list_ref))
+        )
+    ]
+    for copy in small:
+        copy.start()
     chunks = width // LANES
     span = LANES // blk
     me = lax.axis_index("dev")
@@ -34,6 +44,8 @@
     ]
     for load in loads:
         load.start()
+    for copy in small:
+        copy.wait()
     total = functools.reduce(lambda a, b: a + b, [fill_ref[b] for b in range(blocks)])
     rows = lax.broadcasted_iota(jnp.int32, (META, LANES), 0)
     lane = lax.broadcasted_iota(jnp.int32, (1, LANES), 1)
@@ -78,18 +90,16 @@
     return pl.pallas_call(
         functools.partial(send_kernel, blk),
         out_shape=jax.ShapeDtypeStruct((devices, height + META, LANES), jnp.bfloat16),
-        in_specs=[
-            pl.BlockSpec(memory_space=pltpu.SMEM),
-            pl.BlockSpec(memory_space=pltpu.SMEM),
-            pl.BlockSpec(memory_space=pl.ANY),
-            pl.BlockSpec(memory_space=pltpu.VMEM),
-        ],
+        in_specs=[pl.BlockSpec(memory_space=pl.ANY)] * 4,
         out_specs=pl.BlockSpec(memory_space=pl.ANY),
         scratch_shapes=[
+            pltpu.SMEM((blocks,), jnp.int32),
+            pltpu.SMEM((blocks,), jnp.int32),
+            pltpu.VMEM((rows // LANES, LANES), jnp.int32),
             pltpu.VMEM((4, rows // 4, width), jnp.bfloat16),
             pltpu.VMEM((blocks, height, LANES), jnp.bfloat16),
             pltpu.VMEM((devices, META, LANES), jnp.bfloat16),
-            pltpu.SemaphoreType.DMA((blocks + 5,)),
+            pltpu.SemaphoreType.DMA((blocks + 8,)),
         ],
         compiler_params=pltpu.CompilerParams(vmem_limit_bytes=LARGE_VMEM),
         name="build_send",
@@ -98,7 +108,7 @@
 
 def update_kernel(
     blk, recv_ref, old_ref, cent_ref, turned, where_ref, packed_ref, total_ref,
-    blocks, info, old, dense, hot, values, column, place_ref, sums, counts, parts, gram, sems,
+    blocks, info, dense, hot, values, column, place_ref, sums, counts, parts, gram, sems,
 ):
     slots, height, _ = recv_ref.shape
     lists, width = old_ref.shape
@@ -118,8 +128,6 @@
     for c in range(blocks.shape[0]):
         fetch(c).start()
 
-    own = pltpu.make_async_copy(old_ref, old, sems.at[1 + blocks.shape[0]])
-    own.start()
     notes.wait()
     lines, seen = [], jnp.zeros((META, LANES), jnp.float32)
     for q in range(slots // span):
@@ -168,7 +176,7 @@
 
     def prepare(g):
         at = pl.ds(pl.multiple_of(g * GROUP, GROUP), GROUP)
-        code = jnp.sum(dense[chunks, at, :].T, axis=0, keepdims=True)
+        code = jnp.sum(dense[chunks, at, :].T[0 : slots // span], axis=0, keepdims=True)
         ids = lax.broadcasted_iota(jnp.int32, (lists, GROUP), 0).astype(jnp.float32) + 1.0
         hot[g] = jnp.where(ids == code, 1.0, 0.0).astype(jnp.bfloat16)
         for j in range(chunks):
@@ -191,9 +199,8 @@
 
     lax.fori_loop(0, groups, gather, 0)
 
-    count = jnp.sum(counts[...], axis=1, keepdims=True) + 1.0
-    own.wait()
-    cent = (sums[...] + old[...]) / count
+    share = 1.0 / (jnp.sum(counts[...], axis=1, keepdims=True) + 1.0)
+    cent = (sums[...] + old_ref[...]) * share
     sums[...] = cent
     write = pltpu.make_async_copy(sums, cent_ref, sems.at[0])
     write.start()
@@ -282,7 +289,7 @@
         ),
         in_specs=[
             pl.BlockSpec(memory_space=pl.ANY),
-            pl.BlockSpec(memory_space=pl.ANY),
+            pl.BlockSpec(memory_space=pltpu.VMEM),
         ],
         out_specs=(
             pl.BlockSpec(memory_space=pl.ANY),
@@ -294,7 +301,6 @@
         scratch_shapes=[
             pltpu.VMEM((8, slots // 8, chunks * blk, LANES), jnp.bfloat16),
             pltpu.VMEM((slots, META, LANES), jnp.bfloat16),
-            pltpu.VMEM((lists, width), jnp.float32),
             pltpu.VMEM((chunks + 1, rows + GROUP + blk, LANES), jnp.float32),
             pltpu.VMEM((groups + 1, lists, GROUP), jnp.bfloat16),
             pltpu.VMEM((2, GROUP, width), jnp.bfloat16),
@@ -466,7 +472,7 @@
     packed = packed + shifted(packed, 1, 1, 2)
     stride = 2
     while True:
-        two, one, three = (shifted(packed, stride, k, 4) for k in (2, 1, 3))
+        three, one, two = (shifted(packed, stride, k, 4) for k in (3, 1, 2))
         even = me // stride % 2 == 0
         terms = (packed, jnp.where(even, three, one), two, jnp.where(even, one, three))
         stride *= 4

time: 134 us -> 133 us (level); the launches traced: 134 us -> 134 us
  transfers between devices with their start and end apart: 11 -> 11, of which waited for: 4 -> 4; matrix products, arithmetic and copies ran while one was open for 3% -> 3% of each run, Pallas kernels for 4% -> 5%
where the time goes in v5:
time: 133 us; the launch traced here: 134 us
  waiting for transfers between devices  76.2 us (57%)
  starting transfers between devices  35.1 us (26%)
  Pallas kernels  17.3 us (13%)
  local copies, waits for them, and re-layouts  3.29 us (2%)
  other arithmetic  1.5 us (1%)
    all_to_all x1, waiting for transfers between devices, body(): recv = lax.all_to_all(send, 'dev', split_axis=0, concat_axis=0, tiled=True)  73.7 us
    ppermute x10, starting transfers between devices, shifted(): return lax.ppermute(values, 'dev', pairs)  23.5 us
    all_to_all x1, starting transfers between devices, body(): recv = lax.all_to_all(send, 'dev', split_axis=0, concat_axis=0, tiled=True)  11.6 us
    pallas_call x1, Pallas kernels, update_lists(): pl.pallas_call(functools.partial(update_kernel, blk), out_shape=(jax.Shap...  7.49 us
    pallas_call x4, Pallas kernels, row_errors(): pl.pallas_call(functools.partial(error_kernel, sub, part, blk), out_shape...  6.33 us
  transfers between devices with their start and end apart: 11, of which 4 were waited for; matrix products, arithmetic and copies ran while one was open for 3% of the time, Pallas kernels for 5%

profile of v5, /device:TPU:0, one launch (start us, length us, event | category | flops | bytes accessed | tf_op | source)
XLA Modules:
  0.0 134.3 jit_solution(13306352806826782936)
XLA Ops:
  0.6 2.6 %build_send.1 = bf16[128,200,128]{2,1,0:T(8,128)(2,1)} custom-call(s32[32]{0:T(128)} %owner_hbm.1, s32[32]{0:T(128)} %fill_hbm.1, bf16[1024,768]{1,0:T(8,128)(2,1)} %vec_ref.1, s32[8,128]{1,0:T(8,128)} %bitcast.12), custom_call_target="tpu_custom_call" | custom-call | tf_op jit(solution)/shard_map/build_send/pallas_call | solution.py:90
  3.2 0.0 copy-start.2
  3.2 11.6 %all-to-all-start = ((bf16[128,200,128]{2,1,0:T(8,128)(2,1)}), bf16[128,200,128]{2,1,0:T(8,128)(2,1)}, u32[]{:S(2)}, u32[]{:S(2)}) async-start(bf16[128,200,128]{2,1,0:T(8,128)(2,1)} %build_send.1), calls=%async_computation | async-start | bytes 13107200 | tf_op jit(solution)/shard_map/all_to_all | solution.py:456
  14.9 0.6 copy.20
  15.6 0.1 multiply_reduce_fusion
  15.7 1.6 %copy.21 = bf16[24,256,3]{2,1,0:T(8,128)(2,1)} copy(bf16[24,256,3]{1,0,2:T(8,128)(2,1)S(1)} %pad_maximum_fusion) | data formatting | bytes 73728 | tf_op jit(solution)/shard_map/stack | solution.py:444
  17.3 0.4 fusion.2
  17.7 1.0 copy-done.1
  18.8 1.0 fusion.1.book_ref
  19.7 73.7 %all-to-all-done.recv_ref = bf16[128,200,128]{2,1,0:T(8,128)(2,1)} async-done(((bf16[128,200,128]{2,1,0:T(8,128)(2,1)}), bf16[128,200,128]{2,1,0:T(8,128)(2,1)}, u32[]{:S(2)}, u32[]{:S(2)}) %all-to-all-start) | async-done | bytes 6553632 | tf_op jit(solution)/shard_map/all_to_all | solution.py:456
  93.4 7.5 %update_lists.1 = (f32[512,768]{1,0:T(8,128)}, bf16[17,768,256]{2,1,0:T(8,128)(2,1)S(1)}, s32[8,128]{1,0:T(8,128)S(1)}, f32[104,128]{1,0:T(8,128)S(1)}, f32[8,128]{1,0:T(8,128)S(1)}) custom-call(bf16[128,200,128]{2,1,0:T(8,128)(2,1)} %all-to-all-done.recv_ref, f32[512,768]{1,0:T(8,128)S(1)} %copy-done), custom_call_target="tpu_custom_call" | custom-call | tf_op jit(solution)/shard_map/update_lists/pallas_call | solution.py:281
  100.9 0.1 collective-permute-start
  101.0 1.6 %row_errors.4.rest_0_ = f32[40,128]{1,0:T(8,128)S(1)} custom-call(s32[8,128]{1,0:T(8,128)S(1)} %get-tuple-element.10.place_ref, bf16[17,768,256]{2,1,0:T(8,128)(2,1)S(1)} %get-tuple-element.11.resid_ref, bf16[24,256,48]{2,1,0:T(8,128)(2,1)S(1)} %fusion.1.book_ref), custom_call_target="tpu_custom_call" | custom-call | flops 2415919104 | bytes 1179648 | tf_op jit(solution)/shard_map/row_errors/pallas_call | solution.py:383
  102.6 0.0 collective-permute-done
  102.6 7.6 %collective-permute-start.3 = (f32[104,128]{1,0:T(8,128)S(1)}, f32[104,128]{1,0:T(8,128)S(1)}, u32[]{:S(2)}, u32[]{:S(2)}) collective-permute-start(f32[104,128]{1,0:T(8,128)S(1)} %add.37), channel_id=1, source_target_pairs={{0,4},{1,5},{2,6},{3,7},{4,0},{5,1},{6,2},{7,3},{8,12},{9,13},{10,... | collective-permute-start | bytes 159752 | tf_op jit(solution)/shard_map/ppermute | solution.py:470
  110.2 3.2 %collective-permute-start.1 = (f32[104,128]{1,0:T(8,128)S(1)}, f32[104,128]{1,0:T(8,128)S(1)}, u32[]{:S(2)}, u32[]{:S(2)}) collective-permute-start(f32[104,128]{1,0:T(8,128)S(1)} %add.37), channel_id=1, source_target_pairs={{0,6},{1,7},{2,0},{3,1},{4,2},{5,3},{6,4},{7,5},{8,14},{9,15},{10,... | collective-permute-start | bytes 159752 | tf_op jit(solution)/shard_map/ppermute | solution.py:470
  113.4 1.6 %row_errors.5.rest_0_ = f32[40,128]{1,0:T(8,128)S(1)} custom-call(s32[8,128]{1,0:T(8,128)S(1)} %get-tuple-element.10.place_ref, bf16[17,768,256]{2,1,0:T(8,128)(2,1)S(1)} %get-tuple-element.11.resid_ref, bf16[24,256,48]{2,1,0:T(8,128)(2,1)S(1)} %fusion.1.book_ref, f32[40,128]{1,0:T(8,128)S(1)} %row_errors.4.rest_0_), custom_call_target="tpu_custom_call" | custom-call | flops 2415919104 | bytes 1179648 | tf_op jit(solution)/shard_map/row_errors/pallas_call | solution.py:383
  115.0 0.0 collective-permute-done.3
  115.0 0.5 collective-permute-done.2
  115.5 0.1 collective-permute-start.6
  115.6 0.4 collective-permute-start.5
  116.1 2.9 %collective-permute-start.4 = (f32[104,128]{1,0:T(8,128)S(1)}, f32[104,128]{1,0:T(8,128)S(1)}, u32[]{:S(2)}, u32[]{:S(2)}) collective-permute-start(f32[104,128]{1,0:T(8,128)S(1)} %add_add_fusion.1), channel_id=1, source_target_pairs={{0,24},{1,25},{2,26},{3,27},{4,28},{5,29},{6,30},{7,31},{8,0},{9,1... | collective-permute-start | bytes 159752 | tf_op jit(solution)/shard_map/ppermute | solution.py:470
  118.9 0.6 row_errors.6.rest_0_
  119.6 1.8 %collective-permute-done.6 = f32[104,128]{1,0:T(8,128)S(1)} collective-permute-done((f32[104,128]{1,0:T(8,128)S(1)}, f32[104,128]{1,0:T(8,128)S(1)}, u32[]{:S(2)}, u32[]{:S(2)}) %collective-permute-start.6) | collective-permute-done | bytes 53280 | tf_op jit(solution)/shard_map/ppermute | solution.py:470
  121.4 0.3 collective-permute-done.5
  121.6 0.0 collective-permute-done.4
  121.6 0.1 collective-permute-start.7
  121.7 6.6 %collective-permute-start.8 = (f32[104,128]{1,0:T(8,128)S(1)}, f32[104,128]{1,0:T(8,128)S(1)}, u32[]{:S(2)}, u32[]{:S(2)}) collective-permute-start(f32[104,128]{1,0:T(8,128)S(1)} %add_add_fusion.own_ref), channel_id=1, source_target_pairs={{0,64},{1,65},{2,66},{3,67},{4,68},{5,69},{6,70},{7,71},{8,72},{9,... | collective-permute-start | bytes 159752 | tf_op jit(solution)/shard_map/ppermute | solution.py:470
  128.3 2.5 %collective-permute-start.9 = (f32[104,128]{1,0:T(8,128)S(1)}, f32[104,128]{1,0:T(8,128)S(1)}, u32[]{:S(2)}, u32[]{:S(2)}) collective-permute-start(f32[104,128]{1,0:T(8,128)S(1)} %add_add_fusion.own_ref), channel_id=1, source_target_pairs={{0,96},{1,97},{2,98},{3,99},{4,100},{5,101},{6,102},{7,103},{8,104... | collective-permute-start | bytes 159752 | tf_op jit(solution)/shard_map/ppermute | solution.py:470
  130.8 2.5 %row_errors.7 = (f32[40,128]{1,0:T(8,128)}, f32[32,128]{1,0:T(8,128)}) custom-call(s32[8,128]{1,0:T(8,128)S(1)} %get-tuple-element.10.place_ref, bf16[17,768,256]{2,1,0:T(8,128)(2,1)S(1)} %get-tuple-element.11.resid_ref, bf16[24,256,48]{2,1,0:T(8,128)(2,1)S(1)} %fusion.1.book_ref, f32[40,128]{1,0:T(8,128)S(1)} %row_errors.6.rest_0_), custom_call_target="tpu_custom_call" | custom-call | flops 2415919104 | bytes 1179648 | tf_op jit(solution)/shard_map/row_errors/pallas_call | solution.py:383
  133.4 0.0 collective-permute-done.7.one_ref
  133.4 1.0 unpack_moments.1
  (13 shorter events, 0.1 us)
Async XLA Ops:
  3.2 11.7 %copy-start.2 = (bf16[24,32,256]{2,1,0:T(8,128)(2,1)S(1)}, bf16[24,32,256]{2,1,0:T(8,128)(2,1)}, u32[]{:S(2)}) copy-start(bf16[24,32,256]{2,1,0:T(8,128)(2,1)} %param.11) | copy-start | bytes 1179652
  3.2 90.2 %all-to-all-start = ((bf16[128,200,128]{2,1,0:T(8,128)(2,1)}), bf16[128,200,128]{2,1,0:T(8,128)(2,1)}, u32[]{:S(2)}, u32[]{:S(2)}) async-start(bf16[128,200,128]{2,1,0:T(8,128)(2,1)} %build_send.1), calls=%async_computation | async-start | bytes 13107200 | tf_op jit(solution)/shard_map/all_to_all | solution.py:456
  17.3 1.4 %copy-start.1 = (bf16[24,256,3]{2,1,0:T(8,128)(2,1)S(1)}, bf16[24,256,3]{2,1,0:T(8,128)(2,1)}, u32[]{:S(2)}) copy-start(bf16[24,256,3]{2,1,0:T(8,128)(2,1)} %copy.21) | copy-start | bytes 110596
  18.8 74.6 %copy-start = (f32[512,768]{1,0:T(8,128)S(1)}, f32[512,768]{1,0:T(8,128)}, u32[]{:S(2)}) copy-start(f32[512,768]{1,0:T(8,128)} %old_ref.1) | copy-start | bytes 4718596
  100.9 1.7 %collective-permute-start = (f32[104,128]{1,0:T(8,128)S(1)}, f32[104,128]{1,0:T(8,128)S(1)}, u32[]{:S(2)}, u32[]{:S(2)}) collective-permute-start(f32[104,128]{1,0:T(8,128)S(1)} %get-tuple-element.13), channel_id=1, source_target_pairs={{0,1},{1,0},{2,3},{3,2},{4,5},{5,4},{6,7},{7,6},{8,9},{9,8},{10,11... | collective-permute-start | bytes 159752 | tf_op jit(solution)/shard_map/ppermute | solution.py:470
  102.6 12.4 %collective-permute-start.3 = (f32[104,128]{1,0:T(8,128)S(1)}, f32[104,128]{1,0:T(8,128)S(1)}, u32[]{:S(2)}, u32[]{:S(2)}) collective-permute-start(f32[104,128]{1,0:T(8,128)S(1)} %add.37), channel_id=1, source_target_pairs={{0,4},{1,5},{2,6},{3,7},{4,0},{5,1},{6,2},{7,3},{8,12},{9,13},{10,... | collective-permute-start | bytes 159752 | tf_op jit(solution)/shard_map/ppermute | solution.py:470
  110.2 5.3 %collective-permute-start.2 = (f32[104,128]{1,0:T(8,128)S(1)}, f32[104,128]{1,0:T(8,128)S(1)}, u32[]{:S(2)}, u32[]{:S(2)}) collective-permute-start(f32[104,128]{1,0:T(8,128)S(1)} %add.37), channel_id=1, source_target_pairs={{0,2},{1,3},{2,4},{3,5},{4,6},{5,7},{6,0},{7,1},{8,10},{9,11},{10,... | collective-permute-start | bytes 159752 | tf_op jit(solution)/shard_map/ppermute | solution.py:470
  110.2 5.3 %collective-permute-start.1 = (f32[104,128]{1,0:T(8,128)S(1)}, f32[104,128]{1,0:T(8,128)S(1)}, u32[]{:S(2)}, u32[]{:S(2)}) collective-permute-start(f32[104,128]{1,0:T(8,128)S(1)} %add.37), channel_id=1, source_target_pairs={{0,6},{1,7},{2,0},{3,1},{4,2},{5,3},{6,4},{7,5},{8,14},{9,15},{10,... | collective-permute-start | bytes 159752 | tf_op jit(solution)/shard_map/ppermute | solution.py:470
  115.5 5.8 %collective-permute-start.6 = (f32[104,128]{1,0:T(8,128)S(1)}, f32[104,128]{1,0:T(8,128)S(1)}, u32[]{:S(2)}, u32[]{:S(2)}) collective-permute-start(f32[104,128]{1,0:T(8,128)S(1)} %add_add_fusion.1), channel_id=1, source_target_pairs={{0,16},{1,17},{2,18},{3,19},{4,20},{5,21},{6,22},{7,23},{8,24},{9,... | collective-permute-start | bytes 159752 | tf_op jit(solution)/shard_map/ppermute | solution.py:470
  115.6 6.0 %collective-permute-start.5 = (f32[104,128]{1,0:T(8,128)S(1)}, f32[104,128]{1,0:T(8,128)S(1)}, u32[]{:S(2)}, u32[]{:S(2)}) collective-permute-start(f32[104,128]{1,0:T(8,128)S(1)} %add_add_fusion.1), channel_id=1, source_target_pairs={{0,8},{1,9},{2,10},{3,11},{4,12},{5,13},{6,14},{7,15},{8,16},{9,17... | collective-permute-start | bytes 159752 | tf_op jit(solution)/shard_map/ppermute | solution.py:470
  116.1 5.5 %collective-permute-start.4 = (f32[104,128]{1,0:T(8,128)S(1)}, f32[104,128]{1,0:T(8,128)S(1)}, u32[]{:S(2)}, u32[]{:S(2)}) collective-permute-start(f32[104,128]{1,0:T(8,128)S(1)} %add_add_fusion.1), channel_id=1, source_target_pairs={{0,24},{1,25},{2,26},{3,27},{4,28},{5,29},{6,30},{7,31},{8,0},{9,1... | collective-permute-start | bytes 159752 | tf_op jit(solution)/shard_map/ppermute | solution.py:470
  121.6 11.7 %collective-permute-start.7 = (f32[104,128]{1,0:T(8,128)S(1)}, f32[104,128]{1,0:T(8,128)S(1)}, u32[]{:S(2)}, u32[]{:S(2)}) collective-permute-start(f32[104,128]{1,0:T(8,128)S(1)} %add_add_fusion.own_ref), channel_id=1, source_target_pairs={{0,32},{1,33},{2,34},{3,35},{4,36},{5,37},{6,38},{7,39},{8,40},{9,... | collective-permute-start | bytes 159752 | tf_op jit(solution)/shard_map/ppermute | solution.py:470
  121.7 11.6 %collective-permute-start.8 = (f32[104,128]{1,0:T(8,128)S(1)}, f32[104,128]{1,0:T(8,128)S(1)}, u32[]{:S(2)}, u32[]{:S(2)}) collective-permute-start(f32[104,128]{1,0:T(8,128)S(1)} %add_add_fusion.own_ref), channel_id=1, source_target_pairs={{0,64},{1,65},{2,66},{3,67},{4,68},{5,69},{6,70},{7,71},{8,72},{9,... | collective-permute-start | bytes 159752 | tf_op jit(solution)/shard_map/ppermute | solution.py:470
  128.3 5.1 %collective-permute-start.9 = (f32[104,128]{1,0:T(8,128)S(1)}, f32[104,128]{1,0:T(8,128)S(1)}, u32[]{:S(2)}, u32[]{:S(2)}) collective-permute-start(f32[104,128]{1,0:T(8,128)S(1)} %add_add_fusion.own_ref), channel_id=1, source_target_pairs={{0,96},{1,97},{2,98},{3,99},{4,100},{5,101},{6,102},{7,103},{8,104... | collective-permute-start | bytes 159752 | tf_op jit(solution)/shard_map/ppermute | solution.py:470

commit v6 on v5

--- a/solution.py
+++ b/solution.py
@@ -186,21 +186,25 @@
 
     prepare(0)
 
-    def gather(g, carry):
+    def add(g):
         chosen = hot[g]
         added = jnp.dot(chosen, values[g & 1], preferred_element_type=jnp.float32)
         part = chosen[:, 0:LANES].astype(jnp.float32)
         for k in range(1, GROUP // LANES):
             part = part + chosen[:, k * LANES : (k + 1) * LANES].astype(jnp.float32)
+        return added, part
+
+    def gather(g, carry):
+        added, part = add(g)
         prepare(g + 1)
         sums[...] += added
         counts[...] += part
         return carry
 
-    lax.fori_loop(0, groups, gather, 0)
-
-    share = 1.0 / (jnp.sum(counts[...], axis=1, keepdims=True) + 1.0)
-    cent = (sums[...] + old_ref[...]) * share
+    lax.fori_loop(0, groups - 1, gather, 0)
+    added, part = add(groups - 1)
+    share = 1.0 / (jnp.sum(counts[...] + part, axis=1, keepdims=True) + 1.0)
+    cent = (sums[...] + added + old_ref[...]) * share
     sums[...] = cent
     write = pltpu.make_async_copy(sums, cent_ref, sems.at[0])
     write.start()

time: 133 us -> 134 us (level); the launches traced: 134 us -> 132 us
  Pallas kernels: 17.3 us -> 14.8 us
    pallas_call x1, Pallas kernels: 7.49 us -> 5.94 us  [update_lists(): pl.pallas_call(functools.partial(update_kernel, blk), out_shape=(jax.Shap...]
  transfers between devices with their start and end apart: 11 -> 11, of which waited for: 4 -> 4; matrix products, arithmetic and copies ran while one was open for 3% -> 3% of each run, Pallas kernels for 5% -> 4%
where the time goes in v6:
time: 134 us; the launch traced here: 132 us
  waiting for transfers between devices  76 us (57%)
  starting transfers between devices  36 us (27%)
  Pallas kernels  14.8 us (11%)
  local copies, waits for them, and re-layouts  3.29 us (2%)
  other arithmetic  1.5 us (1%)
    all_to_all x1, waiting for transfers between devices, body(): recv = lax.all_to_all(send, 'dev', split_axis=0, concat_axis=0, tiled=True)  73.7 us
    ppermute x10, starting transfers between devices, shifted(): return lax.ppermute(values, 'dev', pairs)  24.4 us
    all_to_all x1, starting transfers between devices, body(): recv = lax.all_to_all(send, 'dev', split_axis=0, concat_axis=0, tiled=True)  11.6 us
    pallas_call x1, Pallas kernels, update_lists(): pl.pallas_call(functools.partial(update_kernel, blk), out_shape=(jax.Shap...  5.94 us
    pallas_call x4, Pallas kernels, row_errors(): pl.pallas_call(functools.partial(error_kernel, sub, part, blk), out_shape...  5.38 us
  transfers between devices with their start and end apart: 11, of which 4 were waited for; matrix products, arithmetic and copies ran while one was open for 3% of the time, Pallas kernels for 4%

profile of v6, /device:TPU:0, one launch (start us, length us, event | category | flops | bytes accessed | tf_op | source)
XLA Modules:
  0.0 132.4 jit_solution(7129653162933346091)
XLA Ops:
  0.6 2.6 %build_send.1 = bf16[128,200,128]{2,1,0:T(8,128)(2,1)} custom-call(s32[32]{0:T(128)} %owner_hbm.1, s32[32]{0:T(128)} %fill_hbm.1, bf16[1024,768]{1,0:T(8,128)(2,1)} %vec_ref.1, s32[8,128]{1,0:T(8,128)} %bitcast.12), custom_call_target="tpu_custom_call" | custom-call | tf_op jit(solution)/shard_map/build_send/pallas_call | solution.py:90
  3.2 0.0 copy-start.2
  3.2 11.6 %all-to-all-start = ((bf16[128,200,128]{2,1,0:T(8,128)(2,1)}), bf16[128,200,128]{2,1,0:T(8,128)(2,1)}, u32[]{:S(2)}, u32[]{:S(2)}) async-start(bf16[128,200,128]{2,1,0:T(8,128)(2,1)} %build_send.1), calls=%async_computation | async-start | bytes 13107200 | tf_op jit(solution)/shard_map/all_to_all | solution.py:460
  14.9 0.6 copy.20
  15.5 0.1 multiply_reduce_fusion
  15.7 1.6 %copy.21 = bf16[24,256,3]{2,1,0:T(8,128)(2,1)} copy(bf16[24,256,3]{1,0,2:T(8,128)(2,1)S(1)} %pad_maximum_fusion) | data formatting | bytes 73728 | tf_op jit(solution)/shard_map/stack | solution.py:448
  17.3 0.4 fusion.2
  17.7 1.0 copy-done.1
  18.7 1.0 fusion.1.book_ref
  19.7 73.7 %all-to-all-done.recv_ref = bf16[128,200,128]{2,1,0:T(8,128)(2,1)} async-done(((bf16[128,200,128]{2,1,0:T(8,128)(2,1)}), bf16[128,200,128]{2,1,0:T(8,128)(2,1)}, u32[]{:S(2)}, u32[]{:S(2)}) %all-to-all-start) | async-done | bytes 6553632 | tf_op jit(solution)/shard_map/all_to_all | solution.py:460
  93.4 5.9 %update_lists.1 = (f32[512,768]{1,0:T(8,128)}, bf16[17,768,256]{2,1,0:T(8,128)(2,1)S(1)}, s32[8,128]{1,0:T(8,128)S(1)}, f32[104,128]{1,0:T(8,128)S(1)}, f32[8,128]{1,0:T(8,128)S(1)}) custom-call(bf16[128,200,128]{2,1,0:T(8,128)(2,1)} %all-to-all-done.recv_ref, f32[512,768]{1,0:T(8,128)S(1)} %copy-done), custom_call_target="tpu_custom_call" | custom-call | tf_op jit(solution)/shard_map/update_lists/pallas_call | solution.py:285
  99.3 0.1 collective-permute-start
  99.4 1.6 %row_errors.4.rest_0_ = f32[40,128]{1,0:T(8,128)S(1)} custom-call(s32[8,128]{1,0:T(8,128)S(1)} %get-tuple-element.10.place_ref, bf16[17,768,256]{2,1,0:T(8,128)(2,1)S(1)} %get-tuple-element.11.resid_ref, bf16[24,256,48]{2,1,0:T(8,128)(2,1)S(1)} %fusion.1.book_ref), custom_call_target="tpu_custom_call" | custom-call | flops 2415919104 | bytes 1179648 | tf_op jit(solution)/shard_map/row_errors/pallas_call | solution.py:387
  101.0 0.0 collective-permute-done
  101.0 1.3 %collective-permute-start.3 = (f32[104,128]{1,0:T(8,128)S(1)}, f32[104,128]{1,0:T(8,128)S(1)}, u32[]{:S(2)}, u32[]{:S(2)}) collective-permute-start(f32[104,128]{1,0:T(8,128)S(1)} %add.37), channel_id=1, source_target_pairs={{0,4},{1,5},{2,6},{3,7},{4,0},{5,1},{6,2},{7,3},{8,12},{9,13},{10,... | collective-permute-start | bytes 159752 | tf_op jit(solution)/shard_map/ppermute | solution.py:474
  102.3 2.6 %collective-permute-start.2 = (f32[104,128]{1,0:T(8,128)S(1)}, f32[104,128]{1,0:T(8,128)S(1)}, u32[]{:S(2)}, u32[]{:S(2)}) collective-permute-start(f32[104,128]{1,0:T(8,128)S(1)} %add.37), channel_id=1, source_target_pairs={{0,2},{1,3},{2,4},{3,5},{4,6},{5,7},{6,0},{7,1},{8,10},{9,11},{10,... | collective-permute-start | bytes 159752 | tf_op jit(solution)/shard_map/ppermute | solution.py:474
  104.9 2.6 %collective-permute-start.1 = (f32[104,128]{1,0:T(8,128)S(1)}, f32[104,128]{1,0:T(8,128)S(1)}, u32[]{:S(2)}, u32[]{:S(2)}) collective-permute-start(f32[104,128]{1,0:T(8,128)S(1)} %add.37), channel_id=1, source_target_pairs={{0,6},{1,7},{2,0},{3,1},{4,2},{5,3},{6,4},{7,5},{8,14},{9,15},{10,... | collective-permute-start | bytes 159752 | tf_op jit(solution)/shard_map/ppermute | solution.py:474
  107.5 0.6 row_errors.5.rest_0_
  108.2 1.6 %collective-permute-done.2 = f32[104,128]{1,0:T(8,128)S(1)} collective-permute-done((f32[104,128]{1,0:T(8,128)S(1)}, f32[104,128]{1,0:T(8,128)S(1)}, u32[]{:S(2)}, u32[]{:S(2)}) %collective-permute-start.2) | collective-permute-done | bytes 53280 | tf_op jit(solution)/shard_map/ppermute | solution.py:474
  109.7 0.0 collective-permute-done.1
  109.8 4.7 %collective-permute-start.6 = (f32[104,128]{1,0:T(8,128)S(1)}, f32[104,128]{1,0:T(8,128)S(1)}, u32[]{:S(2)}, u32[]{:S(2)}) collective-permute-start(f32[104,128]{1,0:T(8,128)S(1)} %add_add_fusion.1), channel_id=1, source_target_pairs={{0,16},{1,17},{2,18},{3,19},{4,20},{5,21},{6,22},{7,23},{8,24},{9,... | collective-permute-start | bytes 159752 | tf_op jit(solution)/shard_map/ppermute | solution.py:474
  114.4 0.0 collective-permute-start.5
  114.5 3.2 %collective-permute-start.4 = (f32[104,128]{1,0:T(8,128)S(1)}, f32[104,128]{1,0:T(8,128)S(1)}, u32[]{:S(2)}, u32[]{:S(2)}) collective-permute-start(f32[104,128]{1,0:T(8,128)S(1)} %add_add_fusion.1), channel_id=1, source_target_pairs={{0,24},{1,25},{2,26},{3,27},{4,28},{5,29},{6,30},{7,31},{8,0},{9,1... | collective-permute-start | bytes 159752 | tf_op jit(solution)/shard_map/ppermute | solution.py:474
  117.7 1.6 %row_errors.6.rest_0_ = f32[40,128]{1,0:T(8,128)S(1)} custom-call(s32[8,128]{1,0:T(8,128)S(1)} %get-tuple-element.10.place_ref, bf16[17,768,256]{2,1,0:T(8,128)(2,1)S(1)} %get-tuple-element.11.resid_ref, bf16[24,256,48]{2,1,0:T(8,128)(2,1)S(1)} %fusion.1.book_ref, f32[40,128]{1,0:T(8,128)S(1)} %row_errors.5.rest_0_), custom_call_target="tpu_custom_call" | custom-call | flops 2415919104 | bytes 1179648 | tf_op jit(solution)/shard_map/row_errors/pallas_call | solution.py:387
  119.3 0.0 collective-permute-done.6
  119.3 0.5 collective-permute-done.5
  119.8 3.1 %collective-permute-start.7 = (f32[104,128]{1,0:T(8,128)S(1)}, f32[104,128]{1,0:T(8,128)S(1)}, u32[]{:S(2)}, u32[]{:S(2)}) collective-permute-start(f32[104,128]{1,0:T(8,128)S(1)} %add_add_fusion.own_ref), channel_id=1, source_target_pairs={{0,32},{1,33},{2,34},{3,35},{4,36},{5,37},{6,38},{7,39},{8,40},{9,... | collective-permute-start | bytes 159752 | tf_op jit(solution)/shard_map/ppermute | solution.py:474
  122.9 4.3 %collective-permute-start.8 = (f32[104,128]{1,0:T(8,128)S(1)}, f32[104,128]{1,0:T(8,128)S(1)}, u32[]{:S(2)}, u32[]{:S(2)}) collective-permute-start(f32[104,128]{1,0:T(8,128)S(1)} %add_add_fusion.own_ref), channel_id=1, source_target_pairs={{0,64},{1,65},{2,66},{3,67},{4,68},{5,69},{6,70},{7,71},{8,72},{9,... | collective-permute-start | bytes 159752 | tf_op jit(solution)/shard_map/ppermute | solution.py:474
  127.2 2.5 %collective-permute-start.9 = (f32[104,128]{1,0:T(8,128)S(1)}, f32[104,128]{1,0:T(8,128)S(1)}, u32[]{:S(2)}, u32[]{:S(2)}) collective-permute-start(f32[104,128]{1,0:T(8,128)S(1)} %add_add_fusion.own_ref), channel_id=1, source_target_pairs={{0,96},{1,97},{2,98},{3,99},{4,100},{5,101},{6,102},{7,103},{8,104... | collective-permute-start | bytes 159752 | tf_op jit(solution)/shard_map/ppermute | solution.py:474
  129.7 1.6 %row_errors.7 = (f32[40,128]{1,0:T(8,128)}, f32[32,128]{1,0:T(8,128)}) custom-call(s32[8,128]{1,0:T(8,128)S(1)} %get-tuple-element.10.place_ref, bf16[17,768,256]{2,1,0:T(8,128)(2,1)S(1)} %get-tuple-element.11.resid_ref, bf16[24,256,48]{2,1,0:T(8,128)(2,1)S(1)} %fusion.1.book_ref, f32[40,128]{1,0:T(8,128)S(1)} %row_errors.6.rest_0_), custom_call_target="tpu_custom_call" | custom-call | flops 2415919104 | bytes 1179648 | tf_op jit(solution)/shard_map/row_errors/pallas_call | solution.py:387
  131.3 0.2 collective-permute-done.9.three_ref
  131.5 0.9 unpack_moments.1
  (13 shorter events, 0.1 us)
Async XLA Ops:
  3.2 11.7 %copy-start.2 = (bf16[24,32,256]{2,1,0:T(8,128)(2,1)S(1)}, bf16[24,32,256]{2,1,0:T(8,128)(2,1)}, u32[]{:S(2)}) copy-start(bf16[24,32,256]{2,1,0:T(8,128)(2,1)} %param.11) | copy-start | bytes 1179652
  3.2 90.1 %all-to-all-start = ((bf16[128,200,128]{2,1,0:T(8,128)(2,1)}), bf16[128,200,128]{2,1,0:T(8,128)(2,1)}, u32[]{:S(2)}, u32[]{:S(2)}) async-start(bf16[128,200,128]{2,1,0:T(8,128)(2,1)} %build_send.1), calls=%async_computation | async-start | bytes 13107200 | tf_op jit(solution)/shard_map/all_to_all | solution.py:460
  17.3 1.4 %copy-start.1 = (bf16[24,256,3]{2,1,0:T(8,128)(2,1)S(1)}, bf16[24,256,3]{2,1,0:T(8,128)(2,1)}, u32[]{:S(2)}) copy-start(bf16[24,256,3]{2,1,0:T(8,128)(2,1)} %copy.21) | copy-start | bytes 110596
  18.7 74.6 %copy-start = (f32[512,768]{1,0:T(8,128)S(1)}, f32[512,768]{1,0:T(8,128)}, u32[]{:S(2)}) copy-start(f32[512,768]{1,0:T(8,128)} %old_ref.1) | copy-start | bytes 4718596
  99.3 1.7 %collective-permute-start = (f32[104,128]{1,0:T(8,128)S(1)}, f32[104,128]{1,0:T(8,128)S(1)}, u32[]{:S(2)}, u32[]{:S(2)}) collective-permute-start(f32[104,128]{1,0:T(8,128)S(1)} %get-tuple-element.13), channel_id=1, source_target_pairs={{0,1},{1,0},{2,3},{3,2},{4,5},{5,4},{6,7},{7,6},{8,9},{9,8},{10,11... | collective-permute-start | bytes 159752 | tf_op jit(solution)/shard_map/ppermute | solution.py:474
  101.0 7.2 %collective-permute-start.3 = (f32[104,128]{1,0:T(8,128)S(1)}, f32[104,128]{1,0:T(8,128)S(1)}, u32[]{:S(2)}, u32[]{:S(2)}) collective-permute-start(f32[104,128]{1,0:T(8,128)S(1)} %add.37), channel_id=1, source_target_pairs={{0,4},{1,5},{2,6},{3,7},{4,0},{5,1},{6,2},{7,3},{8,12},{9,13},{10,... | collective-permute-start | bytes 159752 | tf_op jit(solution)/shard_map/ppermute | solution.py:474
  102.3 7.4 %collective-permute-start.2 = (f32[104,128]{1,0:T(8,128)S(1)}, f32[104,128]{1,0:T(8,128)S(1)}, u32[]{:S(2)}, u32[]{:S(2)}) collective-permute-start(f32[104,128]{1,0:T(8,128)S(1)} %add.37), channel_id=1, source_target_pairs={{0,2},{1,3},{2,4},{3,5},{4,6},{5,7},{6,0},{7,1},{8,10},{9,11},{10,... | collective-permute-start | bytes 159752 | tf_op jit(solution)/shard_map/ppermute | solution.py:474
  104.9 4.8 %collective-permute-start.1 = (f32[104,128]{1,0:T(8,128)S(1)}, f32[104,128]{1,0:T(8,128)S(1)}, u32[]{:S(2)}, u32[]{:S(2)}) collective-permute-start(f32[104,128]{1,0:T(8,128)S(1)} %add.37), channel_id=1, source_target_pairs={{0,6},{1,7},{2,0},{3,1},{4,2},{5,3},{6,4},{7,5},{8,14},{9,15},{10,... | collective-permute-start | bytes 159752 | tf_op jit(solution)/shard_map/ppermute | solution.py:474
  109.8 9.5 %collective-permute-start.6 = (f32[104,128]{1,0:T(8,128)S(1)}, f32[104,128]{1,0:T(8,128)S(1)}, u32[]{:S(2)}, u32[]{:S(2)}) collective-permute-start(f32[104,128]{1,0:T(8,128)S(1)} %add_add_fusion.1), channel_id=1, source_target_pairs={{0,16},{1,17},{2,18},{3,19},{4,20},{5,21},{6,22},{7,23},{8,24},{9,... | collective-permute-start | bytes 159752 | tf_op jit(solution)/shard_map/ppermute | solution.py:474
  114.4 5.3 %collective-permute-start.5 = (f32[104,128]{1,0:T(8,128)S(1)}, f32[104,128]{1,0:T(8,128)S(1)}, u32[]{:S(2)}, u32[]{:S(2)}) collective-permute-start(f32[104,128]{1,0:T(8,128)S(1)} %add_add_fusion.1), channel_id=1, source_target_pairs={{0,8},{1,9},{2,10},{3,11},{4,12},{5,13},{6,14},{7,15},{8,16},{9,17... | collective-permute-start | bytes 159752 | tf_op jit(solution)/shard_map/ppermute | solution.py:474
  114.5 5.3 %collective-permute-start.4 = (f32[104,128]{1,0:T(8,128)S(1)}, f32[104,128]{1,0:T(8,128)S(1)}, u32[]{:S(2)}, u32[]{:S(2)}) collective-permute-start(f32[104,128]{1,0:T(8,128)S(1)} %add_add_fusion.1), channel_id=1, source_target_pairs={{0,24},{1,25},{2,26},{3,27},{4,28},{5,29},{6,30},{7,31},{8,0},{9,1... | collective-permute-start | bytes 159752 | tf_op jit(solution)/shard_map/ppermute | solution.py:474
  119.8 11.5 %collective-permute-start.7 = (f32[104,128]{1,0:T(8,128)S(1)}, f32[104,128]{1,0:T(8,128)S(1)}, u32[]{:S(2)}, u32[]{:S(2)}) collective-permute-start(f32[104,128]{1,0:T(8,128)S(1)} %add_add_fusion.own_ref), channel_id=1, source_target_pairs={{0,32},{1,33},{2,34},{3,35},{4,36},{5,37},{6,38},{7,39},{8,40},{9,... | collective-permute-start | bytes 159752 | tf_op jit(solution)/shard_map/ppermute | solution.py:474
  122.9 8.4 %collective-permute-start.8 = (f32[104,128]{1,0:T(8,128)S(1)}, f32[104,128]{1,0:T(8,128)S(1)}, u32[]{:S(2)}, u32[]{:S(2)}) collective-permute-start(f32[104,128]{1,0:T(8,128)S(1)} %add_add_fusion.own_ref), channel_id=1, source_target_pairs={{0,64},{1,65},{2,66},{3,67},{4,68},{5,69},{6,70},{7,71},{8,72},{9,... | collective-permute-start | bytes 159752 | tf_op jit(solution)/shard_map/ppermute | solution.py:474
  127.2 4.3 %collective-permute-start.9 = (f32[104,128]{1,0:T(8,128)S(1)}, f32[104,128]{1,0:T(8,128)S(1)}, u32[]{:S(2)}, u32[]{:S(2)}) collective-permute-start(f32[104,128]{1,0:T(8,128)S(1)} %add_add_fusion.own_ref), channel_id=1, source_target_pairs={{0,96},{1,97},{2,98},{3,99},{4,100},{5,101},{6,102},{7,103},{8,104... | collective-permute-start | bytes 159752 | tf_op jit(solution)/shard_map/ppermute | solution.py:474

commit v7 on v6

--- a/solution.py
+++ b/solution.py
@@ -168,7 +168,8 @@
             dense[chunks, at, :] = jnp.where(lane == c * (some // span) + s // span, ids, 0.0)
         return carry
 
-    lax.fori_loop(0, blocks.shape[0], pack, 0)
+    for c in range(blocks.shape[0]):
+        pack(c, 0)
     used = place_ref[0, slots - 1] + place_ref[1, slots - 1]
     for j in range(chunks + 1):
         dense[j, pl.ds(used, GROUP + blk), :] = jnp.zeros((GROUP + blk, LANES), jnp.float32)

time: 134 us -> 134 us (level)
  waiting for transfers between devices: 76 us -> 78.4 us
  starting transfers between devices: 36 us -> 34.5 us
    ppermute x10, waiting for transfers between devices: 2.28 us -> 4.69 us  [shifted(): return lax.ppermute(values, 'dev', pairs)]
    ppermute x10, starting transfers between devices: 24.4 us -> 22.9 us  [shifted(): return lax.ppermute(values, 'dev', pairs)]
  transfers between devices with their start and end apart: 11 -> 11, of which waited for: 4 -> 6; matrix products, arithmetic and copies ran while one was open for 3% -> 3% of each run, Pallas kernels for 4% -> 4%
where the time goes in v7:
time: 134 us
  waiting for transfers between devices  78.4 us (59%)
  starting transfers between devices  34.5 us (26%)
  Pallas kernels  15 us (11%)
  local copies, waits for them, and re-layouts  3.29 us (2%)
  other arithmetic  1.5 us (1%)
    all_to_all x1, waiting for transfers between devices, body(): recv = lax.all_to_all(send, 'dev', split_axis=0, concat_axis=0, tiled=True)  73.7 us
    ppermute x10, starting transfers between devices, shifted(): return lax.ppermute(values, 'dev', pairs)  22.9 us
    all_to_all x1, starting transfers between devices, body(): recv = lax.all_to_all(send, 'dev', split_axis=0, concat_axis=0, tiled=True)  11.6 us
    pallas_call x1, Pallas kernels, update_lists(): pl.pallas_call(functools.partial(update_kernel, blk), out_shape=(jax.Shap...  5.93 us
    pallas_call x4, Pallas kernels, row_errors(): pl.pallas_call(functools.partial(error_kernel, sub, part, blk), out_shape...  5.55 us
    ppermute x10, waiting for transfers between devices, shifted(): return lax.ppermute(values, 'dev', pairs)  4.69 us
  transfers between devices with their start and end apart: 11, of which 6 were waited for; matrix products, arithmetic and copies ran while one was open for 3% of the time, Pallas kernels for 4%

profile of v7, /device:TPU:0, one launch (start us, length us, event | category | flops | bytes accessed | tf_op | source)
XLA Modules:
  0.0 133.5 jit_solution(10447064815723853956)
XLA Ops:
  0.6 2.5 %build_send.1 = bf16[128,200,128]{2,1,0:T(8,128)(2,1)} custom-call(s32[32]{0:T(128)} %owner_hbm.1, s32[32]{0:T(128)} %fill_hbm.1, bf16[1024,768]{1,0:T(8,128)(2,1)} %vec_ref.1, s32[8,128]{1,0:T(8,128)} %bitcast.12), custom_call_target="tpu_custom_call" | custom-call | tf_op jit(solution)/shard_map/build_send/pallas_call | solution.py:90
  3.2 0.0 copy-start.2
  3.2 11.6 %all-to-all-start = ((bf16[128,200,128]{2,1,0:T(8,128)(2,1)}), bf16[128,200,128]{2,1,0:T(8,128)(2,1)}, u32[]{:S(2)}, u32[]{:S(2)}) async-start(bf16[128,200,128]{2,1,0:T(8,128)(2,1)} %build_send.1), calls=%async_computation | async-start | bytes 13107200 | tf_op jit(solution)/shard_map/all_to_all | solution.py:461
  14.9 0.6 copy.20
  15.5 0.1 multiply_reduce_fusion
  15.7 1.6 %copy.21 = bf16[24,256,3]{2,1,0:T(8,128)(2,1)} copy(bf16[24,256,3]{1,0,2:T(8,128)(2,1)S(1)} %pad_maximum_fusion) | data formatting | bytes 73728 | tf_op jit(solution)/shard_map/stack | solution.py:449
  17.3 0.4 fusion.2
  17.6 1.0 copy-done.1
  18.7 1.0 fusion.1.book_ref
  19.7 73.7 %all-to-all-done.recv_ref = bf16[128,200,128]{2,1,0:T(8,128)(2,1)} async-done(((bf16[128,200,128]{2,1,0:T(8,128)(2,1)}), bf16[128,200,128]{2,1,0:T(8,128)(2,1)}, u32[]{:S(2)}, u32[]{:S(2)}) %all-to-all-start) | async-done | bytes 6553632 | tf_op jit(solution)/shard_map/all_to_all | solution.py:461
  93.3 5.9 %update_lists.1 = (f32[512,768]{1,0:T(8,128)}, bf16[17,768,256]{2,1,0:T(8,128)(2,1)S(1)}, s32[8,128]{1,0:T(8,128)S(1)}, f32[104,128]{1,0:T(8,128)S(1)}, f32[8,128]{1,0:T(8,128)S(1)}) custom-call(bf16[128,200,128]{2,1,0:T(8,128)(2,1)} %all-to-all-done.recv_ref, f32[512,768]{1,0:T(8,128)S(1)} %copy-done), custom_call_target="tpu_custom_call" | custom-call | tf_op jit(solution)/shard_map/update_lists/pallas_call | solution.py:286
  99.3 0.1 collective-permute-start
  99.4 1.6 %row_errors.4.rest_0_ = f32[40,128]{1,0:T(8,128)S(1)} custom-call(s32[8,128]{1,0:T(8,128)S(1)} %get-tuple-element.10.place_ref, bf16[17,768,256]{2,1,0:T(8,128)(2,1)S(1)} %get-tuple-element.11.resid_ref, bf16[24,256,48]{2,1,0:T(8,128)(2,1)S(1)} %fusion.1.book_ref), custom_call_target="tpu_custom_call" | custom-call | flops 2415919104 | bytes 1179648 | tf_op jit(solution)/shard_map/row_errors/pallas_call | solution.py:388
  101.0 1.3 collective-permute-start.3
  102.3 3.0 %collective-permute-start.2 = (f32[104,128]{1,0:T(8,128)S(1)}, f32[104,128]{1,0:T(8,128)S(1)}, u32[]{:S(2)}, u32[]{:S(2)}) collective-permute-start(f32[104,128]{1,0:T(8,128)S(1)} %add.37), channel_id=1, source_target_pairs={{0,2},{1,3},{2,4},{3,5},{4,6},{5,7},{6,0},{7,1},{8,10},{9,11},{10,... | collective-permute-start | bytes 159752 | tf_op jit(solution)/shard_map/ppermute | solution.py:475
  105.4 2.2 %collective-permute-start.1 = (f32[104,128]{1,0:T(8,128)S(1)}, f32[104,128]{1,0:T(8,128)S(1)}, u32[]{:S(2)}, u32[]{:S(2)}) collective-permute-start(f32[104,128]{1,0:T(8,128)S(1)} %add.37), channel_id=1, source_target_pairs={{0,6},{1,7},{2,0},{3,1},{4,2},{5,3},{6,4},{7,5},{8,14},{9,15},{10,... | collective-permute-start | bytes 159752 | tf_op jit(solution)/shard_map/ppermute | solution.py:475
  107.5 0.6 row_errors.5.rest_0_
  108.2 1.6 %collective-permute-done.2 = f32[104,128]{1,0:T(8,128)S(1)} collective-permute-done((f32[104,128]{1,0:T(8,128)S(1)}, f32[104,128]{1,0:T(8,128)S(1)}, u32[]{:S(2)}, u32[]{:S(2)}) %collective-permute-start.2) | collective-permute-done | bytes 53280 | tf_op jit(solution)/shard_map/ppermute | solution.py:475
  109.7 0.0 collective-permute-done.1
  109.7 1.1 collective-permute-start.6
  110.8 2.3 %collective-permute-start.5 = (f32[104,128]{1,0:T(8,128)S(1)}, f32[104,128]{1,0:T(8,128)S(1)}, u32[]{:S(2)}, u32[]{:S(2)}) collective-permute-start(f32[104,128]{1,0:T(8,128)S(1)} %add_add_fusion.1), channel_id=1, source_target_pairs={{0,8},{1,9},{2,10},{3,11},{4,12},{5,13},{6,14},{7,15},{8,16},{9,17... | collective-permute-start | bytes 159752 | tf_op jit(solution)/shard_map/ppermute | solution.py:475
  113.1 1.7 %collective-permute-start.4 = (f32[104,128]{1,0:T(8,128)S(1)}, f32[104,128]{1,0:T(8,128)S(1)}, u32[]{:S(2)}, u32[]{:S(2)}) collective-permute-start(f32[104,128]{1,0:T(8,128)S(1)} %add_add_fusion.1), channel_id=1, source_target_pairs={{0,24},{1,25},{2,26},{3,27},{4,28},{5,29},{6,30},{7,31},{8,0},{9,1... | collective-permute-start | bytes 159752 | tf_op jit(solution)/shard_map/ppermute | solution.py:475
  114.8 1.8 %row_errors.6.rest_0_ = f32[40,128]{1,0:T(8,128)S(1)} custom-call(s32[8,128]{1,0:T(8,128)S(1)} %get-tuple-element.10.place_ref, bf16[17,768,256]{2,1,0:T(8,128)(2,1)S(1)} %get-tuple-element.11.resid_ref, bf16[24,256,48]{2,1,0:T(8,128)(2,1)S(1)} %fusion.1.book_ref, f32[40,128]{1,0:T(8,128)S(1)} %row_errors.5.rest_0_), custom_call_target="tpu_custom_call" | custom-call | flops 2415919104 | bytes 1179648 | tf_op jit(solution)/shard_map/row_errors/pallas_call | solution.py:388
  116.6 0.3 collective-permute-done.5
  116.9 0.3 collective-permute-done.4
  117.3 5.1 %collective-permute-start.7 = (f32[104,128]{1,0:T(8,128)S(1)}, f32[104,128]{1,0:T(8,128)S(1)}, u32[]{:S(2)}, u32[]{:S(2)}) collective-permute-start(f32[104,128]{1,0:T(8,128)S(1)} %add_add_fusion.own_ref), channel_id=1, source_target_pairs={{0,32},{1,33},{2,34},{3,35},{4,36},{5,37},{6,38},{7,39},{8,40},{9,... | collective-permute-start | bytes 159752 | tf_op jit(solution)/shard_map/ppermute | solution.py:475
  122.4 6.0 %collective-permute-start.8 = (f32[104,128]{1,0:T(8,128)S(1)}, f32[104,128]{1,0:T(8,128)S(1)}, u32[]{:S(2)}, u32[]{:S(2)}) collective-permute-start(f32[104,128]{1,0:T(8,128)S(1)} %add_add_fusion.own_ref), channel_id=1, source_target_pairs={{0,64},{1,65},{2,66},{3,67},{4,68},{5,69},{6,70},{7,71},{8,72},{9,... | collective-permute-start | bytes 159752 | tf_op jit(solution)/shard_map/ppermute | solution.py:475
  128.4 0.1 collective-permute-start.9
  128.5 1.6 %row_errors.7 = (f32[40,128]{1,0:T(8,128)}, f32[32,128]{1,0:T(8,128)}) custom-call(s32[8,128]{1,0:T(8,128)S(1)} %get-tuple-element.10.place_ref, bf16[17,768,256]{2,1,0:T(8,128)(2,1)S(1)} %get-tuple-element.11.resid_ref, bf16[24,256,48]{2,1,0:T(8,128)(2,1)S(1)} %fusion.1.book_ref, f32[40,128]{1,0:T(8,128)S(1)} %row_errors.6.rest_0_), custom_call_target="tpu_custom_call" | custom-call | flops 2415919104 | bytes 1179648 | tf_op jit(solution)/shard_map/row_errors/pallas_call | solution.py:388
  130.1 1.0 collective-permute-done.8.two_ref
  131.1 1.5 %collective-permute-done.9.three_ref = f32[104,128]{1,0:T(8,128)S(1)} collective-permute-done((f32[104,128]{1,0:T(8,128)S(1)}, f32[104,128]{1,0:T(8,128)S(1)}, u32[]{:S(2)}, u32[]{:S(2)}) %collective-permute-start.9) | collective-permute-done | bytes 53280 | tf_op jit(solution)/shard_map/ppermute | solution.py:475
  132.6 0.9 unpack_moments.1
  (13 shorter events, 0.1 us)
Async XLA Ops:
  3.2 11.7 %copy-start.2 = (bf16[24,32,256]{2,1,0:T(8,128)(2,1)S(1)}, bf16[24,32,256]{2,1,0:T(8,128)(2,1)}, u32[]{:S(2)}) copy-start(bf16[24,32,256]{2,1,0:T(8,128)(2,1)} %param.11) | copy-start | bytes 1179652
  3.2 90.1 %all-to-all-start = ((bf16[128,200,128]{2,1,0:T(8,128)(2,1)}), bf16[128,200,128]{2,1,0:T(8,128)(2,1)}, u32[]{:S(2)}, u32[]{:S(2)}) async-start(bf16[128,200,128]{2,1,0:T(8,128)(2,1)} %build_send.1), calls=%async_computation | async-start | bytes 13107200 | tf_op jit(solution)/shard_map/all_to_all | solution.py:461
  17.3 1.4 %copy-start.1 = (bf16[24,256,3]{2,1,0:T(8,128)(2,1)S(1)}, bf16[24,256,3]{2,1,0:T(8,128)(2,1)}, u32[]{:S(2)}) copy-start(bf16[24,256,3]{2,1,0:T(8,128)(2,1)} %copy.21) | copy-start | bytes 110596
  18.7 74.6 %copy-start = (f32[512,768]{1,0:T(8,128)S(1)}, f32[512,768]{1,0:T(8,128)}, u32[]{:S(2)}) copy-start(f32[512,768]{1,0:T(8,128)} %old_ref.1) | copy-start | bytes 4718596
  99.3 1.7 %collective-permute-start = (f32[104,128]{1,0:T(8,128)S(1)}, f32[104,128]{1,0:T(8,128)S(1)}, u32[]{:S(2)}, u32[]{:S(2)}) collective-permute-start(f32[104,128]{1,0:T(8,128)S(1)} %get-tuple-element.13), channel_id=1, source_target_pairs={{0,1},{1,0},{2,3},{3,2},{4,5},{5,4},{6,7},{7,6},{8,9},{9,8},{10,11... | collective-permute-start | bytes 159752 | tf_op jit(solution)/shard_map/ppermute | solution.py:475
  101.0 7.2 %collective-permute-start.3 = (f32[104,128]{1,0:T(8,128)S(1)}, f32[104,128]{1,0:T(8,128)S(1)}, u32[]{:S(2)}, u32[]{:S(2)}) collective-permute-start(f32[104,128]{1,0:T(8,128)S(1)} %add.37), channel_id=1, source_target_pairs={{0,4},{1,5},{2,6},{3,7},{4,0},{5,1},{6,2},{7,3},{8,12},{9,13},{10,... | collective-permute-start | bytes 159752 | tf_op jit(solution)/shard_map/ppermute | solution.py:475
  102.3 7.4 %collective-permute-start.2 = (f32[104,128]{1,0:T(8,128)S(1)}, f32[104,128]{1,0:T(8,128)S(1)}, u32[]{:S(2)}, u32[]{:S(2)}) collective-permute-start(f32[104,128]{1,0:T(8,128)S(1)} %add.37), channel_id=1, source_target_pairs={{0,2},{1,3},{2,4},{3,5},{4,6},{5,7},{6,0},{7,1},{8,10},{9,11},{10,... | collective-permute-start | bytes 159752 | tf_op jit(solution)/shard_map/ppermute | solution.py:475
  105.4 4.4 %collective-permute-start.1 = (f32[104,128]{1,0:T(8,128)S(1)}, f32[104,128]{1,0:T(8,128)S(1)}, u32[]{:S(2)}, u32[]{:S(2)}) collective-permute-start(f32[104,128]{1,0:T(8,128)S(1)} %add.37), channel_id=1, source_target_pairs={{0,6},{1,7},{2,0},{3,1},{4,2},{5,3},{6,4},{7,5},{8,14},{9,15},{10,... | collective-permute-start | bytes 159752 | tf_op jit(solution)/shard_map/ppermute | solution.py:475
  109.7 6.9 %collective-permute-start.6 = (f32[104,128]{1,0:T(8,128)S(1)}, f32[104,128]{1,0:T(8,128)S(1)}, u32[]{:S(2)}, u32[]{:S(2)}) collective-permute-start(f32[104,128]{1,0:T(8,128)S(1)} %add_add_fusion.1), channel_id=1, source_target_pairs={{0,16},{1,17},{2,18},{3,19},{4,20},{5,21},{6,22},{7,23},{8,24},{9,... | collective-permute-start | bytes 159752 | tf_op jit(solution)/shard_map/ppermute | solution.py:475
  110.8 6.1 %collective-permute-start.5 = (f32[104,128]{1,0:T(8,128)S(1)}, f32[104,128]{1,0:T(8,128)S(1)}, u32[]{:S(2)}, u32[]{:S(2)}) collective-permute-start(f32[104,128]{1,0:T(8,128)S(1)} %add_add_fusion.1), channel_id=1, source_target_pairs={{0,8},{1,9},{2,10},{3,11},{4,12},{5,13},{6,14},{7,15},{8,16},{9,17... | collective-permute-start | bytes 159752 | tf_op jit(solution)/shard_map/ppermute | solution.py:475
  113.1 4.1 %collective-permute-start.4 = (f32[104,128]{1,0:T(8,128)S(1)}, f32[104,128]{1,0:T(8,128)S(1)}, u32[]{:S(2)}, u32[]{:S(2)}) collective-permute-start(f32[104,128]{1,0:T(8,128)S(1)} %add_add_fusion.1), channel_id=1, source_target_pairs={{0,24},{1,25},{2,26},{3,27},{4,28},{5,29},{6,30},{7,31},{8,0},{9,1... | collective-permute-start | bytes 159752 | tf_op jit(solution)/shard_map/ppermute | solution.py:475
  117.3 12.8 %collective-permute-start.7 = (f32[104,128]{1,0:T(8,128)S(1)}, f32[104,128]{1,0:T(8,128)S(1)}, u32[]{:S(2)}, u32[]{:S(2)}) collective-permute-start(f32[104,128]{1,0:T(8,128)S(1)} %add_add_fusion.own_ref), channel_id=1, source_target_pairs={{0,32},{1,33},{2,34},{3,35},{4,36},{5,37},{6,38},{7,39},{8,40},{9,... | collective-permute-start | bytes 159752 | tf_op jit(solution)/shard_map/ppermute | solution.py:475
  122.4 8.7 %collective-permute-start.8 = (f32[104,128]{1,0:T(8,128)S(1)}, f32[104,128]{1,0:T(8,128)S(1)}, u32[]{:S(2)}, u32[]{:S(2)}) collective-permute-start(f32[104,128]{1,0:T(8,128)S(1)} %add_add_fusion.own_ref), channel_id=1, source_target_pairs={{0,64},{1,65},{2,66},{3,67},{4,68},{5,69},{6,70},{7,71},{8,72},{9,... | collective-permute-start | bytes 159752 | tf_op jit(solution)/shard_map/ppermute | solution.py:475
  128.4 4.1 %collective-permute-start.9 = (f32[104,128]{1,0:T(8,128)S(1)}, f32[104,128]{1,0:T(8,128)S(1)}, u32[]{:S(2)}, u32[]{:S(2)}) collective-permute-start(f32[104,128]{1,0:T(8,128)S(1)} %add_add_fusion.own_ref), channel_id=1, source_target_pairs={{0,96},{1,97},{2,98},{3,99},{4,100},{5,101},{6,102},{7,103},{8,104... | collective-permute-start | bytes 159752 | tf_op jit(solution)/shard_map/ppermute | solution.py:475
